TPU v7x, 32 devices: a whole 2x2x4 slice. The times are simulated.
32 devices in a mesh: prow: 8 (over y, x, core), pcol: 4 (over z).
Axes of the slice: x: 2, y: 2, z: 4, core: 2. Of those that a mesh axis runs over, the one named last changes fastest.
Arguments:
- inverse_blocks: bfloat16 [32, 32, 128, 128], P('pcol', 'prow'), may hold values from -6 to 6
- lower_blocks: bfloat16 [32, 4, 128, 128], P('prow', None, 'pcol'), may hold values from -1 to 1
- pattern: int32 [4, 16], replicated, may hold values from 0 to 31, as said below
- diag_inverse: float32 [4, 16384], P(None, ('prow', 'pcol')), may hold values from -6 to 6
Outputs:
- inverse_column: float32 [32, 4, 128, 128], P('pcol', None, 'prow')
- inverse_diag: float32 [4, 16384], P(None, ('prow', 'pcol'))
Inputs may be any that keep to these rules, and one draw needn't show every extreme that they name: `pattern`: each row names 16 different ancestor blocks.
All inputs are finite; a program needn't handle non-finite values.
Results may differ from a plain program's by a relative error of at most 0.0003.
Values may be sent and summed in bfloat16 or wider, within the bound.
No kernel may reach another device: no remote copies, remote signals or barrier semaphores. Data moves between devices by JAX's collectives and lax.ppermute only.
A program may use at most 64 MiB of HBM per device.

v0:
```python
import jax
import jax.numpy as jnp
from jax import lax
from jax.sharding import PartitionSpec as P


def per_device(inverse_blocks, lower_blocks, pattern, diag_inverse):
    blocks_i = inverse_blocks.shape[0]
    blocks_j = inverse_blocks.shape[1]
    block_width = inverse_blocks.shape[3]
    node_count = lower_blocks.shape[1]
    row_groups = lax.axis_size("prow")
    col_groups = lax.axis_size("pcol")
    block_count = blocks_j * row_groups
    matches = pattern[None, :, :] == jnp.arange(block_count, dtype=jnp.int32)[:, None, None]
    present = jnp.sum(matches.astype(jnp.float32), axis=2)
    start_j = lax.axis_index("prow") * blocks_j
    start_i = lax.axis_index("pcol") * blocks_i
    keep_j = lax.dynamic_slice_in_dim(present, start_j, blocks_j, 0)
    keep_i = lax.dynamic_slice_in_dim(present, start_i, blocks_i, 0)
    whole = lax.all_gather(lower_blocks, "pcol", axis=2, tiled=True)
    masked = whole * keep_j.astype(jnp.bfloat16)[:, :, None, None]
    summed = lax.psum_scatter(
        jnp.einsum("ijrb,jkbe->rike", inverse_blocks, masked, preferred_element_type=jnp.float32),
        "prow",
        scatter_dimension=0,
        tiled=True,
    )
    column = summed * (-keep_i)[None, :, :, None]
    spread = lax.all_to_all(masked, "prow", split_axis=2, concat_axis=0, tiled=True)
    own_lower = lax.dynamic_slice_in_dim(spread, start_i, blocks_i, 0)
    partial_value = jnp.einsum(
        "ikra,rikb->kab", own_lower.astype(jnp.float32), column, precision=lax.Precision.HIGHEST
    )
    partial_value = partial_value.reshape(node_count, block_width * block_width)
    totals = lax.psum(partial_value, ("prow", "pcol"))
    piece_len = block_width * block_width // (row_groups * col_groups)
    flat_index = lax.axis_index("prow") * col_groups + lax.axis_index("pcol")
    diag_piece = lax.dynamic_slice_in_dim(totals, flat_index * piece_len, piece_len, 1)
    return (jnp.transpose(column, (1, 2, 0, 3)), diag_inverse - diag_piece)


def solution(mesh):
    placed = (
        P("pcol", "prow", None, None),
        P("prow", None, "pcol", None),
        P(),
        P(None, ("prow", "pcol")),
    )
    return jax.shard_map(
        per_device,
        mesh=mesh,
        in_specs=placed,
        out_specs=(P("pcol", None, "prow", None), P(None, ("prow", "pcol"))),
        check_vma=False,
    )
```

profile of v0, /device:TPU:0, one launch (start us, length us, event | category | flops | bytes accessed | tf_op | source)
XLA Modules:
  0.0 213.2 jit_solution(1040591015274846539)
XLA Ops:
  7.2 0.0 copy-start
  7.2 0.0 reduce-scatter.2.cloned.1.call-start
  7.2 0.8 convert_reduce_fusion
  8.1 0.1 dynamic-slice_convert_fusion
  8.2 0.1 copy.26
  8.3 1.0 copy.25
  9.2 17.4 %all_gather.3 = bf16[4,4,128,128]{3,1,0,2:T(4,128)(2,1)S(1)} all-gather(bf16[4,4,32,128]{3,1,0,2:T(4,128)(2,1)S(1)} %copy.25), channel_id=1, replica_groups=mesh['prow'=8,'pcol'=4] {'pcol'}, dimensions={2}, use_global_device_ids=true | all-gather | bytes 655360 | tf_op jit(solution)/shard_map/all_gather | solution.py:21
  26.6 0.0 copy-start.1
  26.6 0.8 copy-done.1
  27.4 0.3 fusion.6
  27.7 0.0 copy-done
  27.7 0.8 convolution_bitcast_fusion
  28.5 2.0 copy.28
  30.5 0.0 copy-start.2
  30.5 0.0 reduce-scatter.2.cloned.1.call-update
  30.5 1.0 copy-done.2
  31.6 1.1 broadcast_multiply_fusion
  32.6 3.7 %all-to-all-start = ((bf16[4,4,128,128]{3,1,0,2:T(4,128)(2,1)}), bf16[4,4,128,128]{3,1,0,2:T(4,128)(2,1)S(1)}, u32[]{:S(2)}, u32[]{:S(2)}) async-start(bf16[4,4,128,128]{3,1,0,2:T(4,128)(2,1)} %broadcast_multiply_fusion), calls=%async_computation.1 | async-start | bytes 1048576 | tf_op jit(solution)/shard_map/all_to_all | solution.py:30
  36.4 0.0 all-reduce.2.cloned.1.call-start
  36.4 0.1 dynamic-slice_negate_fusion
  36.5 9.6 %all-to-all-done = bf16[4,4,128,128]{3,1,0,2:T(4,128)(2,1)S(1)} async-done(((bf16[4,4,128,128]{3,1,0,2:T(4,128)(2,1)}), bf16[4,4,128,128]{3,1,0,2:T(4,128)(2,1)S(1)}, u32[]{:S(2)}, u32[]{:S(2)}) %all-to-all-start) | async-done | bytes 524320 | tf_op jit(solution)/shard_map/all_to_all | solution.py:30
  46.1 0.0 copy-start.4
  46.1 0.1 copy.29
  46.2 27.4 %reduce-scatter.2.cloned.1.call-done = f32[16,8,4,128]{3,1,2,0:T(8,128)} async-done(((f32[128,8,4,128]{3,1,2,0:T(8,128)}), f32[16,8,4,128]{3,1,2,0:T(8,128)}) %reduce-scatter.2.cloned.1.call-update) | async-done | bytes 262160 | tf_op jit(solution)/shard_map/reduce_scatter | solution.py:23
  73.7 0.0 copy-start.3
  73.7 1.1 broadcast_multiply_fusion.1
  74.8 0.4 convolution_bitcast_fusion.1
  75.2 0.9 copy.43
  76.1 0.0 all-reduce.2.cloned.1.call-update
  76.1 0.0 copy-done.3
  76.1 0.1 fusion.5
  76.2 0.9 copy.31
  77.1 128.0 %all-reduce.2.cloned.1.call-done = f32[4,16384]{1,0:T(4,128)} async-done(((f32[4,16384]{1,0:T(4,128)}), f32[4,16384]{1,0:T(4,128)}) %all-reduce.2.cloned.1.call-update) | async-done | bytes 262160 | tf_op jit(solution)/shard_map/psum | solution.py:36
  205.1 0.0 copy-done.4
  205.1 1.3 dynamic-slice_subtract_fusion
Async XLA Ops:
  7.2 20.5 %copy-start = (bf16[8,4,128,128]{3,2,1,0:T(8,128)(2,1)S(1)}, bf16[8,4,128,128]{3,2,1,0:T(8,128)(2,1)}, u32[]{:S(2)}) copy-start(bf16[8,4,128,128]{3,2,1,0:T(8,128)(2,1)} %param.4) | copy-start | bytes 3145732
  7.2 66.5 %reduce-scatter.2.cloned.1.call-start = ((), (), s32[]{:S(2)}) async-start(), calls=%async_computation.2 | async-start | bytes 2359296 | tf_op jit(solution)/shard_map/reduce_scatter | solution.py:23
  26.6 0.8 copy-start.1
  30.5 1.0 copy-start.2
  32.6 13.5 %all-to-all-start = ((bf16[4,4,128,128]{3,1,0,2:T(4,128)(2,1)}), bf16[4,4,128,128]{3,1,0,2:T(4,128)(2,1)S(1)}, u32[]{:S(2)}, u32[]{:S(2)}) async-start(bf16[4,4,128,128]{3,1,0,2:T(4,128)(2,1)} %broadcast_multiply_fusion), calls=%async_computation.1 | async-start | bytes 1048576 | tf_op jit(solution)/shard_map/all_to_all | solution.py:30
  36.4 168.7 %all-reduce.2.cloned.1.call-start = ((), (), s32[]{:S(2)}) async-start(), calls=%async_computation.3 | async-start | bytes 524288 | tf_op jit(solution)/shard_map/psum | solution.py:36
  46.1 159.0 %copy-start.4 = (f32[4,512]{1,0:T(4,128)S(1)}, f32[4,512]{1,0:T(4,128)}, u32[]{:S(2)}) copy-start(f32[4,512]{1,0:T(4,128)} %param.7) | copy-start | bytes 24580
  73.7 2.5 %copy-start.3 = (f32[16,8,4,128]{3,1,2,0:T(8,128)S(1)}, f32[16,8,4,128]{3,1,2,0:T(8,128)}, u32[]{:S(2)}) copy-start(f32[16,8,4,128]{3,1,2,0:T(8,128)} %reduce-scatter.2.cloned.1.call-done) | copy-start | bytes 786436
Sparse Core Ops, SparseCore 0:
  30.7 42.9 reduce-scatter.1
  80.1 124.9 all-reduce.1
where the time goes:
time: 214 us; the launch traced here: 213 us
  waiting for transfers between devices  165 us (77%)
  blocking collectives  17.4 us (8%)
  between operations  14.1 us (7%)
  local copies, waits for them, and re-layouts  6.9 us (3%)
  other arithmetic  4.79 us (2%)
  starting transfers between devices  3.8 us (2%)
    psum x1, waiting for transfers between devices, per_device(): totals = lax.psum(partial_value, ('prow', 'pcol'))  128 us
    reduce_scatter x1, waiting for transfers between devices, per_device(): lax.psum_scatter(jnp.einsum('ijrb,jkbe->rike', inverse_blocks, masked, pr...  27.4 us
    all_gather x1, blocking collectives, per_device(): whole = lax.all_gather(lower_blocks, 'pcol', axis=2, tiled=True)  17.4 us
    all_to_all x1, waiting for transfers between devices, per_device(): lax.all_to_all(masked, 'prow', split_axis=2, concat_axis=0, tiled=True)  9.62 us
    unnamed x13, local copies, waits for them, and re-layouts  4.53 us
  transfers between devices with their start and end apart: 3, of which 3 were waited for; matrix products, arithmetic and copies ran while one was open for 1% of the time, Pallas kernels for 0%

commit v1 on v0

v1 whole, which is shorter than its diff:
```python
import jax
import jax.numpy as jnp
from jax import lax
from jax.sharding import PartitionSpec as P

CORES = 2


def swap(value, axis, size, step):
    return lax.ppermute(value, axis, [(at, at ^ step) for at in range(size)])


def take(value, index, axis):
    return lax.dynamic_index_in_dim(value, index, axis, keepdims=False)


def gather_pieces(piece, axis, size):
    held = {0: piece}
    step = size // 2
    while step:
        held.update({at ^ step: swap(held[at], axis, size, step) for at in sorted(held)})
        step //= 2
    return held


def scatter_sum(parts, part_of, axis, size, own, stride):
    total = part_of(parts, own)
    for step in range(1, size):
        total = total + swap(part_of(parts, own ^ step), axis, size * stride, step * stride)
    return total


def per_device(inverse_blocks, lower_blocks, pattern, diag_inverse):
    blocks_i, blocks_j, width, _ = inverse_blocks.shape
    node_count = lower_blocks.shape[1]
    row_groups = lax.axis_size("prow")
    col_groups = lax.axis_size("pcol")
    chips = row_groups // CORES
    ratio = row_groups // col_groups
    block_count = blocks_j * row_groups
    prow, pcol = lax.axis_index("prow"), lax.axis_index("pcol")
    chip, core = prow // CORES, prow % CORES
    rows = width // row_groups

    matches = pattern[None, :, :] == jnp.arange(block_count, dtype=jnp.int32)[:, None, None]
    present = jnp.sum(matches.astype(jnp.float32), axis=2)
    keep_j = lax.dynamic_slice_in_dim(present, prow * blocks_j, blocks_j, 0)
    keep_i = lax.dynamic_slice_in_dim(present, pcol * blocks_i, blocks_i, 0)

    held = gather_pieces(lower_blocks, "pcol", col_groups)
    whole = jnp.zeros((col_groups,) + lower_blocks.shape, lower_blocks.dtype)
    for at, piece in held.items():
        whole = lax.dynamic_update_index_in_dim(whole, piece, pcol ^ at, 0)
    masked = whole * keep_j.astype(jnp.bfloat16)[None, :, :, None, None]

    by_row = lower_blocks.reshape(blocks_j, node_count, ratio, rows, width)
    own_parts = []
    for step in range(ratio):
        pairs = []
        for p in range(row_groups):
            for c in range(col_groups):
                to_p = c * ratio + (p + step) % ratio
                pairs.append((p * col_groups + c, to_p * col_groups + p // ratio))
        sent = take(by_row, (prow + step) % ratio, 2)
        own_parts.append(lax.ppermute(sent, ("prow", "pcol"), pairs))
    own = jnp.zeros((ratio,) + own_parts[0].shape, lower_blocks.dtype)
    for step, part in enumerate(own_parts):
        own = lax.dynamic_update_index_in_dim(own, part, (prow - step) % ratio, 0)
    own = own.reshape(blocks_i, node_count, rows, width) * keep_i.astype(jnp.bfloat16)[:, :, None, None]

    inv = inverse_blocks.reshape(blocks_i, blocks_j, width, col_groups, width // col_groups)
    partial_sums = jnp.einsum("ijrcb,cjkbe->rike", inv, masked, preferred_element_type=jnp.float32)
    partial_sums = partial_sums.reshape(chips, CORES, rows, blocks_i, node_count, width)
    pair_sums = take(partial_sums, core, 1) + swap(take(partial_sums, 1 - core, 1), "prow", row_groups, 1)
    summed = scatter_sum(pair_sums, lambda v, at: take(v, at, 0), "prow", chips, chip, CORES)
    column = jnp.transpose(summed, (1, 2, 0, 3)) * (-keep_i)[:, :, None, None]

    update = jnp.einsum(
        "ikra,ikrb->kab", own.astype(jnp.float32), column, precision=lax.Precision.HIGHEST
    )
    length = width * width // (row_groups * col_groups)
    update = update.reshape(node_count, chips, CORES, col_groups, length)
    update = take(update, core, 2) + swap(take(update, 1 - core, 2), "prow", row_groups, 1)
    update = scatter_sum(update, lambda v, at: take(v, at, 1), "prow", chips, chip, CORES)
    update = scatter_sum(update, lambda v, at: take(v, at, 1), "pcol", col_groups, pcol, 1)
    return column, diag_inverse - update


def solution(mesh):
    placed = (
        P("pcol", "prow", None, None),
        P("prow", None, "pcol", None),
        P(),
        P(None, ("prow", "pcol")),
    )
    return jax.shard_map(
        per_device,
        mesh=mesh,
        in_specs=placed,
        out_specs=(P("pcol", None, "prow", None), P(None, ("prow", "pcol"))),
        check_vma=False,
    )
```

time: 214 us -> 61.5 us (0.29)
  waiting for transfers between devices: 165 us -> 27.9 us
  starting transfers between devices: 3.8 us -> 23.8 us
  blocking collectives: 17.4 us -> 0 us
  between operations: 14.1 us -> 0.94 us
  other arithmetic: 4.79 us -> 2.27 us
    psum x1 -> x0, waiting for transfers between devices: 128 us -> none  [per_device(): totals = lax.psum(partial_value, ('prow', 'pcol'))]
    ppermute x0 -> x16, waiting for transfers between devices: none -> 27.9 us  [the longest x14 27.9 us: swap(): return lax.ppermute(value, axis, [(at, at ^ step) for at in range(size)])]
    reduce_scatter x1 -> x0, waiting for transfers between devices: 27.4 us -> none  [per_device(): lax.psum_scatter(jnp.einsum('ijrb,jkbe->rike', inverse_blocks, masked, pr...]
    ppermute x0 -> x16, starting transfers between devices: none -> 23.8 us  [the longest x14 22.8 us: swap(): return lax.ppermute(value, axis, [(at, at ^ step) for at in range(size)])]
    all_gather x1 -> x0, blocking collectives: 17.4 us -> none  [per_device(): whole = lax.all_gather(lower_blocks, 'pcol', axis=2, tiled=True)]
    all_to_all x1 -> x0, waiting for transfers between devices: 9.62 us -> none  [per_device(): lax.all_to_all(masked, 'prow', split_axis=2, concat_axis=0, tiled=True)]
    all_to_all x1 -> x0, starting transfers between devices: 3.72 us -> none  [per_device(): lax.all_to_all(masked, 'prow', split_axis=2, concat_axis=0, tiled=True)]
    mul x3 -> x1, other arithmetic: 2.48 us -> 0.13 us  [per_device(): column = jnp.transpose(summed, (1, 2, 0, 3)) * (-keep_i)[:, :, None, None]]
  transfers between devices with their start and end apart: 3 -> 16, of which waited for: 3 -> 10; matrix products, arithmetic and copies ran while one was open for 1% -> 9% of each run, Pallas kernels for 0% -> 0%
where the time goes in v1:
time: 61.5 us; the launch traced here: 61.3 us
  waiting for transfers between devices  27.9 us (45%)
  starting transfers between devices  23.8 us (39%)
  local copies, waits for them, and re-layouts  5.08 us (8%)
  other arithmetic  2.27 us (4%)
  matrix products  1.27 us (2%)
  between operations  0.94 us (2%)
    ppermute x14, waiting for transfers between devices, swap(): return lax.ppermute(value, axis, [(at, at ^ step) for at in range(size)])  27.9 us
    ppermute x14, starting transfers between devices, swap(): return lax.ppermute(value, axis, [(at, at ^ step) for at in range(size)])  22.8 us
    unnamed x7, local copies, waits for them, and re-layouts  3.28 us
  transfers between devices with their start and end apart: 16, of which 10 were waited for; matrix products, arithmetic and copies ran while one was open for 9% of the time, Pallas kernels for 0%

profile of v1, /device:TPU:0, one launch (start us, length us, event | category | flops | bytes accessed | tf_op | source)
XLA Modules:
  0.0 61.3 jit_solution(2786958518019589821)
XLA Ops:
  0.6 4.1 %collective-permute-start = (bf16[4,4,32,128]{3,2,1,0:T(8,128)(2,1)}, bf16[4,4,32,128]{3,2,1,0:T(8,128)(2,1)S(1)}, u32[]{:S(2)}, u32[]{:S(2)}) collective-permute-start(bf16[4,4,32,128]{3,2,1,0:T(8,128)(2,1)} %param.5), channel_id=1, source_target_pairs={{0,2},{1,3},{2,0},{3,1},{4,6},{5,7},{6,4},{7,5},{8,10},{9,11},{10,... | collective-permute-start | bytes 393224 | tf_op jit(solution)/shard_map/ppermute | solution.py:10
  4.7 1.6 %collective-permute-start.1 = (bf16[4,4,32,128]{3,2,1,0:T(8,128)(2,1)}, bf16[4,4,32,128]{3,2,1,0:T(8,128)(2,1)S(1)}, u32[]{:S(2)}, u32[]{:S(2)}) collective-permute-start(bf16[4,4,32,128]{3,2,1,0:T(8,128)(2,1)} %param.5), channel_id=1, source_target_pairs={{0,1},{1,0},{2,3},{3,2},{4,5},{5,4},{6,7},{7,6},{8,9},{9,8},{10,11... | collective-permute-start | bytes 393224 | tf_op jit(solution)/shard_map/ppermute | solution.py:10
  6.3 0.1 broadcast_in_dim.31
  6.4 0.9 %copy_dynamic-update-slice_fusion.3 = bf16[4,4,4,32,128]{4,3,1,0,2:T(8,128)(2,1)S(1)} fusion(bf16[4,4,4,32,128]{4,3,1,0,2:T(8,128)(2,1)S(1)} %broadcast_in_dim.31, s32[]{:T(128)S(6)} %select_n.85, bf16[4,4,32,128]{3,2,1,0:T(8,128)(2,1)} %param.5), kind=kLoop, calls=%fused_computation.23 | loop fusion | bytes 262148 | tf_op jit(solution)/shard_map/jit(dynamic_update_index_in_dim)/dynamic_update_slice | solution.py:53
  7.3 0.8 %convert_reduce_fusion = f32[32,4]{0,1:T(4,128)S(1)} fusion(s32[4,16]{1,0:T(4,128)} %param.6), kind=kLoop, calls=%fused_computation.37 | loop fusion | flops 6016 | bytes 768 | tf_op jit(solution)/shard_map/reduce_sum | solution.py:46
  8.1 1.6 %copy.55 = bf16[8,4,128,128]{2,3,1,0:T(8,128)(2,1)S(1)} copy(bf16[8,4,128,128]{3,2,1,0:T(8,128)(2,1)} %param.4) | data formatting | bytes 2097152 | tf_op args[0]
  9.8 0.1 fusion.19
  9.9 1.5 %collective-permute-done = bf16[4,4,32,128]{3,2,1,0:T(8,128)(2,1)S(1)} collective-permute-done((bf16[4,4,32,128]{3,2,1,0:T(8,128)(2,1)}, bf16[4,4,32,128]{3,2,1,0:T(8,128)(2,1)S(1)}, u32[]{:S(2)}, u32[]{:S(2)}) %collective-permute-start) | collective-permute-done | bytes 131104 | tf_op jit(solution)/shard_map/ppermute | solution.py:10
  11.4 0.7 %collective-permute-start.2 = (bf16[4,4,32,128]{3,2,1,0:T(8,128)(2,1)S(1)}, bf16[4,4,32,128]{3,2,1,0:T(8,128)(2,1)S(1)}, u32[]{:S(2)}, u32[]{:S(2)}) collective-permute-start(bf16[4,4,32,128]{3,2,1,0:T(8,128)(2,1)S(1)} %collective-permute-done), channel_id=1, source_target_pairs={{0,1},{1,0},{2,3},{3,2},{4,5},{5,4},{6,7},{7,6},{8,9},{9,8},{10,11... | collective-permute-start | bytes 393224 | tf_op jit(solution)/shard_map/ppermute | solution.py:10
  12.1 0.0 collective-permute-done.1
  12.1 4.2 %collective-permute-done.2 = bf16[4,4,32,128]{3,2,1,0:T(8,128)(2,1)S(1)} collective-permute-done((bf16[4,4,32,128]{3,2,1,0:T(8,128)(2,1)S(1)}, bf16[4,4,32,128]{3,2,1,0:T(8,128)(2,1)S(1)}, u32[]{:S(2)}, u32[]{:S(2)}) %collective-permute-start.2) | collective-permute-done | bytes 131104 | tf_op jit(solution)/shard_map/ppermute | solution.py:10
  16.3 0.8 %fusion.1 = f32[4,128,8,128,1,1]{1,3,5,4,2,0:T(8,128)S(1)} fusion(bf16[8,4,128,4,32]{2,4,3,1,0:T(8,128)(2,1)S(1)} %bitcast.102, bf16[4,4,4,32,128]{4,3,1,0,2:T(8,128)(2,1)S(1)} %copy_dynamic-update-slice_fusion, bf16[4,4]{0,1:T(4,128)(2,1)S(1)} %fusion.19), kind=kOutput, calls=%fused_computation.4 | convolution fusion | flops 537919488 | bytes 3670048 | tf_op jit(solution)/shard_map/ijrcb,cjkbe->rike/dot_general | solution.py:72
  17.1 0.2 constant_dynamic-slice_fusion.6
  17.4 0.0 copy-start
  17.4 0.6 copy.92
  18.0 0.1 collective-permute-start.3
  18.1 0.2 copy-done
  18.3 0.7 %collective-permute-start.7 = (bf16[4,4,16,128]{3,2,1,0:T(8,128)(2,1)S(1)}, bf16[4,4,16,128]{3,2,1,0:T(8,128)(2,1)S(1)}, u32[]{:S(2)}, u32[]{:S(2)}) collective-permute-start(bf16[4,4,16,128]{3,2,1,0:T(8,128)(2,1)S(1)} %get-tuple-element.16), channel_id=1, source_target_pairs={{0,0},{1,8},{2,16},{3,24},{4,4},{5,12},{6,20},{7,28},{8,1},{9,9},{... | collective-permute-start | bytes 196616 | tf_op jit(solution)/shard_map/ppermute | solution.py:65
  19.0 0.4 collective-permute-start.8
  19.4 0.1 fusion.20
  19.4 0.1 fusion.21
  19.5 1.2 %collective-permute-done.3 = f32[4,16,8,4,128]{4,2,3,1,0:T(8,128)S(1)} collective-permute-done((f32[4,16,8,4,128]{4,2,3,1,0:T(8,128)S(1)}, f32[4,16,8,4,128]{4,2,3,1,0:T(8,128)S(1)}, u32[]{:S(2)}, u32[]{:S(2)}) %collective-permute-start.3) | collective-permute-done | bytes 1048608 | tf_op jit(solution)/shard_map/ppermute | solution.py:10
  20.8 0.6 %fusion = f32[4,16,8,4,128]{4,2,3,1,0:T(8,128)S(1)} fusion(f32[4,16,8,4,128]{4,2,3,1,0:T(8,128)S(1)} %collective-permute-done.3, f32[4,1,16,8,4,128]{5,2,1,0,3,4:T(8,128)S(1)} %get-tuple-element.6), kind=kLoop, calls=%fused_computation.3 | loop fusion | flops 262144 | bytes 3145728 | tf_op jit(solution)/shard_map/add | solution.py:74
  21.4 0.1 dynamic-slice_bitcast_fusion.2
  21.5 3.8 %collective-permute-start.4 = (f32[16,8,4,128]{3,1,2,0:T(8,128)S(1)}, f32[16,8,4,128]{3,1,2,0:T(8,128)S(1)}, u32[]{:S(2)}, u32[]{:S(2)}) collective-permute-start(f32[16,8,4,128]{3,1,2,0:T(8,128)S(1)} %get-tuple-element.8), channel_id=1, source_target_pairs={{0,8},{4,12},{8,0},{12,4},{16,24},{20,28},{24,16},{28,20},{1,9},{5... | collective-permute-start | bytes 786440 | tf_op jit(solution)/shard_map/ppermute | solution.py:10
  25.3 4.2 %collective-permute-start.5 = (f32[16,8,4,128]{3,1,2,0:T(8,128)S(1)}, f32[16,8,4,128]{3,1,2,0:T(8,128)S(1)}, u32[]{:S(2)}, u32[]{:S(2)}) collective-permute-start(f32[16,8,4,128]{3,1,2,0:T(8,128)S(1)} %get-tuple-element.10), channel_id=1, source_target_pairs={{0,16},{4,20},{8,24},{12,28},{16,0},{20,4},{24,8},{28,12},{1,17},{... | collective-permute-start | bytes 786440 | tf_op jit(solution)/shard_map/ppermute | solution.py:10
  29.5 0.0 collective-permute-start.6
  29.5 0.0 collective-permute-done.7
  29.6 0.0 copy-start.1
  29.6 6.1 %collective-permute-done.4 = f32[16,8,4,128]{3,1,2,0:T(8,128)S(1)} collective-permute-done((f32[16,8,4,128]{3,1,2,0:T(8,128)S(1)}, f32[16,8,4,128]{3,1,2,0:T(8,128)S(1)}, u32[]{:S(2)}, u32[]{:S(2)}) %collective-permute-start.4) | collective-permute-done | bytes 262176 | tf_op jit(solution)/shard_map/ppermute | solution.py:10
  35.7 6.1 %collective-permute-done.5 = f32[16,8,4,128]{3,1,2,0:T(8,128)S(1)} collective-permute-done((f32[16,8,4,128]{3,1,2,0:T(8,128)S(1)}, f32[16,8,4,128]{3,1,2,0:T(8,128)S(1)}, u32[]{:S(2)}, u32[]{:S(2)}) %collective-permute-start.5) | collective-permute-done | bytes 262176 | tf_op jit(solution)/shard_map/ppermute | solution.py:10
  41.8 0.1 fusion.9
  42.0 0.5 convolution_bitcast_fusion
  42.4 0.1 reshape.27
  42.6 0.1 collective-permute-start.9
  42.6 1.3 %collective-permute-done.9 = f32[4,4,4,512]{3,2,1,0:T(4,128)S(1)} collective-permute-done((f32[4,4,4,512]{3,2,1,0:T(4,128)S(1)}, f32[4,4,4,512]{3,2,1,0:T(4,128)S(1)}, u32[]{:S(2)}, u32[]{:S(2)}) %collective-permute-start.9) | collective-permute-done | bytes 131104 | tf_op jit(solution)/shard_map/ppermute | solution.py:10
  44.1 1.5 %collective-permute-start.10 = (f32[4,4,512]{2,0,1:T(4,128)S(1)}, f32[4,4,512]{2,0,1:T(4,128)S(1)}, u32[]{:S(2)}, u32[]{:S(2)}) collective-permute-start(f32[4,4,512]{2,0,1:T(4,128)S(1)} %bitcast.106), channel_id=1, source_target_pairs={{0,8},{4,12},{8,0},{12,4},{16,24},{20,28},{24,16},{28,20},{1,9},{5... | collective-permute-start | bytes 98312 | tf_op jit(solution)/shard_map/ppermute | solution.py:10
  45.6 2.1 %collective-permute-start.11 = (f32[4,4,512]{2,0,1:T(4,128)S(1)}, f32[4,4,512]{2,0,1:T(4,128)S(1)}, u32[]{:S(2)}, u32[]{:S(2)}) collective-permute-start(f32[4,4,512]{2,0,1:T(4,128)S(1)} %bitcast.107), channel_id=1, source_target_pairs={{0,16},{4,20},{8,24},{12,28},{16,0},{20,4},{24,8},{28,12},{1,17},{... | collective-permute-start | bytes 98312 | tf_op jit(solution)/shard_map/ppermute | solution.py:10
  47.7 0.1 collective-permute-start.12
  47.8 0.2 collective-permute-done.10
  48.1 1.6 %collective-permute-done.11 = f32[4,4,512]{2,0,1:T(4,128)S(1)} collective-permute-done((f32[4,4,512]{2,0,1:T(4,128)S(1)}, f32[4,4,512]{2,0,1:T(4,128)S(1)}, u32[]{:S(2)}, u32[]{:S(2)}) %collective-permute-start.11) | collective-permute-done | bytes 32800 | tf_op jit(solution)/shard_map/ppermute | solution.py:10
  49.6 3.0 %collective-permute-done.12 = f32[4,4,512]{2,0,1:T(4,128)S(1)} collective-permute-done((f32[4,4,512]{2,0,1:T(4,128)S(1)}, f32[4,4,512]{2,0,1:T(4,128)S(1)}, u32[]{:S(2)}, u32[]{:S(2)}) %collective-permute-start.12) | collective-permute-done | bytes 32800 | tf_op jit(solution)/shard_map/ppermute | solution.py:10
  52.7 0.1 collective-permute-start.13
  52.8 2.5 %collective-permute-start.14 = (f32[4,512]{1,0:T(4,128)S(1)}, f32[4,512]{1,0:T(4,128)S(1)}, u32[]{:S(2)}, u32[]{:S(2)}) collective-permute-start(f32[4,512]{1,0:T(4,128)S(1)} %get-tuple-element.19), channel_id=1, source_target_pairs={{0,2},{1,3},{2,0},{3,1},{4,6},{5,7},{6,4},{7,5},{8,10},{9,11},{10,... | collective-permute-start | bytes 24584 | tf_op jit(solution)/shard_map/ppermute | solution.py:10
  55.2 1.9 %collective-permute-start.15 = (f32[4,512]{1,0:T(4,128)S(1)}, f32[4,512]{1,0:T(4,128)S(1)}, u32[]{:S(2)}, u32[]{:S(2)}) collective-permute-start(f32[4,512]{1,0:T(4,128)S(1)} %get-tuple-element.18), channel_id=1, source_target_pairs={{0,3},{1,2},{2,1},{3,0},{4,7},{5,6},{6,5},{7,4},{8,11},{9,10},{10,... | collective-permute-start | bytes 24584 | tf_op jit(solution)/shard_map/ppermute | solution.py:10
  57.1 0.9 %copy.66 = f32[8,4,16,128]{3,2,1,0:T(8,128)} copy(f32[8,4,16,128]{3,0,1,2:T(8,128)S(1)} %fusion.9) | data formatting | bytes 524288
  58.0 2.7 %collective-permute-done.15 = f32[4,512]{1,0:T(4,128)S(1)} collective-permute-done((f32[4,512]{1,0:T(4,128)S(1)}, f32[4,512]{1,0:T(4,128)S(1)}, u32[]{:S(2)}, u32[]{:S(2)}) %collective-permute-start.15) | collective-permute-done | bytes 8224 | tf_op jit(solution)/shard_map/ppermute | solution.py:10
  60.7 0.6 fusion.18
  (20 shorter events, 0.3 us)
Async XLA Ops:
  0.6 10.7 %collective-permute-start = (bf16[4,4,32,128]{3,2,1,0:T(8,128)(2,1)}, bf16[4,4,32,128]{3,2,1,0:T(8,128)(2,1)S(1)}, u32[]{:S(2)}, u32[]{:S(2)}) collective-permute-start(bf16[4,4,32,128]{3,2,1,0:T(8,128)(2,1)} %param.5), channel_id=1, source_target_pairs={{0,2},{1,3},{2,0},{3,1},{4,6},{5,7},{6,4},{7,5},{8,10},{9,11},{10,... | collective-permute-start | bytes 393224 | tf_op jit(solution)/shard_map/ppermute | solution.py:10
  4.7 7.4 %collective-permute-start.1 = (bf16[4,4,32,128]{3,2,1,0:T(8,128)(2,1)}, bf16[4,4,32,128]{3,2,1,0:T(8,128)(2,1)S(1)}, u32[]{:S(2)}, u32[]{:S(2)}) collective-permute-start(bf16[4,4,32,128]{3,2,1,0:T(8,128)(2,1)} %param.5), channel_id=1, source_target_pairs={{0,1},{1,0},{2,3},{3,2},{4,5},{5,4},{6,7},{7,6},{8,9},{9,8},{10,11... | collective-permute-start | bytes 393224 | tf_op jit(solution)/shard_map/ppermute | solution.py:10
  11.4 5.0 %collective-permute-start.2 = (bf16[4,4,32,128]{3,2,1,0:T(8,128)(2,1)S(1)}, bf16[4,4,32,128]{3,2,1,0:T(8,128)(2,1)S(1)}, u32[]{:S(2)}, u32[]{:S(2)}) collective-permute-start(bf16[4,4,32,128]{3,2,1,0:T(8,128)(2,1)S(1)} %collective-permute-done), channel_id=1, source_target_pairs={{0,1},{1,0},{2,3},{3,2},{4,5},{5,4},{6,7},{7,6},{8,9},{9,8},{10,11... | collective-permute-start | bytes 393224 | tf_op jit(solution)/shard_map/ppermute | solution.py:10
  17.4 0.9 %copy-start = (bf16[4,4,32,128]{3,2,1,0:T(8,128)(2,1)S(1)}, bf16[4,4,32,128]{3,2,1,0:T(8,128)(2,1)}, u32[]{:S(2)}) copy-start(bf16[4,4,32,128]{3,2,1,0:T(8,128)(2,1)} %param.5) | copy-start | bytes 393220
  18.0 2.7 %collective-permute-start.3 = (f32[4,16,8,4,128]{4,2,3,1,0:T(8,128)S(1)}, f32[4,16,8,4,128]{4,2,3,1,0:T(8,128)S(1)}, u32[]{:S(2)}, u32[]{:S(2)}) collective-permute-start(f32[4,16,8,4,128]{4,2,3,1,0:T(8,128)S(1)} %bitcast.103), channel_id=1, source_target_pairs={{0,4},{4,0},{8,12},{12,8},{16,20},{20,16},{24,28},{28,24},{1,5},{5... | collective-permute-start | bytes 3145736 | tf_op jit(solution)/shard_map/ppermute | solution.py:10
  18.3 11.2 %collective-permute-start.7 = (bf16[4,4,16,128]{3,2,1,0:T(8,128)(2,1)S(1)}, bf16[4,4,16,128]{3,2,1,0:T(8,128)(2,1)S(1)}, u32[]{:S(2)}, u32[]{:S(2)}) collective-permute-start(bf16[4,4,16,128]{3,2,1,0:T(8,128)(2,1)S(1)} %get-tuple-element.16), channel_id=1, source_target_pairs={{0,0},{1,8},{2,16},{3,24},{4,4},{5,12},{6,20},{7,28},{8,1},{9,9},{... | collective-permute-start | bytes 196616 | tf_op jit(solution)/shard_map/ppermute | solution.py:65
  19.0 10.6 %collective-permute-start.8 = (bf16[4,4,16,128]{3,2,1,0:T(8,128)(2,1)S(1)}, bf16[4,4,16,128]{3,2,1,0:T(8,128)(2,1)S(1)}, u32[]{:S(2)}, u32[]{:S(2)}) collective-permute-start(bf16[4,4,16,128]{3,2,1,0:T(8,128)(2,1)S(1)} %get-tuple-element.15), channel_id=1, source_target_pairs={{0,4},{1,12},{2,20},{3,28},{4,0},{5,8},{6,16},{7,24},{8,5},{9,13},... | collective-permute-start | bytes 196616 | tf_op jit(solution)/shard_map/ppermute | solution.py:65
  21.5 14.3 %collective-permute-start.4 = (f32[16,8,4,128]{3,1,2,0:T(8,128)S(1)}, f32[16,8,4,128]{3,1,2,0:T(8,128)S(1)}, u32[]{:S(2)}, u32[]{:S(2)}) collective-permute-start(f32[16,8,4,128]{3,1,2,0:T(8,128)S(1)} %get-tuple-element.8), channel_id=1, source_target_pairs={{0,8},{4,12},{8,0},{12,4},{16,24},{20,28},{24,16},{28,20},{1,9},{5... | collective-permute-start | bytes 786440 | tf_op jit(solution)/shard_map/ppermute | solution.py:10
  25.3 16.5 %collective-permute-start.5 = (f32[16,8,4,128]{3,1,2,0:T(8,128)S(1)}, f32[16,8,4,128]{3,1,2,0:T(8,128)S(1)}, u32[]{:S(2)}, u32[]{:S(2)}) collective-permute-start(f32[16,8,4,128]{3,1,2,0:T(8,128)S(1)} %get-tuple-element.10), channel_id=1, source_target_pairs={{0,16},{4,20},{8,24},{12,28},{16,0},{20,4},{24,8},{28,12},{1,17},{... | collective-permute-start | bytes 786440 | tf_op jit(solution)/shard_map/ppermute | solution.py:10
  29.5 12.3 %collective-permute-start.6 = (f32[16,8,4,128]{3,1,2,0:T(8,128)S(1)}, f32[16,8,4,128]{3,1,2,0:T(8,128)S(1)}, u32[]{:S(2)}, u32[]{:S(2)}) collective-permute-start(f32[16,8,4,128]{3,1,2,0:T(8,128)S(1)} %get-tuple-element.9), channel_id=1, source_target_pairs={{0,24},{4,28},{8,16},{12,20},{16,8},{20,12},{24,0},{28,4},{1,25},{... | collective-permute-start | bytes 786440 | tf_op jit(solution)/shard_map/ppermute | solution.py:10
  29.6 31.1 %copy-start.1 = (f32[4,512]{1,0:T(4,128)S(1)}, f32[4,512]{1,0:T(4,128)}, u32[]{:S(2)}) copy-start(f32[4,512]{1,0:T(4,128)} %param.7) | copy-start | bytes 24580
  42.6 1.4 %collective-permute-start.9 = (f32[4,4,4,512]{3,2,1,0:T(4,128)S(1)}, f32[4,4,4,512]{3,2,1,0:T(4,128)S(1)}, u32[]{:S(2)}, u32[]{:S(2)}) collective-permute-start(f32[4,4,4,512]{3,2,1,0:T(4,128)S(1)} %dynamic-slice_bitcast_fusion.3), channel_id=1, source_target_pairs={{0,4},{4,0},{8,12},{12,8},{16,20},{20,16},{24,28},{28,24},{1,5},{5... | collective-permute-start | bytes 393224 | tf_op jit(solution)/shard_map/ppermute | solution.py:10
  44.1 4.0 %collective-permute-start.10 = (f32[4,4,512]{2,0,1:T(4,128)S(1)}, f32[4,4,512]{2,0,1:T(4,128)S(1)}, u32[]{:S(2)}, u32[]{:S(2)}) collective-permute-start(f32[4,4,512]{2,0,1:T(4,128)S(1)} %bitcast.106), channel_id=1, source_target_pairs={{0,8},{4,12},{8,0},{12,4},{16,24},{20,28},{24,16},{28,20},{1,9},{5... | collective-permute-start | bytes 98312 | tf_op jit(solution)/shard_map/ppermute | solution.py:10
  45.6 4.0 %collective-permute-start.11 = (f32[4,4,512]{2,0,1:T(4,128)S(1)}, f32[4,4,512]{2,0,1:T(4,128)S(1)}, u32[]{:S(2)}, u32[]{:S(2)}) collective-permute-start(f32[4,4,512]{2,0,1:T(4,128)S(1)} %bitcast.107), channel_id=1, source_target_pairs={{0,16},{4,20},{8,24},{12,28},{16,0},{20,4},{24,8},{28,12},{1,17},{... | collective-permute-start | bytes 98312 | tf_op jit(solution)/shard_map/ppermute | solution.py:10
  47.7 4.9 %collective-permute-start.12 = (f32[4,4,512]{2,0,1:T(4,128)S(1)}, f32[4,4,512]{2,0,1:T(4,128)S(1)}, u32[]{:S(2)}, u32[]{:S(2)}) collective-permute-start(f32[4,4,512]{2,0,1:T(4,128)S(1)} %bitcast.108), channel_id=1, source_target_pairs={{0,24},{4,28},{8,16},{12,20},{16,8},{20,12},{24,0},{28,4},{1,25},{... | collective-permute-start | bytes 98312 | tf_op jit(solution)/shard_map/ppermute | solution.py:10
  52.7 5.3 %collective-permute-start.13 = (f32[4,512]{1,0:T(4,128)S(1)}, f32[4,512]{1,0:T(4,128)S(1)}, u32[]{:S(2)}, u32[]{:S(2)}) collective-permute-start(f32[4,512]{1,0:T(4,128)S(1)} %get-tuple-element.17), channel_id=1, source_target_pairs={{0,1},{1,0},{2,3},{3,2},{4,5},{5,4},{6,7},{7,6},{8,9},{9,8},{10,11... | collective-permute-start | bytes 24584 | tf_op jit(solution)/shard_map/ppermute | solution.py:10
  52.8 5.2 %collective-permute-start.14 = (f32[4,512]{1,0:T(4,128)S(1)}, f32[4,512]{1,0:T(4,128)S(1)}, u32[]{:S(2)}, u32[]{:S(2)}) collective-permute-start(f32[4,512]{1,0:T(4,128)S(1)} %get-tuple-element.19), channel_id=1, source_target_pairs={{0,2},{1,3},{2,0},{3,1},{4,6},{5,7},{6,4},{7,5},{8,10},{9,11},{10,... | collective-permute-start | bytes 24584 | tf_op jit(solution)/shard_map/ppermute | solution.py:10
  55.2 5.4 %collective-permute-start.15 = (f32[4,512]{1,0:T(4,128)S(1)}, f32[4,512]{1,0:T(4,128)S(1)}, u32[]{:S(2)}, u32[]{:S(2)}) collective-permute-start(f32[4,512]{1,0:T(4,128)S(1)} %get-tuple-element.18), channel_id=1, source_target_pairs={{0,3},{1,2},{2,1},{3,0},{4,7},{5,6},{6,5},{7,4},{8,11},{9,10},{10,... | collective-permute-start | bytes 24584 | tf_op jit(solution)/shard_map/ppermute | solution.py:10

commit v2 on v1

v2 whole, which is shorter than its diff:
```python
import jax
import jax.numpy as jnp
from jax import lax
from jax.sharding import PartitionSpec as P

CORES = 2
HEADROOM = 14.0


def swap(value, axis, size, step):
    return lax.ppermute(value, axis, [(at, at ^ step) for at in range(size)])


def take(value, index, axis):
    return lax.dynamic_index_in_dim(value, index, axis, keepdims=False)


def tied(*values):
    return lax.optimization_barrier(values)


def largest(value):
    return jnp.max(jnp.abs(value)).astype(jnp.float32)


def gather_pieces(piece, axis, size):
    held = {0: piece}
    step = size // 2
    while step:
        held.update({at ^ step: swap(held[at], axis, size, step) for at in sorted(held)})
        step //= 2
    return held


def forward(piece, at, col_groups):
    pairs = []
    for z in range(col_groups):
        for k in range(CORES):
            source, target = z * CORES + k, (z ^ at) * CORES + k
            pairs.append((source * col_groups + z, target * col_groups + z))
    return lax.ppermute(piece, ("prow", "pcol"), pairs)


def per_device(inverse_blocks, lower_blocks, pattern, diag_inverse):
    blocks_i, blocks_j, width, _ = inverse_blocks.shape
    node_count = lower_blocks.shape[1]
    row_groups = lax.axis_size("prow")
    col_groups = lax.axis_size("pcol")
    chips = row_groups // CORES
    block_count = blocks_j * row_groups
    prow, pcol = lax.axis_index("prow"), lax.axis_index("pcol")
    chip, core = prow // CORES, prow % CORES
    rows = width // row_groups

    matches = pattern[None, :, :] == jnp.arange(block_count, dtype=jnp.int32)[:, None, None]
    present = jnp.sum(matches.astype(jnp.float32), axis=2)
    keep_j = lax.dynamic_slice_in_dim(present, prow * blocks_j, blocks_j, 0)
    keep_i = lax.dynamic_slice_in_dim(present, pcol * blocks_i, blocks_i, 0)

    held = gather_pieces(lower_blocks, "pcol", col_groups)
    by_core = []
    for at in range(col_groups):
        split = held[at].reshape(blocks_j, node_count, CORES, rows, width)
        mine = take(split, core, 2)
        other = swap(take(split, 1 - core, 2), "prow", row_groups, 1)
        both = jnp.stack([jnp.where(core == 0, mine, other), jnp.where(core == 0, other, mine)])
        by_core.append(both.reshape(blocks_i, node_count, rows, width))
    own = by_core[0] * (chip == pcol).astype(lower_blocks.dtype)
    first = forward(by_core[1], 1, col_groups)

    whole = jnp.zeros((col_groups,) + lower_blocks.shape, lower_blocks.dtype)
    for at, piece in held.items():
        whole = lax.dynamic_update_index_in_dim(whole, piece, pcol ^ at, 0)
    masked = whole * keep_j.astype(jnp.bfloat16)[None, :, :, None, None]

    inv = inverse_blocks.reshape(blocks_i, blocks_j, width, col_groups, width // col_groups)
    partial_sums = jnp.einsum("ijrcb,cjkbe->rike", inv, masked, preferred_element_type=jnp.float32)
    partial_sums = partial_sums.reshape(chips, CORES, rows, blocks_i, node_count, width)
    sent, first = tied(take(partial_sums, 1 - core, 1), first)
    own = own + first
    pair_sums = take(partial_sums, core, 1) + swap(sent, "prow", row_groups, 1)
    top = jnp.max(jnp.abs(pair_sums), axis=(0, 1, 2, 3))
    power = jnp.maximum(jnp.ceil(jnp.log2(top)), -110.0)
    packed = (pair_sums * jnp.exp2(HEADROOM - power)).astype(jnp.float16).reshape(chips, -1, width)
    mark = jnp.broadcast_to(power.astype(jnp.float16), (chips, 16, width))
    packed = jnp.concatenate([packed, mark], axis=1)
    pieces = [take(packed, chip ^ step, 0) for step in range(1, chips)]
    later = by_core[2:]
    pieces, later = tied(pieces, later)
    for at in range(2, col_groups):
        own = own + forward(later[at - 2], at, col_groups)
    own = own * keep_i.astype(jnp.bfloat16)[:, :, None, None]
    summed = take(pair_sums, chip, 0)
    for step in range(1, chips):
        came = swap(pieces[step - 1], "prow", row_groups, step * CORES)
        came = lax.optimization_barrier(came.astype(jnp.float32))
        summed = summed + (came[:-16] * jnp.exp2(came[-1] - HEADROOM)).reshape(summed.shape)
    column = jnp.transpose(summed, (1, 2, 0, 3)) * (-keep_i)[:, :, None, None]

    parts = row_groups * col_groups
    wide = own.astype(jnp.float32)
    if width % parts == 0:
        update = jnp.einsum("ikra,ikrb->akb", wide, column, precision=lax.Precision.HIGHEST)
        update = update.reshape(parts, width // parts, node_count, width)
        update = jnp.sum(lax.all_to_all(update, ("prow", "pcol"), 0, 0, tiled=True), axis=0)
        update = jnp.transpose(update, (1, 0, 2)).reshape(diag_inverse.shape)
    else:
        update = jnp.einsum("ikra,ikrb->kab", wide, column, precision=lax.Precision.HIGHEST)
        update = update.reshape(node_count, parts, width * width // parts)
        update = jnp.sum(lax.all_to_all(update, ("prow", "pcol"), 1, 1, tiled=True), axis=1)
    return column, diag_inverse - update


def solution(mesh):
    placed = (
        P("pcol", "prow", None, None),
        P("prow", None, "pcol", None),
        P(),
        P(None, ("prow", "pcol")),
    )
    return jax.shard_map(
        per_device,
        mesh=mesh,
        in_specs=placed,
        out_specs=(P("pcol", None, "prow", None), P(None, ("prow", "pcol"))),
        check_vma=False,
    )
```

time: 61.5 us -> 54.2 us (0.88)
  waiting for transfers between devices: 27.9 us -> 16.2 us
  local copies, waits for them, and re-layouts: 5.08 us -> 7.43 us
  other arithmetic: 2.27 us -> 3.65 us
    ppermute x14 -> x11, waiting for transfers between devices: 27.9 us -> 4.19 us  [swap(): return lax.ppermute(value, axis, [(at, at ^ step) for at in range(size)])]
    ppermute x14 -> x11, starting transfers between devices: 22.8 us -> 12 us  [swap(): return lax.ppermute(value, axis, [(at, at ^ step) for at in range(size)])]
    all_to_all x0 -> x1, waiting for transfers between devices: none -> 9.34 us  [per_device(): lax.all_to_all(update, ('prow', 'pcol'), 0, 0, tiled=True)]
    ppermute x2 -> x3, starting transfers between devices: 1.03 us -> 8.15 us  [forward(): return lax.ppermute(piece, ('prow', 'pcol'), pairs)]
    all_to_all x0 -> x1, starting transfers between devices: none -> 4.18 us  [per_device(): lax.all_to_all(update, ('prow', 'pcol'), 0, 0, tiled=True)]
    ppermute x2 -> x3, waiting for transfers between devices: 0.01 us -> 2.7 us  [forward(): return lax.ppermute(piece, ('prow', 'pcol'), pairs)]
    squeeze x4, local copies, waits for them, and re-layouts: 0.1 us -> 1.53 us  [take(): return lax.dynamic_index_in_dim(value, index, axis, keepdims=False)]
    another operation x0 -> x7, other arithmetic: none -> 0.95 us  [per_device(): jnp.stack([jnp.where(core == 0, mine, other), jnp.where(core == 0, other,...]
  transfers between devices with their start and end apart: 16 -> 15, of which waited for: 10 -> 8; matrix products, arithmetic and copies ran while one was open for 9% -> 19% of each run, Pallas kernels for 0% -> 0%
where the time goes in v2:
time: 54.2 us; the launch traced here: 53.8 us
  starting transfers between devices  24.3 us (45%)
  waiting for transfers between devices  16.2 us (30%)
  local copies, waits for them, and re-layouts  7.43 us (14%)
  other arithmetic  3.65 us (7%)
  matrix products  1.19 us (2%)
  between operations  0.99 us (2%)
    ppermute x11, starting transfers between devices, swap(): return lax.ppermute(value, axis, [(at, at ^ step) for at in range(size)])  12 us
    all_to_all x1, waiting for transfers between devices, per_device(): lax.all_to_all(update, ('prow', 'pcol'), 0, 0, tiled=True)  9.34 us
    ppermute x3, starting transfers between devices, forward(): return lax.ppermute(piece, ('prow', 'pcol'), pairs)  8.15 us
    ppermute x11, waiting for transfers between devices, swap(): return lax.ppermute(value, axis, [(at, at ^ step) for at in range(size)])  4.19 us
    all_to_all x1, starting transfers between devices, per_device(): lax.all_to_all(update, ('prow', 'pcol'), 0, 0, tiled=True)  4.18 us
    unnamed x7, local copies, waits for them, and re-layouts  3.1 us
    ppermute x3, waiting for transfers between devices, forward(): return lax.ppermute(piece, ('prow', 'pcol'), pairs)  2.7 us
    squeeze x4, local copies, waits for them, and re-layouts, take(): return lax.dynamic_index_in_dim(value, index, axis, keepdims=False)  1.53 us
  transfers between devices with their start and end apart: 15, of which 8 were waited for; matrix products, arithmetic and copies ran while one was open for 19% of the time, Pallas kernels for 0%

profile of v2, /device:TPU:0, one launch (start us, length us, event | category | flops | bytes accessed | tf_op | source)
XLA Modules:
  0.0 53.8 jit_solution(14272758495043966320)
XLA Ops:
  0.6 4.1 %collective-permute-start = (bf16[4,4,32,128]{3,2,1,0:T(8,128)(2,1)}, bf16[4,4,32,128]{3,2,1,0:T(8,128)(2,1)S(1)}, u32[]{:S(2)}, u32[]{:S(2)}) collective-permute-start(bf16[4,4,32,128]{3,2,1,0:T(8,128)(2,1)} %param.5), channel_id=1, source_target_pairs={{0,2},{1,3},{2,0},{3,1},{4,6},{5,7},{6,4},{7,5},{8,10},{9,11},{10,... | collective-permute-start | bytes 393224 | tf_op jit(solution)/shard_map/ppermute | solution.py:11
  4.7 1.6 %collective-permute-start.1 = (bf16[4,4,32,128]{3,2,1,0:T(8,128)(2,1)}, bf16[4,4,32,128]{3,2,1,0:T(8,128)(2,1)S(1)}, u32[]{:S(2)}, u32[]{:S(2)}) collective-permute-start(bf16[4,4,32,128]{3,2,1,0:T(8,128)(2,1)} %param.5), channel_id=1, source_target_pairs={{0,1},{1,0},{2,3},{3,2},{4,5},{5,4},{6,7},{7,6},{8,9},{9,8},{10,11... | collective-permute-start | bytes 393224 | tf_op jit(solution)/shard_map/ppermute | solution.py:11
  6.3 1.5 %dynamic-slice_bitcast_fusion = bf16[4,4,16,128]{3,2,1,0:T(8,128)(2,1)} fusion(bf16[4,4,2,16,128]{4,3,2,1,0:T(8,128)(2,1)} %bitcast.143, s32[]{:T(128)S(6)} %select_n.103), kind=kLoop, calls=%fused_computation.61 | loop fusion | bytes 131076 | tf_op jit(solution)/shard_map/jit(dynamic_index_in_dim)/squeeze | solution.py:15
  7.8 0.0 collective-permute-start.11
  7.8 0.1 broadcast_in_dim.28
  7.9 0.9 %copy_dynamic-update-slice_fusion.3 = bf16[4,4,4,32,128]{4,3,1,0,2:T(8,128)(2,1)S(1)} fusion(bf16[4,4,4,32,128]{4,3,1,0,2:T(8,128)(2,1)S(1)} %broadcast_in_dim.28, s32[]{:T(128)S(6)} %select_n.96, bf16[4,4,32,128]{3,2,1,0:T(8,128)(2,1)} %param.5), kind=kLoop, calls=%fused_computation.43 | loop fusion | bytes 262148 | tf_op jit(solution)/shard_map/jit(dynamic_update_index_in_dim)/dynamic_update_slice | solution.py:73
  8.9 0.8 %convert_reduce_fusion = f32[32,4]{0,1:T(4,128)S(1)} fusion(s32[4,16]{1,0:T(4,128)} %param.6), kind=kLoop, calls=%fused_computation.65 | loop fusion | flops 6016 | bytes 768 | tf_op jit(solution)/shard_map/reduce_sum | solution.py:56
  9.6 0.1 fusion.31
  9.7 1.6 %copy.75 = bf16[8,4,128,128]{2,3,1,0:T(8,128)(2,1)S(1)} copy(bf16[8,4,128,128]{3,2,1,0:T(8,128)(2,1)} %param.4) | data formatting | bytes 2097152 | tf_op args[0]
  11.3 0.2 collective-permute-done.1
  11.6 0.4 collective-permute-start.3
  12.0 0.0 collective-permute-done
  12.0 1.1 %collective-permute-start.2 = (bf16[4,4,32,128]{3,2,1,0:T(8,128)(2,1)S(1)}, bf16[4,4,32,128]{3,2,1,0:T(8,128)(2,1)S(1)}, u32[]{:S(2)}, u32[]{:S(2)}) collective-permute-start(bf16[4,4,32,128]{3,2,1,0:T(8,128)(2,1)S(1)} %collective-permute-done), channel_id=1, source_target_pairs={{0,1},{1,0},{2,3},{3,2},{4,5},{5,4},{6,7},{7,6},{8,9},{9,8},{10,11... | collective-permute-start | bytes 393224 | tf_op jit(solution)/shard_map/ppermute | solution.py:11
  13.2 0.1 copy.79
  13.3 3.4 %collective-permute-start.4 = (bf16[8,4,16,128]{3,0,1,2:T(8,128)(2,1)S(1)}, bf16[8,4,16,128]{3,0,1,2:T(8,128)(2,1)S(1)}, u32[]{:S(2)}, u32[]{:S(2)}) collective-permute-start(bf16[8,4,16,128]{3,0,1,2:T(8,128)(2,1)S(1)} %copy.79), channel_id=1, source_target_pairs={{0,8},{4,12},{9,1},{13,5},{18,26},{22,30},{27,19},{31,23}} | collective-permute-start | bytes 393224 | tf_op jit(solution)/shard_map/ppermute | solution.py:41
  16.7 0.8 %collective-permute-done.2 = bf16[4,4,32,128]{3,2,1,0:T(8,128)(2,1)S(1)} collective-permute-done((bf16[4,4,32,128]{3,2,1,0:T(8,128)(2,1)S(1)}, bf16[4,4,32,128]{3,2,1,0:T(8,128)(2,1)S(1)}, u32[]{:S(2)}, u32[]{:S(2)}) %collective-permute-start.2) | collective-permute-done | bytes 131104 | tf_op jit(solution)/shard_map/ppermute | solution.py:11
  17.5 0.8 %fusion.1 = f32[4,128,8,128,1,1]{1,3,5,4,2,0:T(8,128)S(1)} fusion(bf16[8,4,128,4,32]{2,4,3,1,0:T(8,128)(2,1)S(1)} %bitcast.135, bf16[4,4,4,32,128]{4,3,1,0,2:T(8,128)(2,1)S(1)} %copy_dynamic-update-slice_fusion, bf16[4,4]{0,1:T(4,128)(2,1)S(1)} %fusion.31), kind=kOutput, calls=%fused_computation.3 | convolution fusion | flops 537919488 | bytes 3670048 | tf_op jit(solution)/shard_map/ijrcb,cjkbe->rike/dot_general | solution.py:77
  18.3 0.2 constant_dynamic-slice_fusion.2
  18.6 0.6 %copy.119 = f32[4,1,16,8,4,128]{5,3,4,2,1,0:T(8,128)S(1)} copy(f32[4,1,16,8,4,128]{5,2,1,0,3,4:T(8,128)S(1)} %get-tuple-element.27) | data formatting | bytes 2097152
  19.2 0.6 %collective-permute-done.4 = bf16[8,4,16,128]{3,0,1,2:T(8,128)(2,1)S(1)} collective-permute-done((bf16[8,4,16,128]{3,0,1,2:T(8,128)(2,1)S(1)}, bf16[8,4,16,128]{3,0,1,2:T(8,128)(2,1)S(1)}, u32[]{:S(2)}, u32[]{:S(2)}) %collective-permute-start.4) | collective-permute-done | bytes 131104 | tf_op jit(solution)/shard_map/ppermute | solution.py:41
  19.8 0.1 fusion.33
  19.8 0.5 collective-permute-start.6
  20.4 0.1 fusion.32
  20.4 2.1 %collective-permute-done.6 = bf16[4,4,16,128]{3,2,1,0:T(8,128)(2,1)S(1)} collective-permute-done((bf16[4,4,16,128]{3,2,1,0:T(8,128)(2,1)S(1)}, bf16[4,4,16,128]{3,2,1,0:T(8,128)(2,1)S(1)}, u32[]{:S(2)}, u32[]{:S(2)}) %collective-permute-start.6) | collective-permute-done | bytes 65568 | tf_op jit(solution)/shard_map/ppermute | solution.py:11
  22.6 0.2 collective-permute-start.7
  22.8 1.1 %collective-permute-done.7 = bf16[4,4,16,128]{3,2,1,0:T(8,128)(2,1)S(1)} collective-permute-done((bf16[4,4,16,128]{3,2,1,0:T(8,128)(2,1)S(1)}, bf16[4,4,16,128]{3,2,1,0:T(8,128)(2,1)S(1)}, u32[]{:S(2)}, u32[]{:S(2)}) %collective-permute-start.7) | collective-permute-done | bytes 65568 | tf_op jit(solution)/shard_map/ppermute | solution.py:11
  23.9 0.6 %abs_reduce_fusion = (f32[128]{0:T(128)S(1)}, f32[4,16,8,4,128]{4,2,3,1,0:T(8,128)S(1)}) fusion(f32[4,16,8,4,128]{4,2,3,1,0:T(8,128)S(1)} %collective-permute-done.5, f32[4,1,16,8,4,128]{5,2,1,0,3,4:T(8,128)S(1)} %get-tuple-element.26), kind=kLoop, calls=%fused_computation.7 | loop fusion | flops 786304 | bytes 3146240 | tf_op jit(solution)/shard_map/reduce_max | solution.py:82
  24.6 0.1 multiply_convert_fusion
  24.7 0.3 copy.80
  25.1 0.1 fusion.16
  25.2 2.0 %collective-permute-start.10 = (f16[528,128]{1,0:T(8,128)(2,1)S(1)}, f16[528,128]{1,0:T(8,128)(2,1)S(1)}, u32[]{:S(2)}, u32[]{:S(2)}) collective-permute-start(f16[528,128]{1,0:T(8,128)(2,1)S(1)} %get-tuple-element.12), channel_id=1, source_target_pairs={{0,24},{4,28},{8,16},{12,20},{16,8},{20,12},{24,0},{28,4},{1,25},{... | collective-permute-start | bytes 405512 | tf_op jit(solution)/shard_map/ppermute | solution.py:11
  27.2 0.9 %fusion.22 = (bf16[1,4,4,16,128]{4,3,2,1,0:T(8,128)(2,1)S(1)}, bf16[1,4,4,16,128]{4,3,2,1,0:T(8,128)(2,1)S(1)}) fusion(bf16[4,4,16,128]{3,2,1,0:T(8,128)(2,1)} %collective-permute-done.11, pred[]{:T(512)S(6)} %eq.15, bf16[4,4,2,16,128]{4,3,2,1,0:T(8,128)(2,1)S(1)} %bitcast.144, s32[]{:T(128)S(6)} %select_n.102), kind=kLoop, calls=%fused_computation.46 | loop fusion | flops 65536 | bytes 262149 | tf_op jit(solution)/shard_map/stack | solution.py:66
  28.1 2.0 %collective-permute-start.9 = (f16[528,128]{1,0:T(8,128)(2,1)S(1)}, f16[528,128]{1,0:T(8,128)(2,1)S(1)}, u32[]{:S(2)}, u32[]{:S(2)}) collective-permute-start(f16[528,128]{1,0:T(8,128)(2,1)S(1)} %get-tuple-element.11), channel_id=1, source_target_pairs={{0,16},{4,20},{8,24},{12,28},{16,0},{20,4},{24,8},{28,12},{1,17},{... | collective-permute-start | bytes 405512 | tf_op jit(solution)/shard_map/ppermute | solution.py:11
  30.2 0.1 copy.86
  30.3 3.4 %collective-permute-start.13 = (bf16[8,4,16,128]{3,0,1,2:T(8,128)(2,1)S(1)}, bf16[8,4,16,128]{3,0,1,2:T(8,128)(2,1)S(1)}, u32[]{:S(2)}, u32[]{:S(2)}) collective-permute-start(bf16[8,4,16,128]{3,0,1,2:T(8,128)(2,1)S(1)} %copy.86), channel_id=1, source_target_pairs={{0,24},{4,28},{9,17},{13,21},{18,10},{22,14},{27,3},{31,7}} | collective-permute-start | bytes 393224 | tf_op jit(solution)/shard_map/ppermute | solution.py:41
  33.7 0.1 copy.85
  33.8 1.3 %collective-permute-start.12 = (bf16[8,4,16,128]{3,0,1,2:T(8,128)(2,1)S(1)}, bf16[8,4,16,128]{3,0,1,2:T(8,128)(2,1)S(1)}, u32[]{:S(2)}, u32[]{:S(2)}) collective-permute-start(bf16[8,4,16,128]{3,0,1,2:T(8,128)(2,1)S(1)} %copy.85), channel_id=1, source_target_pairs={{0,16},{4,20},{9,25},{13,29},{18,2},{22,6},{27,11},{31,15}} | collective-permute-start | bytes 393224 | tf_op jit(solution)/shard_map/ppermute | solution.py:41
  35.4 0.0 copy-start.1
  35.4 0.1 fusion.9
  35.5 0.7 %collective-permute-done.13 = bf16[8,4,16,128]{3,0,1,2:T(8,128)(2,1)S(1)} collective-permute-done((bf16[8,4,16,128]{3,0,1,2:T(8,128)(2,1)S(1)}, bf16[8,4,16,128]{3,0,1,2:T(8,128)(2,1)S(1)}, u32[]{:S(2)}, u32[]{:S(2)}) %collective-permute-start.13) | collective-permute-done | bytes 131104 | tf_op jit(solution)/shard_map/ppermute | solution.py:41
  36.2 1.4 %collective-permute-done.12 = bf16[8,4,16,128]{3,0,1,2:T(8,128)(2,1)S(1)} collective-permute-done((bf16[8,4,16,128]{3,0,1,2:T(8,128)(2,1)S(1)}, bf16[8,4,16,128]{3,0,1,2:T(8,128)(2,1)S(1)}, u32[]{:S(2)}, u32[]{:S(2)}) %collective-permute-start.12) | collective-permute-done | bytes 131104 | tf_op jit(solution)/shard_map/ppermute | solution.py:41
  37.6 0.4 fusion.20
  38.0 0.7 %copy.87 = f32[32,4,4,128]{3,1,2,0:T(4,128)} copy(f32[32,4,4,128]{3,1,0,2:T(4,128)S(1)} %bitcast.140) | data formatting | bytes 524288 | tf_op jit(solution)/shard_map/reshape | solution.py:104
  38.8 4.2 %all-to-all-start = ((f32[32,4,4,128]{3,1,2,0:T(4,128)}), f32[32,4,4,128]{3,1,2,0:T(4,128)S(1)}, u32[]{:S(2)}, u32[]{:S(2)}) async-start(f32[32,4,4,128]{3,1,2,0:T(4,128)} %copy.87), calls=%async_computation | async-start | bytes 524288 | tf_op jit(solution)/shard_map/all_to_all | solution.py:105
  42.9 0.9 %copy.88 = f32[8,4,16,128]{3,2,1,0:T(8,128)} copy(f32[8,4,16,128]{3,0,1,2:T(8,128)S(1)} %fusion.9) | data formatting | bytes 524288
  43.8 9.3 %all-to-all-done = f32[32,4,4,128]{3,1,2,0:T(4,128)S(1)} async-done(((f32[32,4,4,128]{3,1,2,0:T(4,128)}), f32[32,4,4,128]{3,1,2,0:T(4,128)S(1)}, u32[]{:S(2)}, u32[]{:S(2)}) %all-to-all-start) | async-done | bytes 262176 | tf_op jit(solution)/shard_map/all_to_all | solution.py:105
  53.1 0.1 reduce_sum.19
  53.2 0.6 %bitcast_subtract_fusion = f32[4,512]{1,0:T(4,128)} fusion(f32[4,512]{1,0:T(4,128)S(1)} %copy-done.1, f32[1,4,4,128]{3,2,1,0:T(4,128)S(1)} %bitcast.154), kind=kLoop, calls=%fused_computation.67 | loop fusion | flops 2048 | bytes 24576 | tf_op jit(solution)/shard_map/sub | solution.py:111
  (35 shorter events, 0.4 us)
Async XLA Ops:
  0.6 11.3 %collective-permute-start = (bf16[4,4,32,128]{3,2,1,0:T(8,128)(2,1)}, bf16[4,4,32,128]{3,2,1,0:T(8,128)(2,1)S(1)}, u32[]{:S(2)}, u32[]{:S(2)}) collective-permute-start(bf16[4,4,32,128]{3,2,1,0:T(8,128)(2,1)} %param.5), channel_id=1, source_target_pairs={{0,2},{1,3},{2,0},{3,1},{4,6},{5,7},{6,4},{7,5},{8,10},{9,11},{10,... | collective-permute-start | bytes 393224 | tf_op jit(solution)/shard_map/ppermute | solution.py:11
  4.7 6.8 %collective-permute-start.1 = (bf16[4,4,32,128]{3,2,1,0:T(8,128)(2,1)}, bf16[4,4,32,128]{3,2,1,0:T(8,128)(2,1)S(1)}, u32[]{:S(2)}, u32[]{:S(2)}) collective-permute-start(bf16[4,4,32,128]{3,2,1,0:T(8,128)(2,1)} %param.5), channel_id=1, source_target_pairs={{0,1},{1,0},{2,3},{3,2},{4,5},{5,4},{6,7},{7,6},{8,9},{9,8},{10,11... | collective-permute-start | bytes 393224 | tf_op jit(solution)/shard_map/ppermute | solution.py:11
  7.8 19.4 %collective-permute-start.11 = (bf16[4,4,16,128]{3,2,1,0:T(8,128)(2,1)}, bf16[4,4,16,128]{3,2,1,0:T(8,128)(2,1)}, u32[]{:S(2)}, u32[]{:S(2)}) collective-permute-start(bf16[4,4,16,128]{3,2,1,0:T(8,128)(2,1)} %dynamic-slice_bitcast_fusion), channel_id=1, source_target_pairs={{0,4},{4,0},{8,12},{12,8},{16,20},{20,16},{24,28},{28,24},{1,5},{5... | collective-permute-start | bytes 196616 | tf_op jit(solution)/shard_map/ppermute | solution.py:11
  11.6 1.6 %collective-permute-start.3 = (bf16[4,4,16,128]{3,2,1,0:T(8,128)(2,1)S(1)}, bf16[4,4,16,128]{3,2,1,0:T(8,128)(2,1)S(1)}, u32[]{:S(2)}, u32[]{:S(2)}) collective-permute-start(bf16[4,4,16,128]{3,2,1,0:T(8,128)(2,1)S(1)} %dynamic-slice_bitcast_fusion.3), channel_id=1, source_target_pairs={{0,4},{4,0},{8,12},{12,8},{16,20},{20,16},{24,28},{28,24},{1,5},{5... | collective-permute-start | bytes 196616 | tf_op jit(solution)/shard_map/ppermute | solution.py:11
  12.0 5.5 %collective-permute-start.2 = (bf16[4,4,32,128]{3,2,1,0:T(8,128)(2,1)S(1)}, bf16[4,4,32,128]{3,2,1,0:T(8,128)(2,1)S(1)}, u32[]{:S(2)}, u32[]{:S(2)}) collective-permute-start(bf16[4,4,32,128]{3,2,1,0:T(8,128)(2,1)S(1)} %collective-permute-done), channel_id=1, source_target_pairs={{0,1},{1,0},{2,3},{3,2},{4,5},{5,4},{6,7},{7,6},{8,9},{9,8},{10,11... | collective-permute-start | bytes 393224 | tf_op jit(solution)/shard_map/ppermute | solution.py:11
  13.3 6.5 %collective-permute-start.4 = (bf16[8,4,16,128]{3,0,1,2:T(8,128)(2,1)S(1)}, bf16[8,4,16,128]{3,0,1,2:T(8,128)(2,1)S(1)}, u32[]{:S(2)}, u32[]{:S(2)}) collective-permute-start(bf16[8,4,16,128]{3,0,1,2:T(8,128)(2,1)S(1)} %copy.79), channel_id=1, source_target_pairs={{0,8},{4,12},{9,1},{13,5},{18,26},{22,30},{27,19},{31,23}} | collective-permute-start | bytes 393224 | tf_op jit(solution)/shard_map/ppermute | solution.py:41
  19.8 4.2 %collective-permute-start.5 = (f32[4,16,8,4,128]{4,2,3,1,0:T(8,128)S(1)}, f32[4,16,8,4,128]{4,2,3,1,0:T(8,128)S(1)}, u32[]{:S(2)}, u32[]{:S(2)}) collective-permute-start(f32[4,16,8,4,128]{4,2,3,1,0:T(8,128)S(1)} %bitcast.141), channel_id=1, source_target_pairs={{0,4},{4,0},{8,12},{12,8},{16,20},{20,16},{24,28},{28,24},{1,5},{5... | collective-permute-start | bytes 3145736 | tf_op jit(solution)/shard_map/ppermute | solution.py:11
  19.8 2.7 %collective-permute-start.6 = (bf16[4,4,16,128]{3,2,1,0:T(8,128)(2,1)S(1)}, bf16[4,4,16,128]{3,2,1,0:T(8,128)(2,1)S(1)}, u32[]{:S(2)}, u32[]{:S(2)}) collective-permute-start(bf16[4,4,16,128]{3,2,1,0:T(8,128)(2,1)S(1)} %dynamic-slice_bitcast_fusion.2), channel_id=1, source_target_pairs={{0,4},{4,0},{8,12},{12,8},{16,20},{20,16},{24,28},{28,24},{1,5},{5... | collective-permute-start | bytes 196616 | tf_op jit(solution)/shard_map/ppermute | solution.py:11
  22.6 1.3 %collective-permute-start.7 = (bf16[4,4,16,128]{3,2,1,0:T(8,128)(2,1)S(1)}, bf16[4,4,16,128]{3,2,1,0:T(8,128)(2,1)S(1)}, u32[]{:S(2)}, u32[]{:S(2)}) collective-permute-start(bf16[4,4,16,128]{3,2,1,0:T(8,128)(2,1)S(1)} %dynamic-slice_bitcast_fusion.1), channel_id=1, source_target_pairs={{0,4},{4,0},{8,12},{12,8},{16,20},{20,16},{24,28},{28,24},{1,5},{5... | collective-permute-start | bytes 196616 | tf_op jit(solution)/shard_map/ppermute | solution.py:11
  24.6 2.7 %copy-start = (bf16[4,4,32,128]{3,2,1,0:T(8,128)(2,1)S(1)}, bf16[4,4,32,128]{3,2,1,0:T(8,128)(2,1)}, u32[]{:S(2)}) copy-start(bf16[4,4,32,128]{3,2,1,0:T(8,128)(2,1)} %param.5) | copy-start | bytes 393220
  25.2 9.9 %collective-permute-start.10 = (f16[528,128]{1,0:T(8,128)(2,1)S(1)}, f16[528,128]{1,0:T(8,128)(2,1)S(1)}, u32[]{:S(2)}, u32[]{:S(2)}) collective-permute-start(f16[528,128]{1,0:T(8,128)(2,1)S(1)} %get-tuple-element.12), channel_id=1, source_target_pairs={{0,24},{4,28},{8,16},{12,20},{16,8},{20,12},{24,0},{28,4},{1,25},{... | collective-permute-start | bytes 405512 | tf_op jit(solution)/shard_map/ppermute | solution.py:11
  28.1 7.1 %collective-permute-start.9 = (f16[528,128]{1,0:T(8,128)(2,1)S(1)}, f16[528,128]{1,0:T(8,128)(2,1)S(1)}, u32[]{:S(2)}, u32[]{:S(2)}) collective-permute-start(f16[528,128]{1,0:T(8,128)(2,1)S(1)} %get-tuple-element.11), channel_id=1, source_target_pairs={{0,16},{4,20},{8,24},{12,28},{16,0},{20,4},{24,8},{28,12},{1,17},{... | collective-permute-start | bytes 405512 | tf_op jit(solution)/shard_map/ppermute | solution.py:11
  30.2 5.1 %collective-permute-start.8 = (f16[528,128]{1,0:T(8,128)(2,1)S(1)}, f16[528,128]{1,0:T(8,128)(2,1)S(1)}, u32[]{:S(2)}, u32[]{:S(2)}) collective-permute-start(f16[528,128]{1,0:T(8,128)(2,1)S(1)} %get-tuple-element.10), channel_id=1, source_target_pairs={{0,8},{4,12},{8,0},{12,4},{16,24},{20,28},{24,16},{28,20},{1,9},{5... | collective-permute-start | bytes 405512 | tf_op jit(solution)/shard_map/ppermute | solution.py:11
  30.3 6.0 %collective-permute-start.13 = (bf16[8,4,16,128]{3,0,1,2:T(8,128)(2,1)S(1)}, bf16[8,4,16,128]{3,0,1,2:T(8,128)(2,1)S(1)}, u32[]{:S(2)}, u32[]{:S(2)}) collective-permute-start(bf16[8,4,16,128]{3,0,1,2:T(8,128)(2,1)S(1)} %copy.86), channel_id=1, source_target_pairs={{0,24},{4,28},{9,17},{13,21},{18,10},{22,14},{27,3},{31,7}} | collective-permute-start | bytes 393224 | tf_op jit(solution)/shard_map/ppermute | solution.py:41
  33.8 3.8 %collective-permute-start.12 = (bf16[8,4,16,128]{3,0,1,2:T(8,128)(2,1)S(1)}, bf16[8,4,16,128]{3,0,1,2:T(8,128)(2,1)S(1)}, u32[]{:S(2)}, u32[]{:S(2)}) collective-permute-start(bf16[8,4,16,128]{3,0,1,2:T(8,128)(2,1)S(1)} %copy.85), channel_id=1, source_target_pairs={{0,16},{4,20},{9,25},{13,29},{18,2},{22,6},{27,11},{31,15}} | collective-permute-start | bytes 393224 | tf_op jit(solution)/shard_map/ppermute | solution.py:41
  35.4 17.8 %copy-start.1 = (f32[4,512]{1,0:T(4,128)S(1)}, f32[4,512]{1,0:T(4,128)}, u32[]{:S(2)}) copy-start(f32[4,512]{1,0:T(4,128)} %param.7) | copy-start | bytes 24580
  38.8 14.4 %all-to-all-start = ((f32[32,4,4,128]{3,1,2,0:T(4,128)}), f32[32,4,4,128]{3,1,2,0:T(4,128)S(1)}, u32[]{:S(2)}, u32[]{:S(2)}) async-start(f32[32,4,4,128]{3,1,2,0:T(4,128)} %copy.87), calls=%async_computation | async-start | bytes 524288 | tf_op jit(solution)/shard_map/all_to_all | solution.py:105

commit v3 on v0

v3 whole, which is shorter than its diff:
```python
import functools

import jax
import jax.numpy as jnp
from jax import lax
from jax.experimental import pallas as pl
from jax.experimental.pallas import tpu as pltpu
from jax.sharding import PartitionSpec as P

CORES = 2
HEADROOM = 14.0


def swap(value, axis, size, step):
    return lax.ppermute(value, axis, [(at, at ^ step) for at in range(size)])


def take(value, index, axis):
    return lax.dynamic_index_in_dim(value, index, axis, keepdims=False)


def tied(*values):
    return lax.optimization_barrier(values)


def forward(piece, bit, col_groups):
    pairs = []
    for z in range(col_groups):
        for at in range(bit):
            for k in range(CORES):
                source, target = z * CORES + k, (z ^ at ^ bit) * CORES + k
                pairs.append((source * col_groups + (z ^ at), target * col_groups + z))
    return lax.ppermute(piece, ("prow", "pcol"), pairs)


def sums_kernel(chips, rows, slices, spot_ref, keep_ref, inv_ref, met_ref, *refs):
    pieces, (out_ref, top_ref, left_ref, right_ref) = refs[: 2 * slices], refs[2 * slices :]
    blocks_i, blocks_j, width, _ = inv_ref.shape
    node_count, height = pieces[0].shape[1:3]
    depth = blocks_j * width
    core, pcol = spot_ref[0], spot_ref[1]
    for side in range(CORES):
        for at in range(slices):
            piece = pieces[side * slices + at]
            start = jnp.bitwise_xor(pcol, at) * height
            for j in range(blocks_j):
                for k in range(node_count):
                    block = jnp.where(keep_ref[side * blocks_j + j, k] > 0, piece[j, k], jnp.zeros_like(piece[j, k]))
                    row = pl.multiple_of(side * depth + j * width + start, height)
                    right_ref[pl.ds(row, height), pl.ds(k * width, width)] = block
    for q in range(chips):
        start = pl.multiple_of((q * CORES + core) * rows, rows)
        for i in range(blocks_i):
            row = pl.ds((q * blocks_i + i) * rows, rows)
            for j in range(blocks_j):
                left_ref[row, pl.ds(j * width, width)] = inv_ref[i, j, pl.ds(start, rows), :]
                left_ref[row, pl.ds(depth + j * width, width)] = met_ref[i, j, q]
    total = jnp.dot(left_ref[...], right_ref[...], preferred_element_type=jnp.float32)
    out_ref[...] = total
    top = jnp.max(jnp.abs(total), axis=0, keepdims=True)
    top_ref[...] = jnp.broadcast_to(top, top_ref.shape)


def chip_sums(spot, keep, inv, met, own_pieces, met_pieces, chips, rows):
    blocks_i, blocks_j, width, _ = inv.shape
    node_count = own_pieces[0].shape[1]
    slices = len(own_pieces)
    height = chips * blocks_i * rows
    across = node_count * width
    in_vmem = pl.BlockSpec(memory_space=pltpu.VMEM)
    in_smem = pl.BlockSpec(memory_space=pltpu.SMEM)
    depth = CORES * blocks_j * width
    return pl.pallas_call(
        functools.partial(sums_kernel, chips, rows, slices),
        out_shape=(
            jax.ShapeDtypeStruct((height, across), jnp.float32),
            jax.ShapeDtypeStruct((16, across), jnp.float32),
        ),
        in_specs=[in_smem, in_smem] + [in_vmem] * (2 + 2 * slices),
        out_specs=(in_vmem, in_vmem),
        scratch_shapes=[
            pltpu.VMEM((height, depth), jnp.bfloat16),
            pltpu.VMEM((depth, across), jnp.bfloat16),
        ],
        compiler_params=pltpu.CompilerParams(vmem_limit_bytes=24 << 20),
        cost_estimate=pl.CostEstimate(
            flops=2 * height * depth * across, bytes_accessed=4 << 20, transcendentals=0
        ),
    )(spot, keep, inv, met, *own_pieces, *met_pieces)


def plain_sums(pcol, keep, inv, met, own_pieces, met_pieces, core, chips, rows):
    blocks_i, blocks_j, width, _ = inv.shape
    node_count = own_pieces[0].shape[1]
    slices = len(own_pieces)
    mine = take(inv.reshape(blocks_i, blocks_j, chips, CORES, rows, width), core, 3)
    total = 0.0
    for side, (blocks, pieces) in enumerate(((mine, own_pieces), (met, met_pieces))):
        whole = jnp.zeros((slices,) + pieces[0].shape, pieces[0].dtype)
        for at, piece in enumerate(pieces):
            whole = lax.dynamic_update_index_in_dim(whole, piece, pcol ^ at, 0)
        shown = keep[side * blocks_j : (side + 1) * blocks_j].astype(whole.dtype)
        whole = whole * shown[:, :, None, None]
        blocks = blocks.reshape(blocks_i, blocks_j, chips, rows, slices, width // slices)
        total = total + jnp.einsum("ijqrcb,cjkbe->qirke", blocks, whole, preferred_element_type=jnp.float32)
    total = total.reshape(chips * blocks_i * rows, node_count * width)
    top = jnp.max(jnp.abs(total), axis=0, keepdims=True)
    return total, jnp.broadcast_to(top, (16, node_count * width))


def per_device(inverse_blocks, lower_blocks, pattern, diag_inverse):
    blocks_i, blocks_j, width, _ = inverse_blocks.shape
    node_count = lower_blocks.shape[1]
    row_groups = lax.axis_size("prow")
    col_groups = lax.axis_size("pcol")
    chips = row_groups // CORES
    block_count = blocks_j * row_groups
    prow, pcol = lax.axis_index("prow"), lax.axis_index("pcol")
    chip, core = prow // CORES, prow % CORES
    rows = width // row_groups
    across = node_count * width

    def core_swap(value):
        return swap(value, "prow", row_groups, 1)

    matches = pattern[None, :, :] == jnp.arange(block_count, dtype=jnp.int32)[:, None, None]
    present = jnp.sum(matches.astype(jnp.float32), axis=2)
    keep_i = lax.dynamic_slice_in_dim(present, pcol * blocks_i, blocks_i, 0)
    keep_own = lax.dynamic_slice_in_dim(present, prow * blocks_j, blocks_j, 0)
    keep_met = lax.dynamic_slice_in_dim(present, (prow ^ 1) * blocks_j, blocks_j, 0)
    keep = jnp.concatenate([keep_own, keep_met], axis=0)

    held = {0: lower_blocks}
    step = col_groups // 2
    while step:
        held.update({at ^ step: swap(held[at], "pcol", col_groups, step) for at in sorted(held)})
        step //= 2
    met_inv = core_swap(
        take(inverse_blocks.reshape(blocks_i, blocks_j, chips, CORES, rows, width), 1 - core, 3)
    )
    met = {at: core_swap(held[at]) for at in sorted(held)}

    def own_rows(at):
        cut = (blocks_j, node_count, CORES, rows, width)
        mine, other = take(held[at].reshape(cut), core, 2), take(met[at].reshape(cut), core, 2)
        both = jnp.stack([jnp.where(core == 0, mine, other), jnp.where(core == 0, other, mine)])
        return both.reshape(blocks_i, node_count, rows, width)

    bits = [1 << n for n in range(col_groups.bit_length() - 1)]
    own = own_rows(0) * (chip == pcol).astype(lower_blocks.dtype)
    first = forward(own_rows(1), 1, col_groups)
    held[col_groups - 1], first = tied(held[col_groups - 1], first)
    order = range(col_groups)
    own_pieces, met_pieces = [held[at] for at in order], [met[at] for at in order]
    if rows % 16 == 0 and (width // col_groups) % 16 == 0:
        spot = jnp.stack([core, pcol]).astype(jnp.int32)
        total, top = chip_sums(spot, keep, inverse_blocks, met_inv, own_pieces, met_pieces, chips, rows)
    else:
        total, top = plain_sums(pcol, keep, inverse_blocks, met_inv, own_pieces, met_pieces, core, chips, rows)
    power = jnp.maximum(jnp.ceil(jnp.log2(top)), -110.0)
    total = total.reshape(chips, blocks_i * rows, across)
    scaled = (total * jnp.exp2(HEADROOM - power[0])).astype(jnp.float16)
    mark = jnp.broadcast_to(power.astype(jnp.float16), (chips, 16, across))
    packed = jnp.concatenate([scaled, mark], axis=1)
    pieces = {step: take(packed, chip ^ step, 0) for step in range(1, chips)}
    own = own + first
    passed = []
    for bit in bits[1:]:
        payload, _ = tied(own_rows(bit), pieces[1])
        passed.append(forward(payload, bit, col_groups))
    summed = take(total, chip, 0)
    for step in range(1, chips):
        came = swap(pieces[step], "prow", row_groups, step * CORES)
        came = lax.optimization_barrier(came.astype(jnp.float32))
        summed = summed + came[:-16] * jnp.exp2(came[-1] - HEADROOM)
    for part in passed:
        own = own + part
    own = own * keep_i.astype(jnp.bfloat16)[:, :, None, None]
    column = summed.reshape(blocks_i, rows, node_count, width) * (-keep_i)[:, None, :, None]

    count = row_groups * col_groups
    wide = own.astype(jnp.float32)
    if width % count == 0:
        update = jnp.einsum("ikra,irkb->akb", wide, column, precision=lax.Precision.HIGHEST)
        update = update.reshape(count, width // count, node_count, width)
        update = jnp.sum(lax.all_to_all(update, ("prow", "pcol"), 0, 0, tiled=True), axis=0)
        update = jnp.transpose(update, (1, 0, 2)).reshape(diag_inverse.shape)
    else:
        update = jnp.einsum("ikra,irkb->kab", wide, column, precision=lax.Precision.HIGHEST)
        update = update.reshape(node_count, count, width * width // count)
        update = jnp.sum(lax.all_to_all(update, ("prow", "pcol"), 1, 1, tiled=True), axis=1)
    return jnp.transpose(column, (0, 2, 1, 3)), diag_inverse - update


def solution(mesh):
    placed = (
        P("pcol", "prow", None, None),
        P("prow", None, "pcol", None),
        P(),
        P(None, ("prow", "pcol")),
    )
    return jax.shard_map(
        per_device,
        mesh=mesh,
        in_specs=placed,
        out_specs=(P("pcol", None, "prow", None), P(None, ("prow", "pcol"))),
        check_vma=False,
    )
```

time: 214 us -> 51.7 us (0.24)
  waiting for transfers between devices: 165 us -> 23.2 us
  blocking collectives: 17.4 us -> 0 us
  starting transfers between devices: 3.8 us -> 20.3 us
  between operations: 14.1 us -> 0.88 us
  local copies, waits for them, and re-layouts: 6.9 us -> 2.63 us
  other arithmetic: 4.79 us -> 2.43 us
    psum x1 -> x0, waiting for transfers between devices: 128 us -> none  [per_device(): totals = lax.psum(partial_value, ('prow', 'pcol'))]
    reduce_scatter x1 -> x0, waiting for transfers between devices: 27.4 us -> none  [per_device(): lax.psum_scatter(jnp.einsum('ijrb,jkbe->rike', inverse_blocks, masked, pr...]
    all_gather x1 -> x0, blocking collectives: 17.4 us -> none  [per_device(): whole = lax.all_gather(lower_blocks, 'pcol', axis=2, tiled=True)]
    ppermute x0 -> x13, starting transfers between devices: none -> 16.1 us  [the longest x11 10.2 us: swap(): return lax.ppermute(value, axis, [(at, at ^ step) for at in range(size)])]
    ppermute x0 -> x13, waiting for transfers between devices: none -> 13.8 us  [the longest x11 11.3 us: swap(): return lax.ppermute(value, axis, [(at, at ^ step) for at in range(size)])]
    unnamed x13 -> x10, local copies, waits for them, and re-layouts: 4.53 us -> 0.3 us
    mul x3 -> x2, other arithmetic: 2.48 us -> 0.12 us  [the longest x1 0.1 us: per_device(): own = own * keep_i.astype(jnp.bfloat16)[:, :, None, None]]
  transfers between devices with their start and end apart: 3 -> 14, of which waited for: 3 -> 9; matrix products, arithmetic and copies ran while one was open for 1% -> 6% of each run, Pallas kernels for 0% -> 0%
where the time goes in v3:
time: 51.7 us; the launch traced here: 51.4 us
  waiting for transfers between devices  23.2 us (45%)
  starting transfers between devices  20.3 us (39%)
  local copies, waits for them, and re-layouts  2.63 us (5%)
  other arithmetic  2.43 us (5%)
  Pallas kernels  1.6 us (3%)
  between operations  0.88 us (2%)
    ppermute x11, waiting for transfers between devices, swap(): return lax.ppermute(value, axis, [(at, at ^ step) for at in range(size)])  11.3 us
    ppermute x11, starting transfers between devices, swap(): return lax.ppermute(value, axis, [(at, at ^ step) for at in range(size)])  10.2 us
    all_to_all x1, waiting for transfers between devices, per_device(): lax.all_to_all(update, ('prow', 'pcol'), 0, 0, tiled=True)  9.39 us
    ppermute x2, starting transfers between devices, forward(): return lax.ppermute(piece, ('prow', 'pcol'), pairs)  5.84 us
    all_to_all x1, starting transfers between devices, per_device(): lax.all_to_all(update, ('prow', 'pcol'), 0, 0, tiled=True)  4.26 us
    ppermute x2, waiting for transfers between devices, forward(): return lax.ppermute(piece, ('prow', 'pcol'), pairs)  2.47 us
    pallas_call x1, Pallas kernels, chip_sums(): pl.pallas_call(functools.partial(sums_kernel, chips, rows, slices), out_s...  1.6 us
    squeeze x1, local copies, waits for them, and re-layouts, take(): return lax.dynamic_index_in_dim(value, index, axis, keepdims=False)  1.17 us
  transfers between devices with their start and end apart: 14, of which 9 were waited for; matrix products, arithmetic and copies ran while one was open for 6% of the time, Pallas kernels for 0%

profile of v3, /device:TPU:0, one launch (start us, length us, event | category | flops | bytes accessed | tf_op | source)
XLA Modules:
  0.0 51.4 jit_solution(14286882850790946016)
XLA Ops:
  0.6 3.1 %collective-permute-start.1 = (bf16[4,4,32,128]{3,2,1,0:T(8,128)(2,1)}, bf16[4,4,32,128]{3,2,1,0:T(8,128)(2,1)S(1)}, u32[]{:S(2)}, u32[]{:S(2)}) collective-permute-start(bf16[4,4,32,128]{3,2,1,0:T(8,128)(2,1)} %refs_0_.1), channel_id=1, source_target_pairs={{0,1},{1,0},{2,3},{3,2},{4,5},{5,4},{6,7},{7,6},{8,9},{9,8},{10,11... | collective-permute-start | bytes 393224 | tf_op jit(solution)/shard_map/ppermute | solution.py:15
  3.7 2.6 %collective-permute-start.2 = (bf16[4,4,32,128]{3,2,1,0:T(8,128)(2,1)}, bf16[4,4,32,128]{3,2,1,0:T(8,128)(2,1)S(1)}, u32[]{:S(2)}, u32[]{:S(2)}) collective-permute-start(bf16[4,4,32,128]{3,2,1,0:T(8,128)(2,1)} %refs_0_.1), channel_id=1, source_target_pairs={{0,2},{1,3},{2,0},{3,1},{4,6},{5,7},{6,4},{7,5},{8,10},{9,11},{10,... | collective-permute-start | bytes 393224 | tf_op jit(solution)/shard_map/ppermute | solution.py:15
  6.3 0.0 collective-permute-start.6
  6.3 1.2 %dynamic-slice_bitcast_fusion = bf16[8,4,4,16,128]{4,3,2,1,0:T(8,128)(2,1)S(1)} fusion(bf16[8,4,4,2,16,128]{5,4,3,2,1,0:T(8,128)(2,1)} %bitcast.90, s32[]{:T(128)S(6)} %select_n.138), kind=kLoop, calls=%fused_computation.4 | loop fusion | bytes 1048580 | tf_op jit(solution)/shard_map/jit(dynamic_index_in_dim)/squeeze | solution.py:19
  7.5 0.0 copy-start.3
  7.5 0.6 %collective-permute-start = (bf16[8,4,4,16,128]{4,3,2,1,0:T(8,128)(2,1)S(1)}, bf16[8,4,4,16,128]{4,3,2,1,0:T(8,128)(2,1)S(1)}, u32[]{:S(2)}, u32[]{:S(2)}) collective-permute-start(bf16[8,4,4,16,128]{4,3,2,1,0:T(8,128)(2,1)S(1)} %dynamic-slice_bitcast_fusion), channel_id=1, source_target_pairs={{0,4},{4,0},{8,12},{12,8},{16,20},{20,16},{24,28},{28,24},{1,5},{5... | collective-permute-start | bytes 1572872 | tf_op jit(solution)/shard_map/ppermute | solution.py:15
  8.1 0.1 copy-done.3
  8.2 0.1 convert_reduce_fusion
  8.3 0.1 fusion.29
  8.3 0.1 fusion.28
  8.4 0.1 constant_dynamic-slice_fusion.2
  8.5 0.7 %collective-permute-done.1.refs_1_ = bf16[4,4,32,128]{3,2,1,0:T(8,128)(2,1)S(1)} collective-permute-done((bf16[4,4,32,128]{3,2,1,0:T(8,128)(2,1)}, bf16[4,4,32,128]{3,2,1,0:T(8,128)(2,1)S(1)}, u32[]{:S(2)}, u32[]{:S(2)}) %collective-permute-start.1) | collective-permute-done | bytes 131104 | tf_op jit(solution)/shard_map/ppermute | solution.py:15
  9.2 0.0 collective-permute-start.4
  9.2 0.1 pad_add_fusion.spot_ref
  9.3 0.1 copy.52
  9.4 0.1 copy.53
  9.5 0.1 copy.50
  9.6 0.1 copy.42
  9.7 3.0 %collective-permute-done.2.refs_2_ = bf16[4,4,32,128]{3,2,1,0:T(8,128)(2,1)S(1)} collective-permute-done((bf16[4,4,32,128]{3,2,1,0:T(8,128)(2,1)}, bf16[4,4,32,128]{3,2,1,0:T(8,128)(2,1)S(1)}, u32[]{:S(2)}, u32[]{:S(2)}) %collective-permute-start.2) | collective-permute-done | bytes 131104 | tf_op jit(solution)/shard_map/ppermute | solution.py:15
  12.7 0.4 collective-permute-start.3
  13.1 0.0 collective-permute-start.7
  13.1 0.0 collective-permute-done.4.refs_5_
  13.1 3.4 %collective-permute-start.5 = (bf16[8,4,16,128]{3,2,1,0:T(8,128)(2,1)S(1)}, bf16[8,4,16,128]{3,2,1,0:T(8,128)(2,1)S(1)}, u32[]{:S(2)}, u32[]{:S(2)}) collective-permute-start(bf16[8,4,16,128]{3,2,1,0:T(8,128)(2,1)S(1)} %bitcast.103), channel_id=1, source_target_pairs={{0,8},{4,12},{9,1},{13,5},{18,26},{22,30},{27,19},{31,23}} | collective-permute-start | bytes 393224 | tf_op jit(solution)/shard_map/ppermute | solution.py:33
  16.5 1.1 %collective-permute-done.3.refs_3_ = bf16[4,4,32,128]{3,2,1,0:T(8,128)(2,1)S(1)} collective-permute-done((bf16[4,4,32,128]{3,2,1,0:T(8,128)(2,1)S(1)}, bf16[4,4,32,128]{3,2,1,0:T(8,128)(2,1)S(1)}, u32[]{:S(2)}, u32[]{:S(2)}) %collective-permute-start.3) | collective-permute-done | bytes 131104 | tf_op jit(solution)/shard_map/ppermute | solution.py:15
  17.7 0.0 copy-start.1
  17.7 2.2 %collective-permute-done.5 = bf16[8,4,16,128]{3,2,1,0:T(8,128)(2,1)S(1)} collective-permute-done((bf16[8,4,16,128]{3,2,1,0:T(8,128)(2,1)S(1)}, bf16[8,4,16,128]{3,2,1,0:T(8,128)(2,1)S(1)}, u32[]{:S(2)}, u32[]{:S(2)}) %collective-permute-start.5) | collective-permute-done | bytes 131104 | tf_op jit(solution)/shard_map/ppermute | solution.py:33
  20.0 0.0 collective-permute-done.6.refs_4_
  20.0 0.0 collective-permute-done.8.refs_7_
  20.0 1.6 %shard_map.59 = (f32[512,512]{1,0:T(8,128)S(1)}, f32[16,512]{1,0:T(8,128)S(1)}) custom-call(s32[2]{0:T(128)S(1)} %pad_add_fusion.spot_ref, f32[8,4]{1,0:T(8,128)S(1)} %pad_maximum_fusion.2.keep_ref, bf16[8,4,128,128]{3,2,1,0:T(8,128)(2,1)S(1)} %copy-done, bf16[8,4,4,16,128]{4,3,2,1,0:T(8,128)(2,1)S(1)} %collective-permute-done.met_ref, ...), custom_call_target="tpu_custom_call" | custom-call | flops 536870912 | bytes 4194304 | tf_op jit(solution)/shard_map/pallas_call | solution.py:73
  21.6 0.1 multiply_convert_fusion
  21.8 0.1 fusion.9
  21.9 2.4 %collective-permute-start.12 = (bf16[8,4,16,128]{3,2,1,0:T(8,128)(2,1)S(1)}, bf16[8,4,16,128]{3,2,1,0:T(8,128)(2,1)S(1)}, u32[]{:S(2)}, u32[]{:S(2)}) collective-permute-start(bf16[8,4,16,128]{3,2,1,0:T(8,128)(2,1)S(1)} %bitcast.102), channel_id=1, source_target_pairs={{0,16},{4,20},{1,24},{5,28},{9,25},{13,29},{8,17},{12,21},{18,2},{... | collective-permute-start | bytes 393224 | tf_op jit(solution)/shard_map/ppermute | solution.py:33
  24.4 1.4 %collective-permute-start.9 = (f16[144,512]{1,0:T(8,128)(2,1)S(1)}, f16[144,512]{1,0:T(8,128)(2,1)S(1)}, u32[]{:S(2)}, u32[]{:S(2)}) collective-permute-start(f16[144,512]{1,0:T(8,128)(2,1)S(1)} %get-tuple-element.12), channel_id=1, source_target_pairs={{0,8},{4,12},{8,0},{12,4},{16,24},{20,28},{24,16},{28,20},{1,9},{5... | collective-permute-start | bytes 442376 | tf_op jit(solution)/shard_map/ppermute | solution.py:15
  25.8 2.1 %collective-permute-start.11 = (f16[144,512]{1,0:T(8,128)(2,1)S(1)}, f16[144,512]{1,0:T(8,128)(2,1)S(1)}, u32[]{:S(2)}, u32[]{:S(2)}) collective-permute-start(f16[144,512]{1,0:T(8,128)(2,1)S(1)} %get-tuple-element.14), channel_id=1, source_target_pairs={{0,24},{4,28},{8,16},{12,20},{16,8},{20,12},{24,0},{28,4},{1,25},{... | collective-permute-start | bytes 442376 | tf_op jit(solution)/shard_map/ppermute | solution.py:15
  28.0 0.2 collective-permute-done.12
  28.2 0.1 fusion.12
  28.3 4.2 %collective-permute-done.9 = f16[144,512]{1,0:T(8,128)(2,1)S(1)} collective-permute-done((f16[144,512]{1,0:T(8,128)(2,1)S(1)}, f16[144,512]{1,0:T(8,128)(2,1)S(1)}, u32[]{:S(2)}, u32[]{:S(2)}) %collective-permute-start.9) | collective-permute-done | bytes 147488 | tf_op jit(solution)/shard_map/ppermute | solution.py:15
  32.5 1.8 %collective-permute-done.10 = f16[144,512]{1,0:T(8,128)(2,1)S(1)} collective-permute-done((f16[144,512]{1,0:T(8,128)(2,1)S(1)}, f16[144,512]{1,0:T(8,128)(2,1)S(1)}, u32[]{:S(2)}, u32[]{:S(2)}) %collective-permute-start.10) | collective-permute-done | bytes 147488 | tf_op jit(solution)/shard_map/ppermute | solution.py:15
  34.4 0.6 %collective-permute-done.11 = f16[144,512]{1,0:T(8,128)(2,1)S(1)} collective-permute-done((f16[144,512]{1,0:T(8,128)(2,1)S(1)}, f16[144,512]{1,0:T(8,128)(2,1)S(1)}, u32[]{:S(2)}, u32[]{:S(2)}) %collective-permute-start.11) | collective-permute-done | bytes 147488 | tf_op jit(solution)/shard_map/ppermute | solution.py:15
  35.0 0.1 fusion
  35.1 0.1 reshape.180
  35.2 0.4 fusion.3
  35.5 0.7 %copy.51 = f32[32,4,4,128]{3,1,2,0:T(4,128)} copy(f32[32,4,4,128]{3,1,0,2:T(4,128)S(1)} %bitcast.101) | data formatting | bytes 524288 | tf_op jit(solution)/shard_map/reshape | solution.py:185
  36.3 4.3 %all-to-all-start = ((f32[32,4,4,128]{3,1,2,0:T(4,128)}), f32[32,4,4,128]{3,1,2,0:T(4,128)S(1)}, u32[]{:S(2)}, u32[]{:S(2)}) async-start(f32[32,4,4,128]{3,1,2,0:T(4,128)} %copy.51), calls=%async_computation | async-start | bytes 524288 | tf_op jit(solution)/shard_map/all_to_all | solution.py:186
  40.6 0.8 %fusion.4 = f32[8,4,16,128]{3,2,1,0:T(8,128)} fusion(f32[8,16,4,128]{3,2,1,0:T(4,128)S(1)} %reshape.180, f32[8,4]{1,0:T(8,128)S(1)} %copy.42), kind=kLoop, calls=%fused_computation.16 | loop fusion | flops 65536 | bytes 524416 | tf_op jit(solution)/shard_map/transpose | solution.py:192
  41.4 9.4 %all-to-all-done = f32[32,4,4,128]{3,1,2,0:T(4,128)S(1)} async-done(((f32[32,4,4,128]{3,1,2,0:T(4,128)}), f32[32,4,4,128]{3,1,2,0:T(4,128)S(1)}, u32[]{:S(2)}, u32[]{:S(2)}) %all-to-all-start) | async-done | bytes 262176 | tf_op jit(solution)/shard_map/all_to_all | solution.py:186
  50.8 0.1 reduce_sum.19
  50.8 0.6 %bitcast_subtract_fusion = f32[4,512]{1,0:T(4,128)} fusion(f32[4,512]{1,0:T(4,128)S(1)} %copy-done.2, f32[1,4,4,128]{3,2,1,0:T(4,128)S(1)} %bitcast.104), kind=kLoop, calls=%fused_computation.45 | loop fusion | flops 2048 | bytes 24576 | tf_op jit(solution)/shard_map/sub | solution.py:192
  (26 shorter events, 0.3 us)
Async XLA Ops:
  0.6 8.6 %collective-permute-start.1 = (bf16[4,4,32,128]{3,2,1,0:T(8,128)(2,1)}, bf16[4,4,32,128]{3,2,1,0:T(8,128)(2,1)S(1)}, u32[]{:S(2)}, u32[]{:S(2)}) collective-permute-start(bf16[4,4,32,128]{3,2,1,0:T(8,128)(2,1)} %refs_0_.1), channel_id=1, source_target_pairs={{0,1},{1,0},{2,3},{3,2},{4,5},{5,4},{6,7},{7,6},{8,9},{9,8},{10,11... | collective-permute-start | bytes 393224 | tf_op jit(solution)/shard_map/ppermute | solution.py:15
  3.7 8.9 %collective-permute-start.2 = (bf16[4,4,32,128]{3,2,1,0:T(8,128)(2,1)}, bf16[4,4,32,128]{3,2,1,0:T(8,128)(2,1)S(1)}, u32[]{:S(2)}, u32[]{:S(2)}) collective-permute-start(bf16[4,4,32,128]{3,2,1,0:T(8,128)(2,1)} %refs_0_.1), channel_id=1, source_target_pairs={{0,2},{1,3},{2,0},{3,1},{4,6},{5,7},{6,4},{7,5},{8,10},{9,11},{10,... | collective-permute-start | bytes 393224 | tf_op jit(solution)/shard_map/ppermute | solution.py:15
  6.3 13.6 %collective-permute-start.6 = (bf16[4,4,32,128]{3,2,1,0:T(8,128)(2,1)}, bf16[4,4,32,128]{3,2,1,0:T(8,128)(2,1)S(1)}, u32[]{:S(2)}, u32[]{:S(2)}) collective-permute-start(bf16[4,4,32,128]{3,2,1,0:T(8,128)(2,1)} %refs_0_.1), channel_id=1, source_target_pairs={{0,4},{4,0},{8,12},{12,8},{16,20},{20,16},{24,28},{28,24},{1,5},{5... | collective-permute-start | bytes 393224 | tf_op jit(solution)/shard_map/ppermute | solution.py:15
  6.3 13.7 %copy-start = (bf16[8,4,128,128]{3,2,1,0:T(8,128)(2,1)S(1)}, bf16[8,4,128,128]{3,2,1,0:T(8,128)(2,1)}, u32[]{:S(2)}) copy-start(bf16[8,4,128,128]{3,2,1,0:T(8,128)(2,1)} %inv_ref.1) | copy-start | bytes 3145732
  7.5 0.7 %copy-start.3 = (s32[4,16]{1,0:T(4,128)S(1)}, s32[4,16]{1,0:T(4,128)}, u32[]{:S(2)}) copy-start(s32[4,16]{1,0:T(4,128)} %param.6) | copy-start | bytes 772
  7.5 12.5 %collective-permute-start = (bf16[8,4,4,16,128]{4,3,2,1,0:T(8,128)(2,1)S(1)}, bf16[8,4,4,16,128]{4,3,2,1,0:T(8,128)(2,1)S(1)}, u32[]{:S(2)}, u32[]{:S(2)}) collective-permute-start(bf16[8,4,4,16,128]{4,3,2,1,0:T(8,128)(2,1)S(1)} %dynamic-slice_bitcast_fusion), channel_id=1, source_target_pairs={{0,4},{4,0},{8,12},{12,8},{16,20},{20,16},{24,28},{28,24},{1,5},{5... | collective-permute-start | bytes 1572872 | tf_op jit(solution)/shard_map/ppermute | solution.py:15
  9.2 3.9 %collective-permute-start.4 = (bf16[4,4,32,128]{3,2,1,0:T(8,128)(2,1)S(1)}, bf16[4,4,32,128]{3,2,1,0:T(8,128)(2,1)S(1)}, u32[]{:S(2)}, u32[]{:S(2)}) collective-permute-start(bf16[4,4,32,128]{3,2,1,0:T(8,128)(2,1)S(1)} %collective-permute-done.1.refs_1_), channel_id=1, source_target_pairs={{0,4},{4,0},{8,12},{12,8},{16,20},{20,16},{24,28},{28,24},{1,5},{5... | collective-permute-start | bytes 393224 | tf_op jit(solution)/shard_map/ppermute | solution.py:15
  12.7 5.0 %collective-permute-start.3 = (bf16[4,4,32,128]{3,2,1,0:T(8,128)(2,1)S(1)}, bf16[4,4,32,128]{3,2,1,0:T(8,128)(2,1)S(1)}, u32[]{:S(2)}, u32[]{:S(2)}) collective-permute-start(bf16[4,4,32,128]{3,2,1,0:T(8,128)(2,1)S(1)} %collective-permute-done.2.refs_2_), channel_id=1, source_target_pairs={{0,1},{1,0},{2,3},{3,2},{4,5},{5,4},{6,7},{7,6},{8,9},{9,8},{10,11... | collective-permute-start | bytes 393224 | tf_op jit(solution)/shard_map/ppermute | solution.py:15
  13.1 4.5 %collective-permute-start.7 = (bf16[4,4,32,128]{3,2,1,0:T(8,128)(2,1)S(1)}, bf16[4,4,32,128]{3,2,1,0:T(8,128)(2,1)S(1)}, u32[]{:S(2)}, u32[]{:S(2)}) collective-permute-start(bf16[4,4,32,128]{3,2,1,0:T(8,128)(2,1)S(1)} %collective-permute-done.2.refs_2_), channel_id=1, source_target_pairs={{0,4},{4,0},{8,12},{12,8},{16,20},{20,16},{24,28},{28,24},{1,5},{5... | collective-permute-start | bytes 393224 | tf_op jit(solution)/shard_map/ppermute | solution.py:15
  13.1 6.8 %collective-permute-start.5 = (bf16[8,4,16,128]{3,2,1,0:T(8,128)(2,1)S(1)}, bf16[8,4,16,128]{3,2,1,0:T(8,128)(2,1)S(1)}, u32[]{:S(2)}, u32[]{:S(2)}) collective-permute-start(bf16[8,4,16,128]{3,2,1,0:T(8,128)(2,1)S(1)} %bitcast.103), channel_id=1, source_target_pairs={{0,8},{4,12},{9,1},{13,5},{18,26},{22,30},{27,19},{31,23}} | collective-permute-start | bytes 393224 | tf_op jit(solution)/shard_map/ppermute | solution.py:33
  17.6 2.3 %collective-permute-start.8 = (bf16[4,4,32,128]{3,2,1,0:T(8,128)(2,1)S(1)}, bf16[4,4,32,128]{3,2,1,0:T(8,128)(2,1)S(1)}, u32[]{:S(2)}, u32[]{:S(2)}) collective-permute-start(bf16[4,4,32,128]{3,2,1,0:T(8,128)(2,1)S(1)} %collective-permute-done.3.refs_3_), channel_id=1, source_target_pairs={{0,4},{4,0},{8,12},{12,8},{16,20},{20,16},{24,28},{28,24},{1,5},{5... | collective-permute-start | bytes 393224 | tf_op jit(solution)/shard_map/ppermute | solution.py:15
  17.7 2.3 %copy-start.1 = (bf16[4,4,32,128]{3,2,1,0:T(8,128)(2,1)S(1)}, bf16[4,4,32,128]{3,2,1,0:T(8,128)(2,1)}, u32[]{:S(2)}) copy-start(bf16[4,4,32,128]{3,2,1,0:T(8,128)(2,1)} %refs_0_.1) | copy-start | bytes 393220
  21.9 6.3 %collective-permute-start.12 = (bf16[8,4,16,128]{3,2,1,0:T(8,128)(2,1)S(1)}, bf16[8,4,16,128]{3,2,1,0:T(8,128)(2,1)S(1)}, u32[]{:S(2)}, u32[]{:S(2)}) collective-permute-start(bf16[8,4,16,128]{3,2,1,0:T(8,128)(2,1)S(1)} %bitcast.102), channel_id=1, source_target_pairs={{0,16},{4,20},{1,24},{5,28},{9,25},{13,29},{8,17},{12,21},{18,2},{... | collective-permute-start | bytes 393224 | tf_op jit(solution)/shard_map/ppermute | solution.py:33
  24.4 8.1 %collective-permute-start.9 = (f16[144,512]{1,0:T(8,128)(2,1)S(1)}, f16[144,512]{1,0:T(8,128)(2,1)S(1)}, u32[]{:S(2)}, u32[]{:S(2)}) collective-permute-start(f16[144,512]{1,0:T(8,128)(2,1)S(1)} %get-tuple-element.12), channel_id=1, source_target_pairs={{0,8},{4,12},{8,0},{12,4},{16,24},{20,28},{24,16},{28,20},{1,9},{5... | collective-permute-start | bytes 442376 | tf_op jit(solution)/shard_map/ppermute | solution.py:15
  25.8 8.5 %collective-permute-start.10 = (f16[144,512]{1,0:T(8,128)(2,1)S(1)}, f16[144,512]{1,0:T(8,128)(2,1)S(1)}, u32[]{:S(2)}, u32[]{:S(2)}) collective-permute-start(f16[144,512]{1,0:T(8,128)(2,1)S(1)} %get-tuple-element.13), channel_id=1, source_target_pairs={{0,16},{4,20},{8,24},{12,28},{16,0},{20,4},{24,8},{28,12},{1,17},{... | collective-permute-start | bytes 442376 | tf_op jit(solution)/shard_map/ppermute | solution.py:15
  25.8 9.1 %collective-permute-start.11 = (f16[144,512]{1,0:T(8,128)(2,1)S(1)}, f16[144,512]{1,0:T(8,128)(2,1)S(1)}, u32[]{:S(2)}, u32[]{:S(2)}) collective-permute-start(f16[144,512]{1,0:T(8,128)(2,1)S(1)} %get-tuple-element.14), channel_id=1, source_target_pairs={{0,24},{4,28},{8,16},{12,20},{16,8},{20,12},{24,0},{28,4},{1,25},{... | collective-permute-start | bytes 442376 | tf_op jit(solution)/shard_map/ppermute | solution.py:15
  36.3 14.5 %all-to-all-start = ((f32[32,4,4,128]{3,1,2,0:T(4,128)}), f32[32,4,4,128]{3,1,2,0:T(4,128)S(1)}, u32[]{:S(2)}, u32[]{:S(2)}) async-start(f32[32,4,4,128]{3,1,2,0:T(4,128)} %copy.51), calls=%async_computation | async-start | bytes 524288 | tf_op jit(solution)/shard_map/all_to_all | solution.py:186
  41.4 9.5 %copy-start.2 = (f32[4,512]{1,0:T(4,128)S(1)}, f32[4,512]{1,0:T(4,128)}, u32[]{:S(2)}) copy-start(f32[4,512]{1,0:T(4,128)} %param.7) | copy-start | bytes 24580

commit v4 on v3

--- a/solution.py
+++ b/solution.py
@@ -23,70 +23,80 @@
     return lax.optimization_barrier(values)
 
 
-def forward(piece, bit, col_groups):
-    pairs = []
-    for z in range(col_groups):
-        for at in range(bit):
-            for k in range(CORES):
-                source, target = z * CORES + k, (z ^ at ^ bit) * CORES + k
-                pairs.append((source * col_groups + (z ^ at), target * col_groups + z))
-    return lax.ppermute(piece, ("prow", "pcol"), pairs)
-
-
-def sums_kernel(chips, rows, slices, spot_ref, keep_ref, inv_ref, met_ref, *refs):
-    pieces, (out_ref, top_ref, left_ref, right_ref) = refs[: 2 * slices], refs[2 * slices :]
+def place(right_ref, spot_ref, keep_ref, piece, side, at, blocks_j, width):
+    node_count, height = piece.shape[1:3]
+    start = jnp.bitwise_xor(spot_ref[1], at) * height
+    for j in range(blocks_j):
+        for k in range(node_count):
+            block = piece[j, k]
+            block = jnp.where(keep_ref[side * blocks_j + j, k] > 0, block, jnp.zeros_like(block))
+            row = pl.multiple_of((side * blocks_j + j) * width + start, height)
+            right_ref[pl.ds(row, height), pl.ds(k * width, width)] = block
+
+
+def layout_kernel(chips, rows, spot_ref, keep_ref, inv_ref, met_ref, *refs):
+    pieces, (left_ref, right_ref) = refs[:-2], refs[-2:]
     blocks_i, blocks_j, width, _ = inv_ref.shape
-    node_count, height = pieces[0].shape[1:3]
-    depth = blocks_j * width
-    core, pcol = spot_ref[0], spot_ref[1]
+    half = len(pieces) // CORES
     for side in range(CORES):
-        for at in range(slices):
-            piece = pieces[side * slices + at]
-            start = jnp.bitwise_xor(pcol, at) * height
-            for j in range(blocks_j):
-                for k in range(node_count):
-                    block = jnp.where(keep_ref[side * blocks_j + j, k] > 0, piece[j, k], jnp.zeros_like(piece[j, k]))
-                    row = pl.multiple_of(side * depth + j * width + start, height)
-                    right_ref[pl.ds(row, height), pl.ds(k * width, width)] = block
+        for at in range(half):
+            place(right_ref, spot_ref, keep_ref, pieces[side * half + at], side, at, blocks_j, width)
     for q in range(chips):
-        start = pl.multiple_of((q * CORES + core) * rows, rows)
+        start = pl.multiple_of((q * CORES + spot_ref[0]) * rows, rows)
         for i in range(blocks_i):
             row = pl.ds((q * blocks_i + i) * rows, rows)
             for j in range(blocks_j):
                 left_ref[row, pl.ds(j * width, width)] = inv_ref[i, j, pl.ds(start, rows), :]
-                left_ref[row, pl.ds(depth + j * width, width)] = met_ref[i, j, q]
+                left_ref[row, pl.ds((blocks_j + j) * width, width)] = met_ref[i, j, q]
+
+
+def sums_kernel(last, spot_ref, keep_ref, left_ref, given_ref, own_ref, met_ref, out_ref, top_ref, right_ref):
+    blocks_j = own_ref.shape[0]
+    width = own_ref.shape[3]
+    right_ref[...] = given_ref[...]
+    place(right_ref, spot_ref, keep_ref, own_ref, 0, last, blocks_j, width)
+    place(right_ref, spot_ref, keep_ref, met_ref, 1, last, blocks_j, width)
     total = jnp.dot(left_ref[...], right_ref[...], preferred_element_type=jnp.float32)
     out_ref[...] = total
     top = jnp.max(jnp.abs(total), axis=0, keepdims=True)
     top_ref[...] = jnp.broadcast_to(top, top_ref.shape)
 
 
-def chip_sums(spot, keep, inv, met, own_pieces, met_pieces, chips, rows):
+def laid_out(spot, keep, inv, met, own_pieces, met_pieces, chips, rows):
     blocks_i, blocks_j, width, _ = inv.shape
     node_count = own_pieces[0].shape[1]
-    slices = len(own_pieces)
-    height = chips * blocks_i * rows
-    across = node_count * width
+    height, depth = chips * blocks_i * rows, CORES * blocks_j * width
     in_vmem = pl.BlockSpec(memory_space=pltpu.VMEM)
     in_smem = pl.BlockSpec(memory_space=pltpu.SMEM)
-    depth = CORES * blocks_j * width
     return pl.pallas_call(
-        functools.partial(sums_kernel, chips, rows, slices),
+        functools.partial(layout_kernel, chips, rows),
+        out_shape=(
+            jax.ShapeDtypeStruct((height, depth), jnp.bfloat16),
+            jax.ShapeDtypeStruct((depth, node_count * width), jnp.bfloat16),
+        ),
+        in_specs=[in_smem, in_smem] + [in_vmem] * (2 + 2 * len(own_pieces)),
+        out_specs=(in_vmem, in_vmem),
+        compiler_params=pltpu.CompilerParams(vmem_limit_bytes=24 << 20),
+        cost_estimate=pl.CostEstimate(flops=0, bytes_accessed=4 << 20, transcendentals=0),
+    )(spot, keep, inv, met, *own_pieces, *met_pieces)
+
+
+def chip_sums(spot, keep, left, right, own_piece, met_piece, last):
+    height, (depth, across) = left.shape[0], right.shape
+    in_vmem = pl.BlockSpec(memory_space=pltpu.VMEM)
+    in_smem = pl.BlockSpec(memory_space=pltpu.SMEM)
+    return pl.pallas_call(
+        functools.partial(sums_kernel, last),
         out_shape=(
             jax.ShapeDtypeStruct((height, across), jnp.float32),
             jax.ShapeDtypeStruct((16, across), jnp.float32),
         ),
-        in_specs=[in_smem, in_smem] + [in_vmem] * (2 + 2 * slices),
+        in_specs=[in_smem, in_smem] + [in_vmem] * 4,
         out_specs=(in_vmem, in_vmem),
-        scratch_shapes=[
-            pltpu.VMEM((height, depth), jnp.bfloat16),
-            pltpu.VMEM((depth, across), jnp.bfloat16),
-        ],
+        scratch_shapes=[pltpu.VMEM((depth, across), jnp.bfloat16)],
         compiler_params=pltpu.CompilerParams(vmem_limit_bytes=24 << 20),
-        cost_estimate=pl.CostEstimate(
-            flops=2 * height * depth * across, bytes_accessed=4 << 20, transcendentals=0
-        ),
-    )(spot, keep, inv, met, *own_pieces, *met_pieces)
+        cost_estimate=pl.CostEstimate(flops=2 * height * depth * across, bytes_accessed=4 << 20, transcendentals=0),
+    )(spot, keep, left, right, own_piece, met_piece)
 
 
 def plain_sums(pcol, keep, inv, met, own_pieces, met_pieces, core, chips, rows):
@@ -146,16 +156,22 @@
         both = jnp.stack([jnp.where(core == 0, mine, other), jnp.where(core == 0, other, mine)])
         return both.reshape(blocks_i, node_count, rows, width)
 
-    bits = [1 << n for n in range(col_groups.bit_length() - 1)]
-    own = own_rows(0) * (chip == pcol).astype(lower_blocks.dtype)
-    first = forward(own_rows(1), 1, col_groups)
-    held[col_groups - 1], first = tied(held[col_groups - 1], first)
+    last = col_groups - 1
     order = range(col_groups)
-    own_pieces, met_pieces = [held[at] for at in order], [met[at] for at in order]
-    if rows % 16 == 0 and (width // col_groups) % 16 == 0:
-        spot = jnp.stack([core, pcol]).astype(jnp.int32)
-        total, top = chip_sums(spot, keep, inverse_blocks, met_inv, own_pieces, met_pieces, chips, rows)
+    fits = rows % 16 == 0 and (width // col_groups) % 16 == 0
+    spot = jnp.stack([core, pcol]).astype(jnp.int32)
+    if fits:
+        left, right = laid_out(
+            spot, keep, inverse_blocks, met_inv,
+            [held[at] for at in order[:-1]], [met[at] for at in order[:-1]], chips, rows,
+        )
+        held[last], left, right = tied(held[last], left, right)
+        met[last] = core_swap(held[last])
+    passed = {at: swap(own_rows(at), "prow", row_groups, at * CORES) for at in range(1, col_groups)}
+    if fits:
+        total, top = chip_sums(spot, keep, left, right, held[last], met[last], last)
     else:
+        own_pieces, met_pieces = [held[at] for at in order], [met[at] for at in order]
         total, top = plain_sums(pcol, keep, inverse_blocks, met_inv, own_pieces, met_pieces, core, chips, rows)
     power = jnp.maximum(jnp.ceil(jnp.log2(top)), -110.0)
     total = total.reshape(chips, blocks_i * rows, across)
@@ -163,18 +179,14 @@
     mark = jnp.broadcast_to(power.astype(jnp.float16), (chips, 16, across))
     packed = jnp.concatenate([scaled, mark], axis=1)
     pieces = {step: take(packed, chip ^ step, 0) for step in range(1, chips)}
-    own = own + first
-    passed = []
-    for bit in bits[1:]:
-        payload, _ = tied(own_rows(bit), pieces[1])
-        passed.append(forward(payload, bit, col_groups))
     summed = take(total, chip, 0)
     for step in range(1, chips):
         came = swap(pieces[step], "prow", row_groups, step * CORES)
         came = lax.optimization_barrier(came.astype(jnp.float32))
         summed = summed + came[:-16] * jnp.exp2(came[-1] - HEADROOM)
-    for part in passed:
-        own = own + part
+    own = own_rows(0)
+    for at in passed:
+        own = jnp.where((chip ^ pcol) == at, passed[at], own)
     own = own * keep_i.astype(jnp.bfloat16)[:, :, None, None]
     column = summed.reshape(blocks_i, rows, node_count, width) * (-keep_i)[:, None, :, None]
 

time: 51.7 us -> 50.8 us (0.983)
  waiting for transfers between devices: 23.2 us -> 20.9 us
  Pallas kernels: 1.6 us -> 2.43 us
  starting transfers between devices: 20.3 us -> 21 us
    ppermute x11 -> x14, starting transfers between devices: 10.2 us -> 16.3 us  [swap(): return lax.ppermute(value, axis, [(at, at ^ step) for at in range(size)])]
    ppermute x2 -> x0, starting transfers between devices: 5.84 us -> none  [forward(): return lax.ppermute(piece, ('prow', 'pcol'), pairs)]
    ppermute x2 -> x0, waiting for transfers between devices: 2.47 us -> none  [forward(): return lax.ppermute(piece, ('prow', 'pcol'), pairs)]
    pallas_call x1 -> x2, Pallas kernels: 1.6 us -> 2.43 us  [the longest x1 1.44 us: chip_sums(): pl.pallas_call(functools.partial(sums_kernel, last), out_shape=(jax.Shape...]
    ppermute x11 -> x14, waiting for transfers between devices: 11.3 us -> 11.5 us  [swap(): return lax.ppermute(value, axis, [(at, at ^ step) for at in range(size)])]
  transfers between devices with their start and end apart: 14 -> 15, of which waited for: 9 -> 6; matrix products, arithmetic and copies ran while one was open for 6% -> 7% of each run, Pallas kernels for 0% -> 5%
where the time goes in v4:
time: 50.8 us; the launch traced here: 50.6 us
  starting transfers between devices  21 us (41%)
  waiting for transfers between devices  20.9 us (41%)
  local copies, waits for them, and re-layouts  2.54 us (5%)
  other arithmetic  2.46 us (5%)
  Pallas kernels  2.43 us (5%)
  between operations  0.87 us (2%)
    ppermute x14, starting transfers between devices, swap(): return lax.ppermute(value, axis, [(at, at ^ step) for at in range(size)])  16.3 us
    ppermute x14, waiting for transfers between devices, swap(): return lax.ppermute(value, axis, [(at, at ^ step) for at in range(size)])  11.5 us
    all_to_all x1, waiting for transfers between devices, per_device(): lax.all_to_all(update, ('prow', 'pcol'), 0, 0, tiled=True)  9.39 us
    all_to_all x1, starting transfers between devices, per_device(): lax.all_to_all(update, ('prow', 'pcol'), 0, 0, tiled=True)  4.68 us
    pallas_call x1, Pallas kernels, chip_sums(): pl.pallas_call(functools.partial(sums_kernel, last), out_shape=(jax.Shape...  1.44 us
    squeeze x1, local copies, waits for them, and re-layouts, take(): return lax.dynamic_index_in_dim(value, index, axis, keepdims=False)  1.17 us
  transfers between devices with their start and end apart: 15, of which 6 were waited for; matrix products, arithmetic and copies ran while one was open for 7% of the time, Pallas kernels for 5%

profile of v4, /device:TPU:0, one launch (start us, length us, event | category | flops | bytes accessed | tf_op | source)
XLA Modules:
  0.0 50.6 jit_solution(9584608426293267834)
XLA Ops:
  0.6 4.1 %collective-permute-start = (bf16[4,4,32,128]{3,2,1,0:T(8,128)(2,1)}, bf16[4,4,32,128]{3,2,1,0:T(8,128)(2,1)S(1)}, u32[]{:S(2)}, u32[]{:S(2)}) collective-permute-start(bf16[4,4,32,128]{3,2,1,0:T(8,128)(2,1)} %refs_0_.1), channel_id=1, source_target_pairs={{0,2},{1,3},{2,0},{3,1},{4,6},{5,7},{6,4},{7,5},{8,10},{9,11},{10,... | collective-permute-start | bytes 393224 | tf_op jit(solution)/shard_map/ppermute | solution.py:15
  4.7 1.6 %collective-permute-start.3 = (bf16[4,4,32,128]{3,2,1,0:T(8,128)(2,1)}, bf16[4,4,32,128]{3,2,1,0:T(8,128)(2,1)S(1)}, u32[]{:S(2)}, u32[]{:S(2)}) collective-permute-start(bf16[4,4,32,128]{3,2,1,0:T(8,128)(2,1)} %refs_0_.1), channel_id=1, source_target_pairs={{0,1},{1,0},{2,3},{3,2},{4,5},{5,4},{6,7},{7,6},{8,9},{9,8},{10,11... | collective-permute-start | bytes 393224 | tf_op jit(solution)/shard_map/ppermute | solution.py:15
  6.3 0.0 collective-permute-start.4
  6.3 1.2 %dynamic-slice_bitcast_fusion = bf16[8,4,4,16,128]{4,3,2,1,0:T(8,128)(2,1)S(1)} fusion(bf16[8,4,4,2,16,128]{5,4,3,2,1,0:T(8,128)(2,1)} %bitcast.109, s32[]{:T(128)S(6)} %select_n.188), kind=kLoop, calls=%fused_computation.4 | loop fusion | bytes 1048580 | tf_op jit(solution)/shard_map/jit(dynamic_index_in_dim)/squeeze | solution.py:19
  7.5 0.0 copy-start.1
  7.5 0.6 %collective-permute-start.2 = (bf16[8,4,4,16,128]{4,3,2,1,0:T(8,128)(2,1)S(1)}, bf16[8,4,4,16,128]{4,3,2,1,0:T(8,128)(2,1)S(1)}, u32[]{:S(2)}, u32[]{:S(2)}) collective-permute-start(bf16[8,4,4,16,128]{4,3,2,1,0:T(8,128)(2,1)S(1)} %dynamic-slice_bitcast_fusion), channel_id=1, source_target_pairs={{0,4},{4,0},{8,12},{12,8},{16,20},{20,16},{24,28},{28,24},{1,5},{5... | collective-permute-start | bytes 1572872 | tf_op jit(solution)/shard_map/ppermute | solution.py:15
  8.1 0.1 convert_reduce_fusion
  8.2 0.1 constant_dynamic-slice_fusion.2
  8.2 0.1 copy.60
  8.3 0.1 copy.61
  8.4 0.1 fusion.32
  8.5 0.1 fusion.31
  8.6 0.1 pad_add_fusion.spot_ref
  8.7 0.1 copy.58
  8.8 0.1 copy.46
  8.8 2.5 %collective-permute-done.refs_2_ = bf16[4,4,32,128]{3,2,1,0:T(8,128)(2,1)S(1)} collective-permute-done((bf16[4,4,32,128]{3,2,1,0:T(8,128)(2,1)}, bf16[4,4,32,128]{3,2,1,0:T(8,128)(2,1)S(1)}, u32[]{:S(2)}, u32[]{:S(2)}) %collective-permute-start) | collective-permute-done | bytes 131104 | tf_op jit(solution)/shard_map/ppermute | solution.py:15
  11.4 0.0 collective-permute-start.6
  11.4 0.8 %collective-permute-start.1 = (bf16[4,4,32,128]{3,2,1,0:T(8,128)(2,1)S(1)}, bf16[4,4,32,128]{3,2,1,0:T(8,128)(2,1)S(1)}, u32[]{:S(2)}, u32[]{:S(2)}) collective-permute-start(bf16[4,4,32,128]{3,2,1,0:T(8,128)(2,1)S(1)} %collective-permute-done.refs_2_), channel_id=1, source_target_pairs={{0,1},{1,0},{2,3},{3,2},{4,5},{5,4},{6,7},{7,6},{8,9},{9,8},{10,11... | collective-permute-start | bytes 393224 | tf_op jit(solution)/shard_map/ppermute | solution.py:15
  12.2 0.2 collective-permute-start.5
  12.4 0.3 collective-permute-done.6.refs_5_
  12.7 1.6 %collective-permute-start.12 = (bf16[8,4,16,128]{3,2,1,0:T(8,128)(2,1)S(1)}, bf16[8,4,16,128]{3,2,1,0:T(8,128)(2,1)S(1)}, u32[]{:S(2)}, u32[]{:S(2)}) collective-permute-start(bf16[8,4,16,128]{3,2,1,0:T(8,128)(2,1)S(1)} %bitcast.123), channel_id=1, source_target_pairs={{0,16},{4,20},{8,24},{12,28},{16,0},{20,4},{24,8},{28,12},{1,17},{... | collective-permute-start | bytes 393224 | tf_op jit(solution)/shard_map/ppermute | solution.py:15
  14.4 0.0 collective-permute-done.2.met_ref
  14.4 1.0 %shard_map.59 = (bf16[512,1024]{1,0:T(8,128)(2,1)S(1)}, bf16[1024,512]{1,0:T(8,128)(2,1)S(1)}) custom-call(s32[2]{0:T(128)S(1)} %pad_add_fusion.spot_ref, f32[8,4]{1,0:T(8,128)S(1)} %pad_maximum_fusion.4.keep_ref, bf16[8,4,128,128]{3,2,1,0:T(8,128)(2,1)S(1)} %copy-done, bf16[8,4,4,16,128]{4,3,2,1,0:T(8,128)(2,1)S(1)} %collective-permute-done.2.met_ref, ...), custom_call_target="tpu_custom_call" | custom-call | bytes 4194304 | tf_op jit(solution)/shard_map/pallas_call | solution.py:71
  15.4 2.0 %collective-permute-done.1.own_ref = bf16[4,4,32,128]{3,2,1,0:T(8,128)(2,1)S(1)} collective-permute-done((bf16[4,4,32,128]{3,2,1,0:T(8,128)(2,1)S(1)}, bf16[4,4,32,128]{3,2,1,0:T(8,128)(2,1)S(1)}, u32[]{:S(2)}, u32[]{:S(2)}) %collective-permute-start.1) | collective-permute-done | bytes 131104 | tf_op jit(solution)/shard_map/ppermute | solution.py:15
  17.4 0.0 collective-permute-start.7
  17.4 1.6 %collective-permute-start.13 = (bf16[8,4,16,128]{3,2,1,0:T(8,128)(2,1)S(1)}, bf16[8,4,16,128]{3,2,1,0:T(8,128)(2,1)S(1)}, u32[]{:S(2)}, u32[]{:S(2)}) collective-permute-start(bf16[8,4,16,128]{3,2,1,0:T(8,128)(2,1)S(1)} %bitcast.124), channel_id=1, source_target_pairs={{0,8},{4,12},{8,0},{12,4},{16,24},{20,28},{24,16},{28,20},{1,9},{5... | collective-permute-start | bytes 393224 | tf_op jit(solution)/shard_map/ppermute | solution.py:15
  19.1 2.3 %collective-permute-start.11 = (bf16[8,4,16,128]{3,2,1,0:T(8,128)(2,1)S(1)}, bf16[8,4,16,128]{3,2,1,0:T(8,128)(2,1)S(1)}, u32[]{:S(2)}, u32[]{:S(2)}) collective-permute-start(bf16[8,4,16,128]{3,2,1,0:T(8,128)(2,1)S(1)} %bitcast.125), channel_id=1, source_target_pairs={{0,24},{4,28},{8,16},{12,20},{16,8},{20,12},{24,0},{28,4},{1,25},{... | collective-permute-start | bytes 393224 | tf_op jit(solution)/shard_map/ppermute | solution.py:15
  21.3 1.4 %shard_map.60 = (f32[512,512]{1,0:T(8,128)S(1)}, f32[16,512]{1,0:T(8,128)S(1)}) custom-call(s32[2]{0:T(128)S(1)} %pad_add_fusion.spot_ref, f32[8,4]{1,0:T(8,128)S(1)} %pad_maximum_fusion.4.keep_ref, bf16[512,1024]{1,0:T(8,128)(2,1)S(1)} %get-tuple-element.11.left_ref, bf16[1024,512]{1,0:T(8,128)(2,1)S(1)} %get-tuple-element.12.given_ref, ...), custom_call_target="tpu_custom_call" | custom-call | flops 536870912 | bytes 4194304 | tf_op jit(solution)/shard_map/pallas_call | solution.py:88
  22.8 0.1 multiply_convert_fusion
  23.0 0.1 fusion.9
  23.1 0.6 %collective-permute-start.9 = (f16[144,512]{1,0:T(8,128)(2,1)S(1)}, f16[144,512]{1,0:T(8,128)(2,1)S(1)}, u32[]{:S(2)}, u32[]{:S(2)}) collective-permute-start(f16[144,512]{1,0:T(8,128)(2,1)S(1)} %get-tuple-element.17), channel_id=1, source_target_pairs={{0,16},{4,20},{8,24},{12,28},{16,0},{20,4},{24,8},{28,12},{1,17},{... | collective-permute-start | bytes 442376 | tf_op jit(solution)/shard_map/ppermute | solution.py:15
  23.7 1.7 %collective-permute-start.10 = (f16[144,512]{1,0:T(8,128)(2,1)S(1)}, f16[144,512]{1,0:T(8,128)(2,1)S(1)}, u32[]{:S(2)}, u32[]{:S(2)}) collective-permute-start(f16[144,512]{1,0:T(8,128)(2,1)S(1)} %get-tuple-element.18), channel_id=1, source_target_pairs={{0,24},{4,28},{8,16},{12,20},{16,8},{20,12},{24,0},{28,4},{1,25},{... | collective-permute-start | bytes 442376 | tf_op jit(solution)/shard_map/ppermute | solution.py:15
  25.4 0.0 collective-permute-done.12
  25.4 1.2 %collective-permute-start.8 = (f16[144,512]{1,0:T(8,128)(2,1)S(1)}, f16[144,512]{1,0:T(8,128)(2,1)S(1)}, u32[]{:S(2)}, u32[]{:S(2)}) collective-permute-start(f16[144,512]{1,0:T(8,128)(2,1)S(1)} %get-tuple-element.16), channel_id=1, source_target_pairs={{0,8},{4,12},{8,0},{12,4},{16,24},{20,28},{24,16},{28,20},{1,9},{5... | collective-permute-start | bytes 442376 | tf_op jit(solution)/shard_map/ppermute | solution.py:15
  26.7 0.0 collective-permute-done.13
  26.7 1.0 %collective-permute-done.11 = bf16[8,4,16,128]{3,2,1,0:T(8,128)(2,1)S(1)} collective-permute-done((bf16[8,4,16,128]{3,2,1,0:T(8,128)(2,1)S(1)}, bf16[8,4,16,128]{3,2,1,0:T(8,128)(2,1)S(1)}, u32[]{:S(2)}, u32[]{:S(2)}) %collective-permute-start.11) | collective-permute-done | bytes 131104 | tf_op jit(solution)/shard_map/ppermute | solution.py:15
  27.7 0.1 fusion.13
  27.8 5.7 %collective-permute-done.9 = f16[144,512]{1,0:T(8,128)(2,1)S(1)} collective-permute-done((f16[144,512]{1,0:T(8,128)(2,1)S(1)}, f16[144,512]{1,0:T(8,128)(2,1)S(1)}, u32[]{:S(2)}, u32[]{:S(2)}) %collective-permute-start.9) | collective-permute-done | bytes 147488 | tf_op jit(solution)/shard_map/ppermute | solution.py:15
  33.6 0.0 collective-permute-done.10
  33.7 0.1 fusion
  33.8 0.1 reshape.224
  33.9 0.3 fusion.3
  34.3 0.7 %copy.59 = f32[32,4,4,128]{3,1,2,0:T(4,128)} copy(f32[32,4,4,128]{3,1,0,2:T(4,128)S(1)} %bitcast.122) | data formatting | bytes 524288 | tf_op jit(solution)/shard_map/reshape | solution.py:197
  35.0 4.7 %all-to-all-start = ((f32[32,4,4,128]{3,1,2,0:T(4,128)}), f32[32,4,4,128]{3,1,2,0:T(4,128)S(1)}, u32[]{:S(2)}, u32[]{:S(2)}) async-start(f32[32,4,4,128]{3,1,2,0:T(4,128)} %copy.59), calls=%async_computation | async-start | bytes 524288 | tf_op jit(solution)/shard_map/all_to_all | solution.py:198
  39.7 0.8 %fusion.4 = f32[8,4,16,128]{3,2,1,0:T(8,128)} fusion(f32[8,16,4,128]{3,2,1,0:T(4,128)S(1)} %reshape.224, f32[8,4]{1,0:T(8,128)S(1)} %copy.46), kind=kLoop, calls=%fused_computation.16 | loop fusion | flops 65536 | bytes 524416 | tf_op jit(solution)/shard_map/transpose | solution.py:204
  40.5 9.4 %all-to-all-done = f32[32,4,4,128]{3,1,2,0:T(4,128)S(1)} async-done(((f32[32,4,4,128]{3,1,2,0:T(4,128)}), f32[32,4,4,128]{3,1,2,0:T(4,128)S(1)}, u32[]{:S(2)}, u32[]{:S(2)}) %all-to-all-start) | async-done | bytes 262176 | tf_op jit(solution)/shard_map/all_to_all | solution.py:198
  49.9 0.1 reduce_sum.19
  50.0 0.6 %bitcast_subtract_fusion = f32[4,512]{1,0:T(4,128)} fusion(f32[4,512]{1,0:T(4,128)S(1)} %copy-done.2, f32[1,4,4,128]{3,2,1,0:T(4,128)S(1)} %bitcast.126), kind=kLoop, calls=%fused_computation.51 | loop fusion | flops 2048 | bytes 24576 | tf_op jit(solution)/shard_map/sub | solution.py:204
  (31 shorter events, 0.3 us)
Async XLA Ops:
  0.6 10.7 %collective-permute-start = (bf16[4,4,32,128]{3,2,1,0:T(8,128)(2,1)}, bf16[4,4,32,128]{3,2,1,0:T(8,128)(2,1)S(1)}, u32[]{:S(2)}, u32[]{:S(2)}) collective-permute-start(bf16[4,4,32,128]{3,2,1,0:T(8,128)(2,1)} %refs_0_.1), channel_id=1, source_target_pairs={{0,2},{1,3},{2,0},{3,1},{4,6},{5,7},{6,4},{7,5},{8,10},{9,11},{10,... | collective-permute-start | bytes 393224 | tf_op jit(solution)/shard_map/ppermute | solution.py:15
  4.7 7.5 %collective-permute-start.3 = (bf16[4,4,32,128]{3,2,1,0:T(8,128)(2,1)}, bf16[4,4,32,128]{3,2,1,0:T(8,128)(2,1)S(1)}, u32[]{:S(2)}, u32[]{:S(2)}) collective-permute-start(bf16[4,4,32,128]{3,2,1,0:T(8,128)(2,1)} %refs_0_.1), channel_id=1, source_target_pairs={{0,1},{1,0},{2,3},{3,2},{4,5},{5,4},{6,7},{7,6},{8,9},{9,8},{10,11... | collective-permute-start | bytes 393224 | tf_op jit(solution)/shard_map/ppermute | solution.py:15
  6.3 5.1 %collective-permute-start.4 = (bf16[4,4,32,128]{3,2,1,0:T(8,128)(2,1)}, bf16[4,4,32,128]{3,2,1,0:T(8,128)(2,1)S(1)}, u32[]{:S(2)}, u32[]{:S(2)}) collective-permute-start(bf16[4,4,32,128]{3,2,1,0:T(8,128)(2,1)} %refs_0_.1), channel_id=1, source_target_pairs={{0,4},{4,0},{8,12},{12,8},{16,20},{20,16},{24,28},{28,24},{1,5},{5... | collective-permute-start | bytes 393224 | tf_op jit(solution)/shard_map/ppermute | solution.py:15
  6.3 1.8 %copy-start.3 = (s32[4,16]{1,0:T(4,128)S(1)}, s32[4,16]{1,0:T(4,128)}, u32[]{:S(2)}) copy-start(s32[4,16]{1,0:T(4,128)} %param.6) | copy-start | bytes 772
  6.3 8.1 %copy-start = (bf16[8,4,128,128]{3,2,1,0:T(8,128)(2,1)S(1)}, bf16[8,4,128,128]{3,2,1,0:T(8,128)(2,1)}, u32[]{:S(2)}) copy-start(bf16[8,4,128,128]{3,2,1,0:T(8,128)(2,1)} %inv_ref.1) | copy-start | bytes 3145732
  7.5 3.9 %copy-start.1 = (bf16[4,4,32,128]{3,2,1,0:T(8,128)(2,1)S(1)}, bf16[4,4,32,128]{3,2,1,0:T(8,128)(2,1)}, u32[]{:S(2)}) copy-start(bf16[4,4,32,128]{3,2,1,0:T(8,128)(2,1)} %refs_0_.1) | copy-start | bytes 393220
  7.5 6.9 %collective-permute-start.2 = (bf16[8,4,4,16,128]{4,3,2,1,0:T(8,128)(2,1)S(1)}, bf16[8,4,4,16,128]{4,3,2,1,0:T(8,128)(2,1)S(1)}, u32[]{:S(2)}, u32[]{:S(2)}) collective-permute-start(bf16[8,4,4,16,128]{4,3,2,1,0:T(8,128)(2,1)S(1)} %dynamic-slice_bitcast_fusion), channel_id=1, source_target_pairs={{0,4},{4,0},{8,12},{12,8},{16,20},{20,16},{24,28},{28,24},{1,5},{5... | collective-permute-start | bytes 1572872 | tf_op jit(solution)/shard_map/ppermute | solution.py:15
  11.4 1.3 %collective-permute-start.6 = (bf16[4,4,32,128]{3,2,1,0:T(8,128)(2,1)S(1)}, bf16[4,4,32,128]{3,2,1,0:T(8,128)(2,1)S(1)}, u32[]{:S(2)}, u32[]{:S(2)}) collective-permute-start(bf16[4,4,32,128]{3,2,1,0:T(8,128)(2,1)S(1)} %collective-permute-done.refs_2_), channel_id=1, source_target_pairs={{0,4},{4,0},{8,12},{12,8},{16,20},{20,16},{24,28},{28,24},{1,5},{5... | collective-permute-start | bytes 393224 | tf_op jit(solution)/shard_map/ppermute | solution.py:15
  11.4 6.0 %collective-permute-start.1 = (bf16[4,4,32,128]{3,2,1,0:T(8,128)(2,1)S(1)}, bf16[4,4,32,128]{3,2,1,0:T(8,128)(2,1)S(1)}, u32[]{:S(2)}, u32[]{:S(2)}) collective-permute-start(bf16[4,4,32,128]{3,2,1,0:T(8,128)(2,1)S(1)} %collective-permute-done.refs_2_), channel_id=1, source_target_pairs={{0,1},{1,0},{2,3},{3,2},{4,5},{5,4},{6,7},{7,6},{8,9},{9,8},{10,11... | collective-permute-start | bytes 393224 | tf_op jit(solution)/shard_map/ppermute | solution.py:15
  12.2 2.2 %collective-permute-start.5 = (bf16[4,4,32,128]{3,2,1,0:T(8,128)(2,1)S(1)}, bf16[4,4,32,128]{3,2,1,0:T(8,128)(2,1)S(1)}, u32[]{:S(2)}, u32[]{:S(2)}) collective-permute-start(bf16[4,4,32,128]{3,2,1,0:T(8,128)(2,1)S(1)} %collective-permute-done.3.refs_1_), channel_id=1, source_target_pairs={{0,4},{4,0},{8,12},{12,8},{16,20},{20,16},{24,28},{28,24},{1,5},{5... | collective-permute-start | bytes 393224 | tf_op jit(solution)/shard_map/ppermute | solution.py:15
  12.7 12.7 %collective-permute-start.12 = (bf16[8,4,16,128]{3,2,1,0:T(8,128)(2,1)S(1)}, bf16[8,4,16,128]{3,2,1,0:T(8,128)(2,1)S(1)}, u32[]{:S(2)}, u32[]{:S(2)}) collective-permute-start(bf16[8,4,16,128]{3,2,1,0:T(8,128)(2,1)S(1)} %bitcast.123), channel_id=1, source_target_pairs={{0,16},{4,20},{8,24},{12,28},{16,0},{20,4},{24,8},{28,12},{1,17},{... | collective-permute-start | bytes 393224 | tf_op jit(solution)/shard_map/ppermute | solution.py:15
  17.4 1.6 %collective-permute-start.7 = (bf16[4,4,32,128]{3,2,1,0:T(8,128)(2,1)S(1)}, bf16[4,4,32,128]{3,2,1,0:T(8,128)(2,1)S(1)}, u32[]{:S(2)}, u32[]{:S(2)}) collective-permute-start(bf16[4,4,32,128]{3,2,1,0:T(8,128)(2,1)S(1)} %collective-permute-done.1.own_ref), channel_id=1, source_target_pairs={{0,4},{4,0},{8,12},{12,8},{16,20},{20,16},{24,28},{28,24},{1,5},{5... | collective-permute-start | bytes 393224 | tf_op jit(solution)/shard_map/ppermute | solution.py:15
  17.4 9.3 %collective-permute-start.13 = (bf16[8,4,16,128]{3,2,1,0:T(8,128)(2,1)S(1)}, bf16[8,4,16,128]{3,2,1,0:T(8,128)(2,1)S(1)}, u32[]{:S(2)}, u32[]{:S(2)}) collective-permute-start(bf16[8,4,16,128]{3,2,1,0:T(8,128)(2,1)S(1)} %bitcast.124), channel_id=1, source_target_pairs={{0,8},{4,12},{8,0},{12,4},{16,24},{20,28},{24,16},{28,20},{1,9},{5... | collective-permute-start | bytes 393224 | tf_op jit(solution)/shard_map/ppermute | solution.py:15
  19.1 8.6 %collective-permute-start.11 = (bf16[8,4,16,128]{3,2,1,0:T(8,128)(2,1)S(1)}, bf16[8,4,16,128]{3,2,1,0:T(8,128)(2,1)S(1)}, u32[]{:S(2)}, u32[]{:S(2)}) collective-permute-start(bf16[8,4,16,128]{3,2,1,0:T(8,128)(2,1)S(1)} %bitcast.125), channel_id=1, source_target_pairs={{0,24},{4,28},{8,16},{12,20},{16,8},{20,12},{24,0},{28,4},{1,25},{... | collective-permute-start | bytes 393224 | tf_op jit(solution)/shard_map/ppermute | solution.py:15
  23.1 10.4 %collective-permute-start.9 = (f16[144,512]{1,0:T(8,128)(2,1)S(1)}, f16[144,512]{1,0:T(8,128)(2,1)S(1)}, u32[]{:S(2)}, u32[]{:S(2)}) collective-permute-start(f16[144,512]{1,0:T(8,128)(2,1)S(1)} %get-tuple-element.17), channel_id=1, source_target_pairs={{0,16},{4,20},{8,24},{12,28},{16,0},{20,4},{24,8},{28,12},{1,17},{... | collective-permute-start | bytes 442376 | tf_op jit(solution)/shard_map/ppermute | solution.py:15
  23.7 9.9 %collective-permute-start.10 = (f16[144,512]{1,0:T(8,128)(2,1)S(1)}, f16[144,512]{1,0:T(8,128)(2,1)S(1)}, u32[]{:S(2)}, u32[]{:S(2)}) collective-permute-start(f16[144,512]{1,0:T(8,128)(2,1)S(1)} %get-tuple-element.18), channel_id=1, source_target_pairs={{0,24},{4,28},{8,16},{12,20},{16,8},{20,12},{24,0},{28,4},{1,25},{... | collective-permute-start | bytes 442376 | tf_op jit(solution)/shard_map/ppermute | solution.py:15
  25.4 8.2 %collective-permute-start.8 = (f16[144,512]{1,0:T(8,128)(2,1)S(1)}, f16[144,512]{1,0:T(8,128)(2,1)S(1)}, u32[]{:S(2)}, u32[]{:S(2)}) collective-permute-start(f16[144,512]{1,0:T(8,128)(2,1)S(1)} %get-tuple-element.16), channel_id=1, source_target_pairs={{0,8},{4,12},{8,0},{12,4},{16,24},{20,28},{24,16},{28,20},{1,9},{5... | collective-permute-start | bytes 442376 | tf_op jit(solution)/shard_map/ppermute | solution.py:15
  35.0 14.9 %all-to-all-start = ((f32[32,4,4,128]{3,1,2,0:T(4,128)}), f32[32,4,4,128]{3,1,2,0:T(4,128)S(1)}, u32[]{:S(2)}, u32[]{:S(2)}) async-start(f32[32,4,4,128]{3,1,2,0:T(4,128)} %copy.59), calls=%async_computation | async-start | bytes 524288 | tf_op jit(solution)/shard_map/all_to_all | solution.py:198
  40.5 9.5 %copy-start.2 = (f32[4,512]{1,0:T(4,128)S(1)}, f32[4,512]{1,0:T(4,128)}, u32[]{:S(2)}) copy-start(f32[4,512]{1,0:T(4,128)} %param.7) | copy-start | bytes 24580

commit v5 on v4

--- a/solution.py
+++ b/solution.py
@@ -176,14 +176,14 @@
     power = jnp.maximum(jnp.ceil(jnp.log2(top)), -110.0)
     total = total.reshape(chips, blocks_i * rows, across)
     scaled = (total * jnp.exp2(HEADROOM - power[0])).astype(jnp.float16)
-    mark = jnp.broadcast_to(power.astype(jnp.float16), (chips, 16, across))
+    mark = jnp.broadcast_to(power[:8].astype(jnp.float16), (chips, 8, across))
     packed = jnp.concatenate([scaled, mark], axis=1)
     pieces = {step: take(packed, chip ^ step, 0) for step in range(1, chips)}
     summed = take(total, chip, 0)
     for step in range(1, chips):
         came = swap(pieces[step], "prow", row_groups, step * CORES)
         came = lax.optimization_barrier(came.astype(jnp.float32))
-        summed = summed + came[:-16] * jnp.exp2(came[-1] - HEADROOM)
+        summed = summed + came[:-8] * jnp.exp2(came[-1] - HEADROOM)
     own = own_rows(0)
     for at in passed:
         own = jnp.where((chip ^ pcol) == at, passed[at], own)

time: 50.8 us -> 50.4 us (level)
  no operation moved by 1% of the time
where the time goes in v5:
time: 50.4 us; the launch traced here: 50.2 us
  starting transfers between devices  21 us (42%)
  waiting for transfers between devices  20.6 us (41%)
  local copies, waits for them, and re-layouts  2.54 us (5%)
  other arithmetic  2.45 us (5%)
  Pallas kernels  2.43 us (5%)
  between operations  0.88 us (2%)
    ppermute x14, starting transfers between devices, swap(): return lax.ppermute(value, axis, [(at, at ^ step) for at in range(size)])  16.3 us
    ppermute x14, waiting for transfers between devices, swap(): return lax.ppermute(value, axis, [(at, at ^ step) for at in range(size)])  11.2 us
    all_to_all x1, waiting for transfers between devices, per_device(): lax.all_to_all(update, ('prow', 'pcol'), 0, 0, tiled=True)  9.39 us
    all_to_all x1, starting transfers between devices, per_device(): lax.all_to_all(update, ('prow', 'pcol'), 0, 0, tiled=True)  4.68 us
    pallas_call x1, Pallas kernels, chip_sums(): pl.pallas_call(functools.partial(sums_kernel, last), out_shape=(jax.Shape...  1.44 us
    squeeze x1, local copies, waits for them, and re-layouts, take(): return lax.dynamic_index_in_dim(value, index, axis, keepdims=False)  1.17 us
  transfers between devices with their start and end apart: 15, of which 6 were waited for; matrix products, arithmetic and copies ran while one was open for 7% of the time, Pallas kernels for 5%

profile of v5, /device:TPU:0, one launch (start us, length us, event | category | flops | bytes accessed | tf_op | source)
XLA Modules:
  0.0 50.2 jit_solution(3824943307784143116)
XLA Ops:
  0.6 4.1 %collective-permute-start = (bf16[4,4,32,128]{3,2,1,0:T(8,128)(2,1)}, bf16[4,4,32,128]{3,2,1,0:T(8,128)(2,1)S(1)}, u32[]{:S(2)}, u32[]{:S(2)}) collective-permute-start(bf16[4,4,32,128]{3,2,1,0:T(8,128)(2,1)} %refs_0_.1), channel_id=1, source_target_pairs={{0,2},{1,3},{2,0},{3,1},{4,6},{5,7},{6,4},{7,5},{8,10},{9,11},{10,... | collective-permute-start | bytes 393224 | tf_op jit(solution)/shard_map/ppermute | solution.py:15
  4.7 1.6 %collective-permute-start.3 = (bf16[4,4,32,128]{3,2,1,0:T(8,128)(2,1)}, bf16[4,4,32,128]{3,2,1,0:T(8,128)(2,1)S(1)}, u32[]{:S(2)}, u32[]{:S(2)}) collective-permute-start(bf16[4,4,32,128]{3,2,1,0:T(8,128)(2,1)} %refs_0_.1), channel_id=1, source_target_pairs={{0,1},{1,0},{2,3},{3,2},{4,5},{5,4},{6,7},{7,6},{8,9},{9,8},{10,11... | collective-permute-start | bytes 393224 | tf_op jit(solution)/shard_map/ppermute | solution.py:15
  6.3 0.0 collective-permute-start.4
  6.3 1.2 %dynamic-slice_bitcast_fusion = bf16[8,4,4,16,128]{4,3,2,1,0:T(8,128)(2,1)S(1)} fusion(bf16[8,4,4,2,16,128]{5,4,3,2,1,0:T(8,128)(2,1)} %bitcast.109, s32[]{:T(128)S(6)} %select_n.188), kind=kLoop, calls=%fused_computation.4 | loop fusion | bytes 1048580 | tf_op jit(solution)/shard_map/jit(dynamic_index_in_dim)/squeeze | solution.py:19
  7.5 0.0 copy-start.1
  7.5 0.6 %collective-permute-start.2 = (bf16[8,4,4,16,128]{4,3,2,1,0:T(8,128)(2,1)S(1)}, bf16[8,4,4,16,128]{4,3,2,1,0:T(8,128)(2,1)S(1)}, u32[]{:S(2)}, u32[]{:S(2)}) collective-permute-start(bf16[8,4,4,16,128]{4,3,2,1,0:T(8,128)(2,1)S(1)} %dynamic-slice_bitcast_fusion), channel_id=1, source_target_pairs={{0,4},{4,0},{8,12},{12,8},{16,20},{20,16},{24,28},{28,24},{1,5},{5... | collective-permute-start | bytes 1572872 | tf_op jit(solution)/shard_map/ppermute | solution.py:15
  8.1 0.1 convert_reduce_fusion
  8.2 0.1 constant_dynamic-slice_fusion.2
  8.2 0.1 copy.60
  8.3 0.1 copy.61
  8.4 0.1 fusion.32
  8.5 0.1 fusion.31
  8.6 0.1 pad_add_fusion.spot_ref
  8.7 0.1 copy.58
  8.8 0.1 copy.46
  8.8 2.5 %collective-permute-done.refs_2_ = bf16[4,4,32,128]{3,2,1,0:T(8,128)(2,1)S(1)} collective-permute-done((bf16[4,4,32,128]{3,2,1,0:T(8,128)(2,1)}, bf16[4,4,32,128]{3,2,1,0:T(8,128)(2,1)S(1)}, u32[]{:S(2)}, u32[]{:S(2)}) %collective-permute-start) | collective-permute-done | bytes 131104 | tf_op jit(solution)/shard_map/ppermute | solution.py:15
  11.4 0.0 collective-permute-start.6
  11.4 0.8 %collective-permute-start.1 = (bf16[4,4,32,128]{3,2,1,0:T(8,128)(2,1)S(1)}, bf16[4,4,32,128]{3,2,1,0:T(8,128)(2,1)S(1)}, u32[]{:S(2)}, u32[]{:S(2)}) collective-permute-start(bf16[4,4,32,128]{3,2,1,0:T(8,128)(2,1)S(1)} %collective-permute-done.refs_2_), channel_id=1, source_target_pairs={{0,1},{1,0},{2,3},{3,2},{4,5},{5,4},{6,7},{7,6},{8,9},{9,8},{10,11... | collective-permute-start | bytes 393224 | tf_op jit(solution)/shard_map/ppermute | solution.py:15
  12.2 0.2 collective-permute-start.5
  12.4 0.3 collective-permute-done.6.refs_5_
  12.7 1.6 %collective-permute-start.12 = (bf16[8,4,16,128]{3,2,1,0:T(8,128)(2,1)S(1)}, bf16[8,4,16,128]{3,2,1,0:T(8,128)(2,1)S(1)}, u32[]{:S(2)}, u32[]{:S(2)}) collective-permute-start(bf16[8,4,16,128]{3,2,1,0:T(8,128)(2,1)S(1)} %bitcast.123), channel_id=1, source_target_pairs={{0,16},{4,20},{8,24},{12,28},{16,0},{20,4},{24,8},{28,12},{1,17},{... | collective-permute-start | bytes 393224 | tf_op jit(solution)/shard_map/ppermute | solution.py:15
  14.4 0.0 collective-permute-done.2.met_ref
  14.4 1.0 %shard_map.59 = (bf16[512,1024]{1,0:T(8,128)(2,1)S(1)}, bf16[1024,512]{1,0:T(8,128)(2,1)S(1)}) custom-call(s32[2]{0:T(128)S(1)} %pad_add_fusion.spot_ref, f32[8,4]{1,0:T(8,128)S(1)} %pad_maximum_fusion.4.keep_ref, bf16[8,4,128,128]{3,2,1,0:T(8,128)(2,1)S(1)} %copy-done, bf16[8,4,4,16,128]{4,3,2,1,0:T(8,128)(2,1)S(1)} %collective-permute-done.2.met_ref, ...), custom_call_target="tpu_custom_call" | custom-call | bytes 4194304 | tf_op jit(solution)/shard_map/pallas_call | solution.py:71
  15.4 2.0 %collective-permute-done.1.own_ref = bf16[4,4,32,128]{3,2,1,0:T(8,128)(2,1)S(1)} collective-permute-done((bf16[4,4,32,128]{3,2,1,0:T(8,128)(2,1)S(1)}, bf16[4,4,32,128]{3,2,1,0:T(8,128)(2,1)S(1)}, u32[]{:S(2)}, u32[]{:S(2)}) %collective-permute-start.1) | collective-permute-done | bytes 131104 | tf_op jit(solution)/shard_map/ppermute | solution.py:15
  17.4 0.0 collective-permute-start.7
  17.4 1.6 %collective-permute-start.13 = (bf16[8,4,16,128]{3,2,1,0:T(8,128)(2,1)S(1)}, bf16[8,4,16,128]{3,2,1,0:T(8,128)(2,1)S(1)}, u32[]{:S(2)}, u32[]{:S(2)}) collective-permute-start(bf16[8,4,16,128]{3,2,1,0:T(8,128)(2,1)S(1)} %bitcast.124), channel_id=1, source_target_pairs={{0,8},{4,12},{8,0},{12,4},{16,24},{20,28},{24,16},{28,20},{1,9},{5... | collective-permute-start | bytes 393224 | tf_op jit(solution)/shard_map/ppermute | solution.py:15
  19.1 2.3 %collective-permute-start.11 = (bf16[8,4,16,128]{3,2,1,0:T(8,128)(2,1)S(1)}, bf16[8,4,16,128]{3,2,1,0:T(8,128)(2,1)S(1)}, u32[]{:S(2)}, u32[]{:S(2)}) collective-permute-start(bf16[8,4,16,128]{3,2,1,0:T(8,128)(2,1)S(1)} %bitcast.125), channel_id=1, source_target_pairs={{0,24},{4,28},{8,16},{12,20},{16,8},{20,12},{24,0},{28,4},{1,25},{... | collective-permute-start | bytes 393224 | tf_op jit(solution)/shard_map/ppermute | solution.py:15
  21.3 1.4 %shard_map.60 = (f32[512,512]{1,0:T(8,128)S(1)}, f32[16,512]{1,0:T(8,128)S(1)}) custom-call(s32[2]{0:T(128)S(1)} %pad_add_fusion.spot_ref, f32[8,4]{1,0:T(8,128)S(1)} %pad_maximum_fusion.4.keep_ref, bf16[512,1024]{1,0:T(8,128)(2,1)S(1)} %get-tuple-element.11.left_ref, bf16[1024,512]{1,0:T(8,128)(2,1)S(1)} %get-tuple-element.12.given_ref, ...), custom_call_target="tpu_custom_call" | custom-call | flops 536870912 | bytes 4194304 | tf_op jit(solution)/shard_map/pallas_call | solution.py:88
  22.8 0.1 multiply_convert_fusion
  23.0 0.1 fusion.9
  23.1 0.6 %collective-permute-start.9 = (f16[136,512]{1,0:T(8,128)(2,1)S(1)}, f16[136,512]{1,0:T(8,128)(2,1)S(1)}, u32[]{:S(2)}, u32[]{:S(2)}) collective-permute-start(f16[136,512]{1,0:T(8,128)(2,1)S(1)} %get-tuple-element.17), channel_id=1, source_target_pairs={{0,16},{4,20},{8,24},{12,28},{16,0},{20,4},{24,8},{28,12},{1,17},{... | collective-permute-start | bytes 417800 | tf_op jit(solution)/shard_map/ppermute | solution.py:15
  23.7 1.7 %collective-permute-start.10 = (f16[136,512]{1,0:T(8,128)(2,1)S(1)}, f16[136,512]{1,0:T(8,128)(2,1)S(1)}, u32[]{:S(2)}, u32[]{:S(2)}) collective-permute-start(f16[136,512]{1,0:T(8,128)(2,1)S(1)} %get-tuple-element.18), channel_id=1, source_target_pairs={{0,24},{4,28},{8,16},{12,20},{16,8},{20,12},{24,0},{28,4},{1,25},{... | collective-permute-start | bytes 417800 | tf_op jit(solution)/shard_map/ppermute | solution.py:15
  25.4 0.0 collective-permute-done.12
  25.4 1.2 %collective-permute-start.8 = (f16[136,512]{1,0:T(8,128)(2,1)S(1)}, f16[136,512]{1,0:T(8,128)(2,1)S(1)}, u32[]{:S(2)}, u32[]{:S(2)}) collective-permute-start(f16[136,512]{1,0:T(8,128)(2,1)S(1)} %get-tuple-element.16), channel_id=1, source_target_pairs={{0,8},{4,12},{8,0},{12,4},{16,24},{20,28},{24,16},{28,20},{1,9},{5... | collective-permute-start | bytes 417800 | tf_op jit(solution)/shard_map/ppermute | solution.py:15
  26.7 0.0 collective-permute-done.13
  26.7 1.0 %collective-permute-done.11 = bf16[8,4,16,128]{3,2,1,0:T(8,128)(2,1)S(1)} collective-permute-done((bf16[8,4,16,128]{3,2,1,0:T(8,128)(2,1)S(1)}, bf16[8,4,16,128]{3,2,1,0:T(8,128)(2,1)S(1)}, u32[]{:S(2)}, u32[]{:S(2)}) %collective-permute-start.11) | collective-permute-done | bytes 131104 | tf_op jit(solution)/shard_map/ppermute | solution.py:15
  27.7 0.1 fusion.13
  27.8 5.4 %collective-permute-done.9 = f16[136,512]{1,0:T(8,128)(2,1)S(1)} collective-permute-done((f16[136,512]{1,0:T(8,128)(2,1)S(1)}, f16[136,512]{1,0:T(8,128)(2,1)S(1)}, u32[]{:S(2)}, u32[]{:S(2)}) %collective-permute-start.9) | collective-permute-done | bytes 139296 | tf_op jit(solution)/shard_map/ppermute | solution.py:15
  33.2 0.0 collective-permute-done.10
  33.3 0.1 fusion
  33.4 0.1 reshape.224
  33.5 0.4 fusion.3
  33.9 0.7 %copy.59 = f32[32,4,4,128]{3,1,2,0:T(4,128)} copy(f32[32,4,4,128]{3,1,0,2:T(4,128)S(1)} %bitcast.122) | data formatting | bytes 524288 | tf_op jit(solution)/shard_map/reshape | solution.py:197
  34.6 4.7 %all-to-all-start = ((f32[32,4,4,128]{3,1,2,0:T(4,128)}), f32[32,4,4,128]{3,1,2,0:T(4,128)S(1)}, u32[]{:S(2)}, u32[]{:S(2)}) async-start(f32[32,4,4,128]{3,1,2,0:T(4,128)} %copy.59), calls=%async_computation | async-start | bytes 524288 | tf_op jit(solution)/shard_map/all_to_all | solution.py:198
  39.3 0.8 %fusion.4 = f32[8,4,16,128]{3,2,1,0:T(8,128)} fusion(f32[8,16,4,128]{3,2,1,0:T(4,128)S(1)} %reshape.224, f32[8,4]{1,0:T(8,128)S(1)} %copy.46), kind=kLoop, calls=%fused_computation.16 | loop fusion | flops 65536 | bytes 524416 | tf_op jit(solution)/shard_map/transpose | solution.py:204
  40.1 9.4 %all-to-all-done = f32[32,4,4,128]{3,1,2,0:T(4,128)S(1)} async-done(((f32[32,4,4,128]{3,1,2,0:T(4,128)}), f32[32,4,4,128]{3,1,2,0:T(4,128)S(1)}, u32[]{:S(2)}, u32[]{:S(2)}) %all-to-all-start) | async-done | bytes 262176 | tf_op jit(solution)/shard_map/all_to_all | solution.py:198
  49.5 0.1 reduce_sum.19
  49.6 0.6 %bitcast_subtract_fusion = f32[4,512]{1,0:T(4,128)} fusion(f32[4,512]{1,0:T(4,128)S(1)} %copy-done.2, f32[1,4,4,128]{3,2,1,0:T(4,128)S(1)} %bitcast.126), kind=kLoop, calls=%fused_computation.52 | loop fusion | flops 2048 | bytes 24576 | tf_op jit(solution)/shard_map/sub | solution.py:204
  (32 shorter events, 0.3 us)
Async XLA Ops:
  0.6 10.7 %collective-permute-start = (bf16[4,4,32,128]{3,2,1,0:T(8,128)(2,1)}, bf16[4,4,32,128]{3,2,1,0:T(8,128)(2,1)S(1)}, u32[]{:S(2)}, u32[]{:S(2)}) collective-permute-start(bf16[4,4,32,128]{3,2,1,0:T(8,128)(2,1)} %refs_0_.1), channel_id=1, source_target_pairs={{0,2},{1,3},{2,0},{3,1},{4,6},{5,7},{6,4},{7,5},{8,10},{9,11},{10,... | collective-permute-start | bytes 393224 | tf_op jit(solution)/shard_map/ppermute | solution.py:15
  4.7 7.5 %collective-permute-start.3 = (bf16[4,4,32,128]{3,2,1,0:T(8,128)(2,1)}, bf16[4,4,32,128]{3,2,1,0:T(8,128)(2,1)S(1)}, u32[]{:S(2)}, u32[]{:S(2)}) collective-permute-start(bf16[4,4,32,128]{3,2,1,0:T(8,128)(2,1)} %refs_0_.1), channel_id=1, source_target_pairs={{0,1},{1,0},{2,3},{3,2},{4,5},{5,4},{6,7},{7,6},{8,9},{9,8},{10,11... | collective-permute-start | bytes 393224 | tf_op jit(solution)/shard_map/ppermute | solution.py:15
  6.3 5.1 %collective-permute-start.4 = (bf16[4,4,32,128]{3,2,1,0:T(8,128)(2,1)}, bf16[4,4,32,128]{3,2,1,0:T(8,128)(2,1)S(1)}, u32[]{:S(2)}, u32[]{:S(2)}) collective-permute-start(bf16[4,4,32,128]{3,2,1,0:T(8,128)(2,1)} %refs_0_.1), channel_id=1, source_target_pairs={{0,4},{4,0},{8,12},{12,8},{16,20},{20,16},{24,28},{28,24},{1,5},{5... | collective-permute-start | bytes 393224 | tf_op jit(solution)/shard_map/ppermute | solution.py:15
  6.3 1.8 %copy-start.3 = (s32[4,16]{1,0:T(4,128)S(1)}, s32[4,16]{1,0:T(4,128)}, u32[]{:S(2)}) copy-start(s32[4,16]{1,0:T(4,128)} %param.6) | copy-start | bytes 772
  6.3 8.1 %copy-start = (bf16[8,4,128,128]{3,2,1,0:T(8,128)(2,1)S(1)}, bf16[8,4,128,128]{3,2,1,0:T(8,128)(2,1)}, u32[]{:S(2)}) copy-start(bf16[8,4,128,128]{3,2,1,0:T(8,128)(2,1)} %inv_ref.1) | copy-start | bytes 3145732
  7.5 3.9 %copy-start.1 = (bf16[4,4,32,128]{3,2,1,0:T(8,128)(2,1)S(1)}, bf16[4,4,32,128]{3,2,1,0:T(8,128)(2,1)}, u32[]{:S(2)}) copy-start(bf16[4,4,32,128]{3,2,1,0:T(8,128)(2,1)} %refs_0_.1) | copy-start | bytes 393220
  7.5 6.9 %collective-permute-start.2 = (bf16[8,4,4,16,128]{4,3,2,1,0:T(8,128)(2,1)S(1)}, bf16[8,4,4,16,128]{4,3,2,1,0:T(8,128)(2,1)S(1)}, u32[]{:S(2)}, u32[]{:S(2)}) collective-permute-start(bf16[8,4,4,16,128]{4,3,2,1,0:T(8,128)(2,1)S(1)} %dynamic-slice_bitcast_fusion), channel_id=1, source_target_pairs={{0,4},{4,0},{8,12},{12,8},{16,20},{20,16},{24,28},{28,24},{1,5},{5... | collective-permute-start | bytes 1572872 | tf_op jit(solution)/shard_map/ppermute | solution.py:15
  11.4 1.3 %collective-permute-start.6 = (bf16[4,4,32,128]{3,2,1,0:T(8,128)(2,1)S(1)}, bf16[4,4,32,128]{3,2,1,0:T(8,128)(2,1)S(1)}, u32[]{:S(2)}, u32[]{:S(2)}) collective-permute-start(bf16[4,4,32,128]{3,2,1,0:T(8,128)(2,1)S(1)} %collective-permute-done.refs_2_), channel_id=1, source_target_pairs={{0,4},{4,0},{8,12},{12,8},{16,20},{20,16},{24,28},{28,24},{1,5},{5... | collective-permute-start | bytes 393224 | tf_op jit(solution)/shard_map/ppermute | solution.py:15
  11.4 6.0 %collective-permute-start.1 = (bf16[4,4,32,128]{3,2,1,0:T(8,128)(2,1)S(1)}, bf16[4,4,32,128]{3,2,1,0:T(8,128)(2,1)S(1)}, u32[]{:S(2)}, u32[]{:S(2)}) collective-permute-start(bf16[4,4,32,128]{3,2,1,0:T(8,128)(2,1)S(1)} %collective-permute-done.refs_2_), channel_id=1, source_target_pairs={{0,1},{1,0},{2,3},{3,2},{4,5},{5,4},{6,7},{7,6},{8,9},{9,8},{10,11... | collective-permute-start | bytes 393224 | tf_op jit(solution)/shard_map/ppermute | solution.py:15
  12.2 2.2 %collective-permute-start.5 = (bf16[4,4,32,128]{3,2,1,0:T(8,128)(2,1)S(1)}, bf16[4,4,32,128]{3,2,1,0:T(8,128)(2,1)S(1)}, u32[]{:S(2)}, u32[]{:S(2)}) collective-permute-start(bf16[4,4,32,128]{3,2,1,0:T(8,128)(2,1)S(1)} %collective-permute-done.3.refs_1_), channel_id=1, source_target_pairs={{0,4},{4,0},{8,12},{12,8},{16,20},{20,16},{24,28},{28,24},{1,5},{5... | collective-permute-start | bytes 393224 | tf_op jit(solution)/shard_map/ppermute | solution.py:15
  12.7 12.7 %collective-permute-start.12 = (bf16[8,4,16,128]{3,2,1,0:T(8,128)(2,1)S(1)}, bf16[8,4,16,128]{3,2,1,0:T(8,128)(2,1)S(1)}, u32[]{:S(2)}, u32[]{:S(2)}) collective-permute-start(bf16[8,4,16,128]{3,2,1,0:T(8,128)(2,1)S(1)} %bitcast.123), channel_id=1, source_target_pairs={{0,16},{4,20},{8,24},{12,28},{16,0},{20,4},{24,8},{28,12},{1,17},{... | collective-permute-start | bytes 393224 | tf_op jit(solution)/shard_map/ppermute | solution.py:15
  17.4 1.6 %collective-permute-start.7 = (bf16[4,4,32,128]{3,2,1,0:T(8,128)(2,1)S(1)}, bf16[4,4,32,128]{3,2,1,0:T(8,128)(2,1)S(1)}, u32[]{:S(2)}, u32[]{:S(2)}) collective-permute-start(bf16[4,4,32,128]{3,2,1,0:T(8,128)(2,1)S(1)} %collective-permute-done.1.own_ref), channel_id=1, source_target_pairs={{0,4},{4,0},{8,12},{12,8},{16,20},{20,16},{24,28},{28,24},{1,5},{5... | collective-permute-start | bytes 393224 | tf_op jit(solution)/shard_map/ppermute | solution.py:15
  17.4 9.3 %collective-permute-start.13 = (bf16[8,4,16,128]{3,2,1,0:T(8,128)(2,1)S(1)}, bf16[8,4,16,128]{3,2,1,0:T(8,128)(2,1)S(1)}, u32[]{:S(2)}, u32[]{:S(2)}) collective-permute-start(bf16[8,4,16,128]{3,2,1,0:T(8,128)(2,1)S(1)} %bitcast.124), channel_id=1, source_target_pairs={{0,8},{4,12},{8,0},{12,4},{16,24},{20,28},{24,16},{28,20},{1,9},{5... | collective-permute-start | bytes 393224 | tf_op jit(solution)/shard_map/ppermute | solution.py:15
  19.1 8.6 %collective-permute-start.11 = (bf16[8,4,16,128]{3,2,1,0:T(8,128)(2,1)S(1)}, bf16[8,4,16,128]{3,2,1,0:T(8,128)(2,1)S(1)}, u32[]{:S(2)}, u32[]{:S(2)}) collective-permute-start(bf16[8,4,16,128]{3,2,1,0:T(8,128)(2,1)S(1)} %bitcast.125), channel_id=1, source_target_pairs={{0,24},{4,28},{8,16},{12,20},{16,8},{20,12},{24,0},{28,4},{1,25},{... | collective-permute-start | bytes 393224 | tf_op jit(solution)/shard_map/ppermute | solution.py:15
  23.1 10.1 %collective-permute-start.9 = (f16[136,512]{1,0:T(8,128)(2,1)S(1)}, f16[136,512]{1,0:T(8,128)(2,1)S(1)}, u32[]{:S(2)}, u32[]{:S(2)}) collective-permute-start(f16[136,512]{1,0:T(8,128)(2,1)S(1)} %get-tuple-element.17), channel_id=1, source_target_pairs={{0,16},{4,20},{8,24},{12,28},{16,0},{20,4},{24,8},{28,12},{1,17},{... | collective-permute-start | bytes 417800 | tf_op jit(solution)/shard_map/ppermute | solution.py:15
  23.7 9.5 %collective-permute-start.10 = (f16[136,512]{1,0:T(8,128)(2,1)S(1)}, f16[136,512]{1,0:T(8,128)(2,1)S(1)}, u32[]{:S(2)}, u32[]{:S(2)}) collective-permute-start(f16[136,512]{1,0:T(8,128)(2,1)S(1)} %get-tuple-element.18), channel_id=1, source_target_pairs={{0,24},{4,28},{8,16},{12,20},{16,8},{20,12},{24,0},{28,4},{1,25},{... | collective-permute-start | bytes 417800 | tf_op jit(solution)/shard_map/ppermute | solution.py:15
  25.4 7.8 %collective-permute-start.8 = (f16[136,512]{1,0:T(8,128)(2,1)S(1)}, f16[136,512]{1,0:T(8,128)(2,1)S(1)}, u32[]{:S(2)}, u32[]{:S(2)}) collective-permute-start(f16[136,512]{1,0:T(8,128)(2,1)S(1)} %get-tuple-element.16), channel_id=1, source_target_pairs={{0,8},{4,12},{8,0},{12,4},{16,24},{20,28},{24,16},{28,20},{1,9},{5... | collective-permute-start | bytes 417800 | tf_op jit(solution)/shard_map/ppermute | solution.py:15
  34.6 14.9 %all-to-all-start = ((f32[32,4,4,128]{3,1,2,0:T(4,128)}), f32[32,4,4,128]{3,1,2,0:T(4,128)S(1)}, u32[]{:S(2)}, u32[]{:S(2)}) async-start(f32[32,4,4,128]{3,1,2,0:T(4,128)} %copy.59), calls=%async_computation | async-start | bytes 524288 | tf_op jit(solution)/shard_map/all_to_all | solution.py:198
  40.1 9.5 %copy-start.2 = (f32[4,512]{1,0:T(4,128)S(1)}, f32[4,512]{1,0:T(4,128)}, u32[]{:S(2)}) copy-start(f32[4,512]{1,0:T(4,128)} %param.7) | copy-start | bytes 24580

commit v6 on v5

--- a/solution.py
+++ b/solution.py
@@ -97,6 +97,36 @@
         compiler_params=pltpu.CompilerParams(vmem_limit_bytes=24 << 20),
         cost_estimate=pl.CostEstimate(flops=2 * height * depth * across, bytes_accessed=4 << 20, transcendentals=0),
     )(spot, keep, left, right, own_piece, met_piece)
+
+
+def diag_kernel(share, own_ref, sums_ref, out_ref, made_ref):
+    node_count, width = own_ref.shape[1], own_ref.shape[3]
+    for k in range(node_count):
+        left = own_ref[:, k].reshape(sums_ref.shape[0], width)
+        sums = sums_ref[:, pl.ds(k * width, width)]
+        high = sums.astype(jnp.bfloat16)
+        low = (sums - high.astype(jnp.float32)).astype(jnp.bfloat16)
+        made = 0.0
+        for part in (high, low):
+            made = made + lax.dot_general(left, part, (((0,), (0,)), ((), ())), preferred_element_type=jnp.float32)
+        made_ref[...] = made
+        for at in range(width // share):
+            out_ref[at, pl.ds(k, share, node_count), :] = made_ref[pl.ds(at * share, share), :]
+
+
+def diag_pieces(own, sums, count):
+    _, node_count, _, width = own.shape
+    share = width // count
+    in_vmem = pl.BlockSpec(memory_space=pltpu.VMEM)
+    return pl.pallas_call(
+        functools.partial(diag_kernel, share),
+        out_shape=jax.ShapeDtypeStruct((count, node_count * share, width), jnp.float32),
+        in_specs=[in_vmem, in_vmem],
+        out_specs=in_vmem,
+        scratch_shapes=[pltpu.VMEM((width, width), jnp.float32)],
+        compiler_params=pltpu.CompilerParams(vmem_limit_bytes=24 << 20),
+        cost_estimate=pl.CostEstimate(flops=4 * sums.size * width, bytes_accessed=1 << 20, transcendentals=0),
+    )(own, sums)
 
 
 def plain_sums(pcol, keep, inv, met, own_pieces, met_pieces, core, chips, rows):
@@ -192,11 +222,13 @@
 
     count = row_groups * col_groups
     wide = own.astype(jnp.float32)
-    if width % count == 0:
-        update = jnp.einsum("ikra,irkb->akb", wide, column, precision=lax.Precision.HIGHEST)
-        update = update.reshape(count, width // count, node_count, width)
+    if fits and width % count == 0:
+        flipped = -diag_inverse
+        summed_held, flipped = tied(summed, flipped)
+        update = diag_pieces(own, summed_held, count)
         update = jnp.sum(lax.all_to_all(update, ("prow", "pcol"), 0, 0, tiled=True), axis=0)
-        update = jnp.transpose(update, (1, 0, 2)).reshape(diag_inverse.shape)
+        update = jnp.transpose(update.reshape(width // count, node_count, width), (1, 0, 2))
+        return jnp.transpose(column, (0, 2, 1, 3)), update.reshape(diag_inverse.shape) - flipped
     else:
         update = jnp.einsum("ikra,irkb->kab", wide, column, precision=lax.Precision.HIGHEST)
         update = update.reshape(node_count, count, width * width // count)

time: 50.4 us -> 50.2 us (level)
  Pallas kernels: 2.43 us -> 3.42 us
  local copies, waits for them, and re-layouts: 2.54 us -> 1.81 us
    pallas_call x0 -> x1, Pallas kernels: none -> 0.98 us  [diag_pieces(): pl.pallas_call(functools.partial(diag_kernel, share), out_shape=jax.Shape...]
    reshape x1 -> x0, local copies, waits for them, and re-layouts: 0.74 us -> none  [per_device(): update = update.reshape(count, width // count, node_count, width)]
where the time goes in v6:
time: 50.2 us; the launch traced here: 50 us
  starting transfers between devices  21 us (42%)
  waiting for transfers between devices  20.5 us (41%)
  Pallas kernels  3.42 us (7%)
  other arithmetic  2.42 us (5%)
  local copies, waits for them, and re-layouts  1.81 us (4%)
  between operations  0.87 us (2%)
    ppermute x14, starting transfers between devices, swap(): return lax.ppermute(value, axis, [(at, at ^ step) for at in range(size)])  16.3 us
    ppermute x14, waiting for transfers between devices, swap(): return lax.ppermute(value, axis, [(at, at ^ step) for at in range(size)])  11.4 us
    all_to_all x1, waiting for transfers between devices, per_device(): lax.all_to_all(update, ('prow', 'pcol'), 0, 0, tiled=True)  9.13 us
    all_to_all x1, starting transfers between devices, per_device(): lax.all_to_all(update, ('prow', 'pcol'), 0, 0, tiled=True)  4.68 us
    pallas_call x1, Pallas kernels, chip_sums(): pl.pallas_call(functools.partial(sums_kernel, last), out_shape=(jax.Shape...  1.44 us
    squeeze x1, local copies, waits for them, and re-layouts, take(): return lax.dynamic_index_in_dim(value, index, axis, keepdims=False)  1.17 us
  transfers between devices with their start and end apart: 15, of which 6 were waited for; matrix products, arithmetic and copies ran while one was open for 7% of the time, Pallas kernels for 5%

profile of v6, /device:TPU:0, one launch (start us, length us, event | category | flops | bytes accessed | tf_op | source)
XLA Modules:
  0.0 50.0 jit_solution(3239095716878081905)
XLA Ops:
  0.6 4.1 %collective-permute-start = (bf16[4,4,32,128]{3,2,1,0:T(8,128)(2,1)}, bf16[4,4,32,128]{3,2,1,0:T(8,128)(2,1)S(1)}, u32[]{:S(2)}, u32[]{:S(2)}) collective-permute-start(bf16[4,4,32,128]{3,2,1,0:T(8,128)(2,1)} %refs_0_.1), channel_id=1, source_target_pairs={{0,2},{1,3},{2,0},{3,1},{4,6},{5,7},{6,4},{7,5},{8,10},{9,11},{10,... | collective-permute-start | bytes 393224 | tf_op jit(solution)/shard_map/ppermute | solution.py:15
  4.7 1.6 %collective-permute-start.3 = (bf16[4,4,32,128]{3,2,1,0:T(8,128)(2,1)}, bf16[4,4,32,128]{3,2,1,0:T(8,128)(2,1)S(1)}, u32[]{:S(2)}, u32[]{:S(2)}) collective-permute-start(bf16[4,4,32,128]{3,2,1,0:T(8,128)(2,1)} %refs_0_.1), channel_id=1, source_target_pairs={{0,1},{1,0},{2,3},{3,2},{4,5},{5,4},{6,7},{7,6},{8,9},{9,8},{10,11... | collective-permute-start | bytes 393224 | tf_op jit(solution)/shard_map/ppermute | solution.py:15
  6.3 0.0 collective-permute-start.4
  6.3 1.2 %dynamic-slice_bitcast_fusion = bf16[8,4,4,16,128]{4,3,2,1,0:T(8,128)(2,1)S(1)} fusion(bf16[8,4,4,2,16,128]{5,4,3,2,1,0:T(8,128)(2,1)} %bitcast.102, s32[]{:T(128)S(6)} %select_n.188), kind=kLoop, calls=%fused_computation.4 | loop fusion | bytes 1048580 | tf_op jit(solution)/shard_map/jit(dynamic_index_in_dim)/squeeze | solution.py:19
  7.5 0.0 copy-start.1
  7.5 0.6 %collective-permute-start.2 = (bf16[8,4,4,16,128]{4,3,2,1,0:T(8,128)(2,1)S(1)}, bf16[8,4,4,16,128]{4,3,2,1,0:T(8,128)(2,1)S(1)}, u32[]{:S(2)}, u32[]{:S(2)}) collective-permute-start(bf16[8,4,4,16,128]{4,3,2,1,0:T(8,128)(2,1)S(1)} %dynamic-slice_bitcast_fusion), channel_id=1, source_target_pairs={{0,4},{4,0},{8,12},{12,8},{16,20},{20,16},{24,28},{28,24},{1,5},{5... | collective-permute-start | bytes 1572872 | tf_op jit(solution)/shard_map/ppermute | solution.py:15
  8.1 0.1 convert_reduce_fusion
  8.2 0.1 constant_dynamic-slice_fusion.2
  8.2 0.1 copy.40
  8.3 0.1 copy.41
  8.4 0.1 fusion.29
  8.5 0.1 pad_add_fusion.spot_ref
  8.6 0.1 copy.39
  8.7 2.7 %collective-permute-done.refs_2_ = bf16[4,4,32,128]{3,2,1,0:T(8,128)(2,1)S(1)} collective-permute-done((bf16[4,4,32,128]{3,2,1,0:T(8,128)(2,1)}, bf16[4,4,32,128]{3,2,1,0:T(8,128)(2,1)S(1)}, u32[]{:S(2)}, u32[]{:S(2)}) %collective-permute-start) | collective-permute-done | bytes 131104 | tf_op jit(solution)/shard_map/ppermute | solution.py:15
  11.4 0.0 collective-permute-start.6
  11.4 0.0 collective-permute-done.4.refs_3_
  11.4 0.8 %collective-permute-start.1 = (bf16[4,4,32,128]{3,2,1,0:T(8,128)(2,1)S(1)}, bf16[4,4,32,128]{3,2,1,0:T(8,128)(2,1)S(1)}, u32[]{:S(2)}, u32[]{:S(2)}) collective-permute-start(bf16[4,4,32,128]{3,2,1,0:T(8,128)(2,1)S(1)} %collective-permute-done.refs_2_), channel_id=1, source_target_pairs={{0,1},{1,0},{2,3},{3,2},{4,5},{5,4},{6,7},{7,6},{8,9},{9,8},{10,11... | collective-permute-start | bytes 393224 | tf_op jit(solution)/shard_map/ppermute | solution.py:15
  12.2 0.0 collective-permute-done.3.refs_1_
  12.2 0.2 collective-permute-start.5
  12.4 0.3 collective-permute-done.6.refs_5_
  12.7 1.6 %collective-permute-start.12 = (bf16[8,4,16,128]{3,2,1,0:T(8,128)(2,1)S(1)}, bf16[8,4,16,128]{3,2,1,0:T(8,128)(2,1)S(1)}, u32[]{:S(2)}, u32[]{:S(2)}) collective-permute-start(bf16[8,4,16,128]{3,2,1,0:T(8,128)(2,1)S(1)} %bitcast.113), channel_id=1, source_target_pairs={{0,16},{4,20},{8,24},{12,28},{16,0},{20,4},{24,8},{28,12},{1,17},{... | collective-permute-start | bytes 393224 | tf_op jit(solution)/shard_map/ppermute | solution.py:15
  14.4 0.0 collective-permute-done.5.refs_4_
  14.4 0.0 collective-permute-done.2.met_ref
  14.4 1.0 %shard_map.59 = (bf16[512,1024]{1,0:T(8,128)(2,1)S(1)}, bf16[1024,512]{1,0:T(8,128)(2,1)S(1)}) custom-call(s32[2]{0:T(128)S(1)} %pad_add_fusion.spot_ref, f32[8,4]{1,0:T(8,128)S(1)} %pad_maximum_fusion.4.keep_ref, bf16[8,4,128,128]{3,2,1,0:T(8,128)(2,1)S(1)} %copy-done, bf16[8,4,4,16,128]{4,3,2,1,0:T(8,128)(2,1)S(1)} %collective-permute-done.2.met_ref, ...), custom_call_target="tpu_custom_call" | custom-call | bytes 4194304 | tf_op jit(solution)/shard_map/pallas_call | solution.py:71
  15.4 2.0 %collective-permute-done.1.own_ref = bf16[4,4,32,128]{3,2,1,0:T(8,128)(2,1)S(1)} collective-permute-done((bf16[4,4,32,128]{3,2,1,0:T(8,128)(2,1)S(1)}, bf16[4,4,32,128]{3,2,1,0:T(8,128)(2,1)S(1)}, u32[]{:S(2)}, u32[]{:S(2)}) %collective-permute-start.1) | collective-permute-done | bytes 131104 | tf_op jit(solution)/shard_map/ppermute | solution.py:15
  17.4 0.0 collective-permute-start.7
  17.4 1.6 %collective-permute-start.13 = (bf16[8,4,16,128]{3,2,1,0:T(8,128)(2,1)S(1)}, bf16[8,4,16,128]{3,2,1,0:T(8,128)(2,1)S(1)}, u32[]{:S(2)}, u32[]{:S(2)}) collective-permute-start(bf16[8,4,16,128]{3,2,1,0:T(8,128)(2,1)S(1)} %bitcast.114), channel_id=1, source_target_pairs={{0,8},{4,12},{8,0},{12,4},{16,24},{20,28},{24,16},{28,20},{1,9},{5... | collective-permute-start | bytes 393224 | tf_op jit(solution)/shard_map/ppermute | solution.py:15
  19.1 2.3 %collective-permute-start.11 = (bf16[8,4,16,128]{3,2,1,0:T(8,128)(2,1)S(1)}, bf16[8,4,16,128]{3,2,1,0:T(8,128)(2,1)S(1)}, u32[]{:S(2)}, u32[]{:S(2)}) collective-permute-start(bf16[8,4,16,128]{3,2,1,0:T(8,128)(2,1)S(1)} %bitcast.115), channel_id=1, source_target_pairs={{0,24},{4,28},{8,16},{12,20},{16,8},{20,12},{24,0},{28,4},{1,25},{... | collective-permute-start | bytes 393224 | tf_op jit(solution)/shard_map/ppermute | solution.py:15
  21.3 1.4 %shard_map.60 = (f32[512,512]{1,0:T(8,128)S(1)}, f32[16,512]{1,0:T(8,128)S(1)}) custom-call(s32[2]{0:T(128)S(1)} %pad_add_fusion.spot_ref, f32[8,4]{1,0:T(8,128)S(1)} %pad_maximum_fusion.4.keep_ref, bf16[512,1024]{1,0:T(8,128)(2,1)S(1)} %get-tuple-element.13.left_ref, bf16[1024,512]{1,0:T(8,128)(2,1)S(1)} %get-tuple-element.14.given_ref, ...), custom_call_target="tpu_custom_call" | custom-call | flops 536870912 | bytes 4194304 | tf_op jit(solution)/shard_map/pallas_call | solution.py:88
  22.8 0.1 multiply_convert_fusion
  23.0 0.1 fusion.8
  23.1 0.6 %collective-permute-start.9 = (f16[136,512]{1,0:T(8,128)(2,1)S(1)}, f16[136,512]{1,0:T(8,128)(2,1)S(1)}, u32[]{:S(2)}, u32[]{:S(2)}) collective-permute-start(f16[136,512]{1,0:T(8,128)(2,1)S(1)} %get-tuple-element.21), channel_id=1, source_target_pairs={{0,16},{4,20},{8,24},{12,28},{16,0},{20,4},{24,8},{28,12},{1,17},{... | collective-permute-start | bytes 417800 | tf_op jit(solution)/shard_map/ppermute | solution.py:15
  23.7 1.7 %collective-permute-start.10 = (f16[136,512]{1,0:T(8,128)(2,1)S(1)}, f16[136,512]{1,0:T(8,128)(2,1)S(1)}, u32[]{:S(2)}, u32[]{:S(2)}) collective-permute-start(f16[136,512]{1,0:T(8,128)(2,1)S(1)} %get-tuple-element.22), channel_id=1, source_target_pairs={{0,24},{4,28},{8,16},{12,20},{16,8},{20,12},{24,0},{28,4},{1,25},{... | collective-permute-start | bytes 417800 | tf_op jit(solution)/shard_map/ppermute | solution.py:15
  25.4 1.2 %collective-permute-start.8 = (f16[136,512]{1,0:T(8,128)(2,1)S(1)}, f16[136,512]{1,0:T(8,128)(2,1)S(1)}, u32[]{:S(2)}, u32[]{:S(2)}) collective-permute-start(f16[136,512]{1,0:T(8,128)(2,1)S(1)} %get-tuple-element.20), channel_id=1, source_target_pairs={{0,8},{4,12},{8,0},{12,4},{16,24},{20,28},{24,16},{28,20},{1,9},{5... | collective-permute-start | bytes 417800 | tf_op jit(solution)/shard_map/ppermute | solution.py:15
  26.6 0.0 collective-permute-done.13
  26.6 1.0 %collective-permute-done.11 = bf16[8,4,16,128]{3,2,1,0:T(8,128)(2,1)S(1)} collective-permute-done((bf16[8,4,16,128]{3,2,1,0:T(8,128)(2,1)S(1)}, bf16[8,4,16,128]{3,2,1,0:T(8,128)(2,1)S(1)}, u32[]{:S(2)}, u32[]{:S(2)}) %collective-permute-start.11) | collective-permute-done | bytes 131104 | tf_op jit(solution)/shard_map/ppermute | solution.py:15
  27.7 0.1 fusion.12.own_ref
  27.8 5.4 %collective-permute-done.9 = f16[136,512]{1,0:T(8,128)(2,1)S(1)} collective-permute-done((f16[136,512]{1,0:T(8,128)(2,1)S(1)}, f16[136,512]{1,0:T(8,128)(2,1)S(1)}, u32[]{:S(2)}, u32[]{:S(2)}) %collective-permute-start.9) | collective-permute-done | bytes 139296 | tf_op jit(solution)/shard_map/ppermute | solution.py:15
  33.2 0.0 collective-permute-done.10
  33.3 0.1 fusion.sums_ref
  33.4 1.0 %shard_map.61 = f32[32,16,128]{2,1,0:T(8,128)} custom-call(bf16[8,4,16,128]{3,2,1,0:T(8,128)(2,1)S(1)} %fusion.12.own_ref, f32[128,512]{1,0:T(8,128)S(1)} %fusion.sums_ref), custom_call_target="tpu_custom_call" | custom-call | flops 33554432 | bytes 1048576 | tf_op jit(solution)/shard_map/pallas_call | solution.py:121
  34.4 4.7 %all-to-all-start = ((f32[32,16,128]{2,1,0:T(8,128)}), f32[32,16,128]{2,1,0:T(8,128)S(1)}, u32[]{:S(2)}, u32[]{:S(2)}) async-start(f32[32,16,128]{2,1,0:T(8,128)} %shard_map.61), calls=%async_computation | async-start | bytes 524288 | tf_op jit(solution)/shard_map/all_to_all | solution.py:229
  39.1 0.1 fusion.30
  39.2 0.1 copy.29
  39.3 0.1 reshape.224
  39.4 0.8 %fusion.3 = f32[8,4,16,128]{3,2,1,0:T(8,128)} fusion(f32[8,16,4,128]{3,2,1,0:T(4,128)S(1)} %reshape.224, f32[8,4]{1,0:T(8,128)S(1)} %copy.29), kind=kLoop, calls=%fused_computation.15 | loop fusion | flops 65536 | bytes 524416 | tf_op jit(solution)/shard_map/transpose | solution.py:231
  40.2 9.1 %all-to-all-done = f32[32,16,128]{2,1,0:T(8,128)S(1)} async-done(((f32[32,16,128]{2,1,0:T(8,128)}), f32[32,16,128]{2,1,0:T(8,128)S(1)}, u32[]{:S(2)}, u32[]{:S(2)}) %all-to-all-start) | async-done | bytes 262176 | tf_op jit(solution)/shard_map/all_to_all | solution.py:229
  49.4 0.6 %sub.33 = f32[4,512]{1,0:T(4,128)} subtract(f32[4,512]{1,0:T(4,128)S(1)} %bitcast.116, f32[4,512]{1,0:T(4,128)S(1)} %neg.7) | non-fusion elementwise | flops 2048 | bytes 24576 | tf_op jit(solution)/shard_map/sub | solution.py:231
  (31 shorter events, 0.3 us)
Async XLA Ops:
  0.6 10.7 %collective-permute-start = (bf16[4,4,32,128]{3,2,1,0:T(8,128)(2,1)}, bf16[4,4,32,128]{3,2,1,0:T(8,128)(2,1)S(1)}, u32[]{:S(2)}, u32[]{:S(2)}) collective-permute-start(bf16[4,4,32,128]{3,2,1,0:T(8,128)(2,1)} %refs_0_.1), channel_id=1, source_target_pairs={{0,2},{1,3},{2,0},{3,1},{4,6},{5,7},{6,4},{7,5},{8,10},{9,11},{10,... | collective-permute-start | bytes 393224 | tf_op jit(solution)/shard_map/ppermute | solution.py:15
  4.7 7.5 %collective-permute-start.3 = (bf16[4,4,32,128]{3,2,1,0:T(8,128)(2,1)}, bf16[4,4,32,128]{3,2,1,0:T(8,128)(2,1)S(1)}, u32[]{:S(2)}, u32[]{:S(2)}) collective-permute-start(bf16[4,4,32,128]{3,2,1,0:T(8,128)(2,1)} %refs_0_.1), channel_id=1, source_target_pairs={{0,1},{1,0},{2,3},{3,2},{4,5},{5,4},{6,7},{7,6},{8,9},{9,8},{10,11... | collective-permute-start | bytes 393224 | tf_op jit(solution)/shard_map/ppermute | solution.py:15
  6.3 5.1 %collective-permute-start.4 = (bf16[4,4,32,128]{3,2,1,0:T(8,128)(2,1)}, bf16[4,4,32,128]{3,2,1,0:T(8,128)(2,1)S(1)}, u32[]{:S(2)}, u32[]{:S(2)}) collective-permute-start(bf16[4,4,32,128]{3,2,1,0:T(8,128)(2,1)} %refs_0_.1), channel_id=1, source_target_pairs={{0,4},{4,0},{8,12},{12,8},{16,20},{20,16},{24,28},{28,24},{1,5},{5... | collective-permute-start | bytes 393224 | tf_op jit(solution)/shard_map/ppermute | solution.py:15
  6.3 1.8 %copy-start.3 = (s32[4,16]{1,0:T(4,128)S(1)}, s32[4,16]{1,0:T(4,128)}, u32[]{:S(2)}) copy-start(s32[4,16]{1,0:T(4,128)} %param.6) | copy-start | bytes 772
  6.3 2.4 %copy-start.2 = (f32[4,512]{1,0:T(4,128)S(1)}, f32[4,512]{1,0:T(4,128)}, u32[]{:S(2)}) copy-start(f32[4,512]{1,0:T(4,128)} %param.7) | copy-start | bytes 24580
  6.3 8.1 %copy-start = (bf16[8,4,128,128]{3,2,1,0:T(8,128)(2,1)S(1)}, bf16[8,4,128,128]{3,2,1,0:T(8,128)(2,1)}, u32[]{:S(2)}) copy-start(bf16[8,4,128,128]{3,2,1,0:T(8,128)(2,1)} %inv_ref.1) | copy-start | bytes 3145732
  7.5 3.9 %copy-start.1 = (bf16[4,4,32,128]{3,2,1,0:T(8,128)(2,1)S(1)}, bf16[4,4,32,128]{3,2,1,0:T(8,128)(2,1)}, u32[]{:S(2)}) copy-start(bf16[4,4,32,128]{3,2,1,0:T(8,128)(2,1)} %refs_0_.1) | copy-start | bytes 393220
  7.5 6.9 %collective-permute-start.2 = (bf16[8,4,4,16,128]{4,3,2,1,0:T(8,128)(2,1)S(1)}, bf16[8,4,4,16,128]{4,3,2,1,0:T(8,128)(2,1)S(1)}, u32[]{:S(2)}, u32[]{:S(2)}) collective-permute-start(bf16[8,4,4,16,128]{4,3,2,1,0:T(8,128)(2,1)S(1)} %dynamic-slice_bitcast_fusion), channel_id=1, source_target_pairs={{0,4},{4,0},{8,12},{12,8},{16,20},{20,16},{24,28},{28,24},{1,5},{5... | collective-permute-start | bytes 1572872 | tf_op jit(solution)/shard_map/ppermute | solution.py:15
  11.4 1.3 %collective-permute-start.6 = (bf16[4,4,32,128]{3,2,1,0:T(8,128)(2,1)S(1)}, bf16[4,4,32,128]{3,2,1,0:T(8,128)(2,1)S(1)}, u32[]{:S(2)}, u32[]{:S(2)}) collective-permute-start(bf16[4,4,32,128]{3,2,1,0:T(8,128)(2,1)S(1)} %collective-permute-done.refs_2_), channel_id=1, source_target_pairs={{0,4},{4,0},{8,12},{12,8},{16,20},{20,16},{24,28},{28,24},{1,5},{5... | collective-permute-start | bytes 393224 | tf_op jit(solution)/shard_map/ppermute | solution.py:15
  11.4 6.0 %collective-permute-start.1 = (bf16[4,4,32,128]{3,2,1,0:T(8,128)(2,1)S(1)}, bf16[4,4,32,128]{3,2,1,0:T(8,128)(2,1)S(1)}, u32[]{:S(2)}, u32[]{:S(2)}) collective-permute-start(bf16[4,4,32,128]{3,2,1,0:T(8,128)(2,1)S(1)} %collective-permute-done.refs_2_), channel_id=1, source_target_pairs={{0,1},{1,0},{2,3},{3,2},{4,5},{5,4},{6,7},{7,6},{8,9},{9,8},{10,11... | collective-permute-start | bytes 393224 | tf_op jit(solution)/shard_map/ppermute | solution.py:15
  12.2 2.2 %collective-permute-start.5 = (bf16[4,4,32,128]{3,2,1,0:T(8,128)(2,1)S(1)}, bf16[4,4,32,128]{3,2,1,0:T(8,128)(2,1)S(1)}, u32[]{:S(2)}, u32[]{:S(2)}) collective-permute-start(bf16[4,4,32,128]{3,2,1,0:T(8,128)(2,1)S(1)} %collective-permute-done.3.refs_1_), channel_id=1, source_target_pairs={{0,4},{4,0},{8,12},{12,8},{16,20},{20,16},{24,28},{28,24},{1,5},{5... | collective-permute-start | bytes 393224 | tf_op jit(solution)/shard_map/ppermute | solution.py:15
  12.7 12.7 %collective-permute-start.12 = (bf16[8,4,16,128]{3,2,1,0:T(8,128)(2,1)S(1)}, bf16[8,4,16,128]{3,2,1,0:T(8,128)(2,1)S(1)}, u32[]{:S(2)}, u32[]{:S(2)}) collective-permute-start(bf16[8,4,16,128]{3,2,1,0:T(8,128)(2,1)S(1)} %bitcast.113), channel_id=1, source_target_pairs={{0,16},{4,20},{8,24},{12,28},{16,0},{20,4},{24,8},{28,12},{1,17},{... | collective-permute-start | bytes 393224 | tf_op jit(solution)/shard_map/ppermute | solution.py:15
  17.4 1.6 %collective-permute-start.7 = (bf16[4,4,32,128]{3,2,1,0:T(8,128)(2,1)S(1)}, bf16[4,4,32,128]{3,2,1,0:T(8,128)(2,1)S(1)}, u32[]{:S(2)}, u32[]{:S(2)}) collective-permute-start(bf16[4,4,32,128]{3,2,1,0:T(8,128)(2,1)S(1)} %collective-permute-done.1.own_ref), channel_id=1, source_target_pairs={{0,4},{4,0},{8,12},{12,8},{16,20},{20,16},{24,28},{28,24},{1,5},{5... | collective-permute-start | bytes 393224 | tf_op jit(solution)/shard_map/ppermute | solution.py:15
  17.4 9.2 %collective-permute-start.13 = (bf16[8,4,16,128]{3,2,1,0:T(8,128)(2,1)S(1)}, bf16[8,4,16,128]{3,2,1,0:T(8,128)(2,1)S(1)}, u32[]{:S(2)}, u32[]{:S(2)}) collective-permute-start(bf16[8,4,16,128]{3,2,1,0:T(8,128)(2,1)S(1)} %bitcast.114), channel_id=1, source_target_pairs={{0,8},{4,12},{8,0},{12,4},{16,24},{20,28},{24,16},{28,20},{1,9},{5... | collective-permute-start | bytes 393224 | tf_op jit(solution)/shard_map/ppermute | solution.py:15
  19.1 8.6 %collective-permute-start.11 = (bf16[8,4,16,128]{3,2,1,0:T(8,128)(2,1)S(1)}, bf16[8,4,16,128]{3,2,1,0:T(8,128)(2,1)S(1)}, u32[]{:S(2)}, u32[]{:S(2)}) collective-permute-start(bf16[8,4,16,128]{3,2,1,0:T(8,128)(2,1)S(1)} %bitcast.115), channel_id=1, source_target_pairs={{0,24},{4,28},{8,16},{12,20},{16,8},{20,12},{24,0},{28,4},{1,25},{... | collective-permute-start | bytes 393224 | tf_op jit(solution)/shard_map/ppermute | solution.py:15
  23.1 10.1 %collective-permute-start.9 = (f16[136,512]{1,0:T(8,128)(2,1)S(1)}, f16[136,512]{1,0:T(8,128)(2,1)S(1)}, u32[]{:S(2)}, u32[]{:S(2)}) collective-permute-start(f16[136,512]{1,0:T(8,128)(2,1)S(1)} %get-tuple-element.21), channel_id=1, source_target_pairs={{0,16},{4,20},{8,24},{12,28},{16,0},{20,4},{24,8},{28,12},{1,17},{... | collective-permute-start | bytes 417800 | tf_op jit(solution)/shard_map/ppermute | solution.py:15
  23.7 9.6 %collective-permute-start.10 = (f16[136,512]{1,0:T(8,128)(2,1)S(1)}, f16[136,512]{1,0:T(8,128)(2,1)S(1)}, u32[]{:S(2)}, u32[]{:S(2)}) collective-permute-start(f16[136,512]{1,0:T(8,128)(2,1)S(1)} %get-tuple-element.22), channel_id=1, source_target_pairs={{0,24},{4,28},{8,16},{12,20},{16,8},{20,12},{24,0},{28,4},{1,25},{... | collective-permute-start | bytes 417800 | tf_op jit(solution)/shard_map/ppermute | solution.py:15
  25.4 7.9 %collective-permute-start.8 = (f16[136,512]{1,0:T(8,128)(2,1)S(1)}, f16[136,512]{1,0:T(8,128)(2,1)S(1)}, u32[]{:S(2)}, u32[]{:S(2)}) collective-permute-start(f16[136,512]{1,0:T(8,128)(2,1)S(1)} %get-tuple-element.20), channel_id=1, source_target_pairs={{0,8},{4,12},{8,0},{12,4},{16,24},{20,28},{24,16},{28,20},{1,9},{5... | collective-permute-start | bytes 417800 | tf_op jit(solution)/shard_map/ppermute | solution.py:15
  34.4 14.9 %all-to-all-start = ((f32[32,16,128]{2,1,0:T(8,128)}), f32[32,16,128]{2,1,0:T(8,128)S(1)}, u32[]{:S(2)}, u32[]{:S(2)}) async-start(f32[32,16,128]{2,1,0:T(8,128)} %shard_map.61), calls=%async_computation | async-start | bytes 524288 | tf_op jit(solution)/shard_map/all_to_all | solution.py:229

commit v7 on v6

--- a/solution.py
+++ b/solution.py
@@ -56,10 +56,13 @@
     right_ref[...] = given_ref[...]
     place(right_ref, spot_ref, keep_ref, own_ref, 0, last, blocks_j, width)
     place(right_ref, spot_ref, keep_ref, met_ref, 1, last, blocks_j, width)
-    total = jnp.dot(left_ref[...], right_ref[...], preferred_element_type=jnp.float32)
-    out_ref[...] = total
-    top = jnp.max(jnp.abs(total), axis=0, keepdims=True)
-    top_ref[...] = jnp.broadcast_to(top, top_ref.shape)
+    across = right_ref.shape[1] // 2
+    for at in range(2):
+        lanes = pl.ds(at * across, across)
+        total = jnp.dot(left_ref[...], right_ref[:, lanes], preferred_element_type=jnp.float32)
+        out_ref[:, lanes] = total
+        top = jnp.max(jnp.abs(total), axis=0, keepdims=True)
+        top_ref[:, lanes] = jnp.broadcast_to(top, (top_ref.shape[0], across))
 
 
 def laid_out(spot, keep, inv, met, own_pieces, met_pieces, chips, rows):

time: 50.2 us -> 50.2 us (level)
  no operation moved by 1% of the time
where the time goes in v7:
time: 50.2 us; the launch traced here: 50 us
  starting transfers between devices  21 us (42%)
  waiting for transfers between devices  20.5 us (41%)
  Pallas kernels  3.42 us (7%)
  other arithmetic  2.42 us (5%)
  local copies, waits for them, and re-layouts  1.81 us (4%)
  between operations  0.87 us (2%)
    ppermute x14, starting transfers between devices, swap(): return lax.ppermute(value, axis, [(at, at ^ step) for at in range(size)])  16.3 us
    ppermute x14, waiting for transfers between devices, swap(): return lax.ppermute(value, axis, [(at, at ^ step) for at in range(size)])  11.4 us
    all_to_all x1, waiting for transfers between devices, per_device(): lax.all_to_all(update, ('prow', 'pcol'), 0, 0, tiled=True)  9.13 us
    all_to_all x1, starting transfers between devices, per_device(): lax.all_to_all(update, ('prow', 'pcol'), 0, 0, tiled=True)  4.68 us
    pallas_call x1, Pallas kernels, chip_sums(): pl.pallas_call(functools.partial(sums_kernel, last), out_shape=(jax.Shape...  1.44 us
    squeeze x1, local copies, waits for them, and re-layouts, take(): return lax.dynamic_index_in_dim(value, index, axis, keepdims=False)  1.17 us
  transfers between devices with their start and end apart: 15, of which 6 were waited for; matrix products, arithmetic and copies ran while one was open for 7% of the time, Pallas kernels for 5%

profile of v7, /device:TPU:0, one launch (start us, length us, event | category | flops | bytes accessed | tf_op | source)
XLA Modules:
  0.0 50.0 jit_solution(3239095716878081905)
XLA Ops:
  0.6 4.1 %collective-permute-start = (bf16[4,4,32,128]{3,2,1,0:T(8,128)(2,1)}, bf16[4,4,32,128]{3,2,1,0:T(8,128)(2,1)S(1)}, u32[]{:S(2)}, u32[]{:S(2)}) collective-permute-start(bf16[4,4,32,128]{3,2,1,0:T(8,128)(2,1)} %refs_0_.1), channel_id=1, source_target_pairs={{0,2},{1,3},{2,0},{3,1},{4,6},{5,7},{6,4},{7,5},{8,10},{9,11},{10,... | collective-permute-start | bytes 393224 | tf_op jit(solution)/shard_map/ppermute | solution.py:15
  4.7 1.6 %collective-permute-start.3 = (bf16[4,4,32,128]{3,2,1,0:T(8,128)(2,1)}, bf16[4,4,32,128]{3,2,1,0:T(8,128)(2,1)S(1)}, u32[]{:S(2)}, u32[]{:S(2)}) collective-permute-start(bf16[4,4,32,128]{3,2,1,0:T(8,128)(2,1)} %refs_0_.1), channel_id=1, source_target_pairs={{0,1},{1,0},{2,3},{3,2},{4,5},{5,4},{6,7},{7,6},{8,9},{9,8},{10,11... | collective-permute-start | bytes 393224 | tf_op jit(solution)/shard_map/ppermute | solution.py:15
  6.3 0.0 collective-permute-start.4
  6.3 1.2 %dynamic-slice_bitcast_fusion = bf16[8,4,4,16,128]{4,3,2,1,0:T(8,128)(2,1)S(1)} fusion(bf16[8,4,4,2,16,128]{5,4,3,2,1,0:T(8,128)(2,1)} %bitcast.102, s32[]{:T(128)S(6)} %select_n.188), kind=kLoop, calls=%fused_computation.4 | loop fusion | bytes 1048580 | tf_op jit(solution)/shard_map/jit(dynamic_index_in_dim)/squeeze | solution.py:19
  7.5 0.0 copy-start.1
  7.5 0.6 %collective-permute-start.2 = (bf16[8,4,4,16,128]{4,3,2,1,0:T(8,128)(2,1)S(1)}, bf16[8,4,4,16,128]{4,3,2,1,0:T(8,128)(2,1)S(1)}, u32[]{:S(2)}, u32[]{:S(2)}) collective-permute-start(bf16[8,4,4,16,128]{4,3,2,1,0:T(8,128)(2,1)S(1)} %dynamic-slice_bitcast_fusion), channel_id=1, source_target_pairs={{0,4},{4,0},{8,12},{12,8},{16,20},{20,16},{24,28},{28,24},{1,5},{5... | collective-permute-start | bytes 1572872 | tf_op jit(solution)/shard_map/ppermute | solution.py:15
  8.1 0.1 convert_reduce_fusion
  8.2 0.1 constant_dynamic-slice_fusion.2
  8.2 0.1 copy.40
  8.3 0.1 copy.41
  8.4 0.1 fusion.29
  8.5 0.1 pad_add_fusion.spot_ref
  8.6 0.1 copy.39
  8.7 2.7 %collective-permute-done.refs_2_ = bf16[4,4,32,128]{3,2,1,0:T(8,128)(2,1)S(1)} collective-permute-done((bf16[4,4,32,128]{3,2,1,0:T(8,128)(2,1)}, bf16[4,4,32,128]{3,2,1,0:T(8,128)(2,1)S(1)}, u32[]{:S(2)}, u32[]{:S(2)}) %collective-permute-start) | collective-permute-done | bytes 131104 | tf_op jit(solution)/shard_map/ppermute | solution.py:15
  11.4 0.0 collective-permute-start.6
  11.4 0.0 collective-permute-done.4.refs_3_
  11.4 0.8 %collective-permute-start.1 = (bf16[4,4,32,128]{3,2,1,0:T(8,128)(2,1)S(1)}, bf16[4,4,32,128]{3,2,1,0:T(8,128)(2,1)S(1)}, u32[]{:S(2)}, u32[]{:S(2)}) collective-permute-start(bf16[4,4,32,128]{3,2,1,0:T(8,128)(2,1)S(1)} %collective-permute-done.refs_2_), channel_id=1, source_target_pairs={{0,1},{1,0},{2,3},{3,2},{4,5},{5,4},{6,7},{7,6},{8,9},{9,8},{10,11... | collective-permute-start | bytes 393224 | tf_op jit(solution)/shard_map/ppermute | solution.py:15
  12.2 0.0 collective-permute-done.3.refs_1_
  12.2 0.2 collective-permute-start.5
  12.4 0.3 collective-permute-done.6.refs_5_
  12.7 1.6 %collective-permute-start.12 = (bf16[8,4,16,128]{3,2,1,0:T(8,128)(2,1)S(1)}, bf16[8,4,16,128]{3,2,1,0:T(8,128)(2,1)S(1)}, u32[]{:S(2)}, u32[]{:S(2)}) collective-permute-start(bf16[8,4,16,128]{3,2,1,0:T(8,128)(2,1)S(1)} %bitcast.113), channel_id=1, source_target_pairs={{0,16},{4,20},{8,24},{12,28},{16,0},{20,4},{24,8},{28,12},{1,17},{... | collective-permute-start | bytes 393224 | tf_op jit(solution)/shard_map/ppermute | solution.py:15
  14.4 0.0 collective-permute-done.5.refs_4_
  14.4 0.0 collective-permute-done.2.met_ref
  14.4 1.0 %shard_map.59 = (bf16[512,1024]{1,0:T(8,128)(2,1)S(1)}, bf16[1024,512]{1,0:T(8,128)(2,1)S(1)}) custom-call(s32[2]{0:T(128)S(1)} %pad_add_fusion.spot_ref, f32[8,4]{1,0:T(8,128)S(1)} %pad_maximum_fusion.4.keep_ref, bf16[8,4,128,128]{3,2,1,0:T(8,128)(2,1)S(1)} %copy-done, bf16[8,4,4,16,128]{4,3,2,1,0:T(8,128)(2,1)S(1)} %collective-permute-done.2.met_ref, ...), custom_call_target="tpu_custom_call" | custom-call | bytes 4194304 | tf_op jit(solution)/shard_map/pallas_call | solution.py:74
  15.4 2.0 %collective-permute-done.1.own_ref = bf16[4,4,32,128]{3,2,1,0:T(8,128)(2,1)S(1)} collective-permute-done((bf16[4,4,32,128]{3,2,1,0:T(8,128)(2,1)S(1)}, bf16[4,4,32,128]{3,2,1,0:T(8,128)(2,1)S(1)}, u32[]{:S(2)}, u32[]{:S(2)}) %collective-permute-start.1) | collective-permute-done | bytes 131104 | tf_op jit(solution)/shard_map/ppermute | solution.py:15
  17.4 0.0 collective-permute-start.7
  17.4 1.6 %collective-permute-start.13 = (bf16[8,4,16,128]{3,2,1,0:T(8,128)(2,1)S(1)}, bf16[8,4,16,128]{3,2,1,0:T(8,128)(2,1)S(1)}, u32[]{:S(2)}, u32[]{:S(2)}) collective-permute-start(bf16[8,4,16,128]{3,2,1,0:T(8,128)(2,1)S(1)} %bitcast.114), channel_id=1, source_target_pairs={{0,8},{4,12},{8,0},{12,4},{16,24},{20,28},{24,16},{28,20},{1,9},{5... | collective-permute-start | bytes 393224 | tf_op jit(solution)/shard_map/ppermute | solution.py:15
  19.1 2.3 %collective-permute-start.11 = (bf16[8,4,16,128]{3,2,1,0:T(8,128)(2,1)S(1)}, bf16[8,4,16,128]{3,2,1,0:T(8,128)(2,1)S(1)}, u32[]{:S(2)}, u32[]{:S(2)}) collective-permute-start(bf16[8,4,16,128]{3,2,1,0:T(8,128)(2,1)S(1)} %bitcast.115), channel_id=1, source_target_pairs={{0,24},{4,28},{8,16},{12,20},{16,8},{20,12},{24,0},{28,4},{1,25},{... | collective-permute-start | bytes 393224 | tf_op jit(solution)/shard_map/ppermute | solution.py:15
  21.3 1.4 %shard_map.60 = (f32[512,512]{1,0:T(8,128)S(1)}, f32[16,512]{1,0:T(8,128)S(1)}) custom-call(s32[2]{0:T(128)S(1)} %pad_add_fusion.spot_ref, f32[8,4]{1,0:T(8,128)S(1)} %pad_maximum_fusion.4.keep_ref, bf16[512,1024]{1,0:T(8,128)(2,1)S(1)} %get-tuple-element.13.left_ref, bf16[1024,512]{1,0:T(8,128)(2,1)S(1)} %get-tuple-element.14.given_ref, ...), custom_call_target="tpu_custom_call" | custom-call | flops 536870912 | bytes 4194304 | tf_op jit(solution)/shard_map/pallas_call | solution.py:91
  22.8 0.1 multiply_convert_fusion
  23.0 0.1 fusion.8
  23.1 0.6 %collective-permute-start.9 = (f16[136,512]{1,0:T(8,128)(2,1)S(1)}, f16[136,512]{1,0:T(8,128)(2,1)S(1)}, u32[]{:S(2)}, u32[]{:S(2)}) collective-permute-start(f16[136,512]{1,0:T(8,128)(2,1)S(1)} %get-tuple-element.21), channel_id=1, source_target_pairs={{0,16},{4,20},{8,24},{12,28},{16,0},{20,4},{24,8},{28,12},{1,17},{... | collective-permute-start | bytes 417800 | tf_op jit(solution)/shard_map/ppermute | solution.py:15
  23.7 1.7 %collective-permute-start.10 = (f16[136,512]{1,0:T(8,128)(2,1)S(1)}, f16[136,512]{1,0:T(8,128)(2,1)S(1)}, u32[]{:S(2)}, u32[]{:S(2)}) collective-permute-start(f16[136,512]{1,0:T(8,128)(2,1)S(1)} %get-tuple-element.22), channel_id=1, source_target_pairs={{0,24},{4,28},{8,16},{12,20},{16,8},{20,12},{24,0},{28,4},{1,25},{... | collective-permute-start | bytes 417800 | tf_op jit(solution)/shard_map/ppermute | solution.py:15
  25.4 1.2 %collective-permute-start.8 = (f16[136,512]{1,0:T(8,128)(2,1)S(1)}, f16[136,512]{1,0:T(8,128)(2,1)S(1)}, u32[]{:S(2)}, u32[]{:S(2)}) collective-permute-start(f16[136,512]{1,0:T(8,128)(2,1)S(1)} %get-tuple-element.20), channel_id=1, source_target_pairs={{0,8},{4,12},{8,0},{12,4},{16,24},{20,28},{24,16},{28,20},{1,9},{5... | collective-permute-start | bytes 417800 | tf_op jit(solution)/shard_map/ppermute | solution.py:15
  26.6 0.0 collective-permute-done.13
  26.6 1.0 %collective-permute-done.11 = bf16[8,4,16,128]{3,2,1,0:T(8,128)(2,1)S(1)} collective-permute-done((bf16[8,4,16,128]{3,2,1,0:T(8,128)(2,1)S(1)}, bf16[8,4,16,128]{3,2,1,0:T(8,128)(2,1)S(1)}, u32[]{:S(2)}, u32[]{:S(2)}) %collective-permute-start.11) | collective-permute-done | bytes 131104 | tf_op jit(solution)/shard_map/ppermute | solution.py:15
  27.7 0.1 fusion.12.own_ref
  27.8 5.4 %collective-permute-done.9 = f16[136,512]{1,0:T(8,128)(2,1)S(1)} collective-permute-done((f16[136,512]{1,0:T(8,128)(2,1)S(1)}, f16[136,512]{1,0:T(8,128)(2,1)S(1)}, u32[]{:S(2)}, u32[]{:S(2)}) %collective-permute-start.9) | collective-permute-done | bytes 139296 | tf_op jit(solution)/shard_map/ppermute | solution.py:15
  33.2 0.0 collective-permute-done.10
  33.3 0.1 fusion.sums_ref
  33.4 1.0 %shard_map.61 = f32[32,16,128]{2,1,0:T(8,128)} custom-call(bf16[8,4,16,128]{3,2,1,0:T(8,128)(2,1)S(1)} %fusion.12.own_ref, f32[128,512]{1,0:T(8,128)S(1)} %fusion.sums_ref), custom_call_target="tpu_custom_call" | custom-call | flops 33554432 | bytes 1048576 | tf_op jit(solution)/shard_map/pallas_call | solution.py:124
  34.4 4.7 %all-to-all-start = ((f32[32,16,128]{2,1,0:T(8,128)}), f32[32,16,128]{2,1,0:T(8,128)S(1)}, u32[]{:S(2)}, u32[]{:S(2)}) async-start(f32[32,16,128]{2,1,0:T(8,128)} %shard_map.61), calls=%async_computation | async-start | bytes 524288 | tf_op jit(solution)/shard_map/all_to_all | solution.py:232
  39.1 0.1 fusion.30
  39.2 0.1 copy.29
  39.3 0.1 reshape.224
  39.4 0.8 %fusion.3 = f32[8,4,16,128]{3,2,1,0:T(8,128)} fusion(f32[8,16,4,128]{3,2,1,0:T(4,128)S(1)} %reshape.224, f32[8,4]{1,0:T(8,128)S(1)} %copy.29), kind=kLoop, calls=%fused_computation.15 | loop fusion | flops 65536 | bytes 524416 | tf_op jit(solution)/shard_map/transpose | solution.py:234
  40.2 9.1 %all-to-all-done = f32[32,16,128]{2,1,0:T(8,128)S(1)} async-done(((f32[32,16,128]{2,1,0:T(8,128)}), f32[32,16,128]{2,1,0:T(8,128)S(1)}, u32[]{:S(2)}, u32[]{:S(2)}) %all-to-all-start) | async-done | bytes 262176 | tf_op jit(solution)/shard_map/all_to_all | solution.py:232
  49.4 0.6 %sub.33 = f32[4,512]{1,0:T(4,128)} subtract(f32[4,512]{1,0:T(4,128)S(1)} %bitcast.116, f32[4,512]{1,0:T(4,128)S(1)} %neg.7) | non-fusion elementwise | flops 2048 | bytes 24576 | tf_op jit(solution)/shard_map/sub | solution.py:234
  (31 shorter events, 0.3 us)
Async XLA Ops:
  0.6 10.7 %collective-permute-start = (bf16[4,4,32,128]{3,2,1,0:T(8,128)(2,1)}, bf16[4,4,32,128]{3,2,1,0:T(8,128)(2,1)S(1)}, u32[]{:S(2)}, u32[]{:S(2)}) collective-permute-start(bf16[4,4,32,128]{3,2,1,0:T(8,128)(2,1)} %refs_0_.1), channel_id=1, source_target_pairs={{0,2},{1,3},{2,0},{3,1},{4,6},{5,7},{6,4},{7,5},{8,10},{9,11},{10,... | collective-permute-start | bytes 393224 | tf_op jit(solution)/shard_map/ppermute | solution.py:15
  4.7 7.5 %collective-permute-start.3 = (bf16[4,4,32,128]{3,2,1,0:T(8,128)(2,1)}, bf16[4,4,32,128]{3,2,1,0:T(8,128)(2,1)S(1)}, u32[]{:S(2)}, u32[]{:S(2)}) collective-permute-start(bf16[4,4,32,128]{3,2,1,0:T(8,128)(2,1)} %refs_0_.1), channel_id=1, source_target_pairs={{0,1},{1,0},{2,3},{3,2},{4,5},{5,4},{6,7},{7,6},{8,9},{9,8},{10,11... | collective-permute-start | bytes 393224 | tf_op jit(solution)/shard_map/ppermute | solution.py:15
  6.3 5.1 %collective-permute-start.4 = (bf16[4,4,32,128]{3,2,1,0:T(8,128)(2,1)}, bf16[4,4,32,128]{3,2,1,0:T(8,128)(2,1)S(1)}, u32[]{:S(2)}, u32[]{:S(2)}) collective-permute-start(bf16[4,4,32,128]{3,2,1,0:T(8,128)(2,1)} %refs_0_.1), channel_id=1, source_target_pairs={{0,4},{4,0},{8,12},{12,8},{16,20},{20,16},{24,28},{28,24},{1,5},{5... | collective-permute-start | bytes 393224 | tf_op jit(solution)/shard_map/ppermute | solution.py:15
  6.3 1.8 %copy-start.3 = (s32[4,16]{1,0:T(4,128)S(1)}, s32[4,16]{1,0:T(4,128)}, u32[]{:S(2)}) copy-start(s32[4,16]{1,0:T(4,128)} %param.6) | copy-start | bytes 772
  6.3 2.4 %copy-start.2 = (f32[4,512]{1,0:T(4,128)S(1)}, f32[4,512]{1,0:T(4,128)}, u32[]{:S(2)}) copy-start(f32[4,512]{1,0:T(4,128)} %param.7) | copy-start | bytes 24580
  6.3 8.1 %copy-start = (bf16[8,4,128,128]{3,2,1,0:T(8,128)(2,1)S(1)}, bf16[8,4,128,128]{3,2,1,0:T(8,128)(2,1)}, u32[]{:S(2)}) copy-start(bf16[8,4,128,128]{3,2,1,0:T(8,128)(2,1)} %inv_ref.1) | copy-start | bytes 3145732
  7.5 3.9 %copy-start.1 = (bf16[4,4,32,128]{3,2,1,0:T(8,128)(2,1)S(1)}, bf16[4,4,32,128]{3,2,1,0:T(8,128)(2,1)}, u32[]{:S(2)}) copy-start(bf16[4,4,32,128]{3,2,1,0:T(8,128)(2,1)} %refs_0_.1) | copy-start | bytes 393220
  7.5 6.9 %collective-permute-start.2 = (bf16[8,4,4,16,128]{4,3,2,1,0:T(8,128)(2,1)S(1)}, bf16[8,4,4,16,128]{4,3,2,1,0:T(8,128)(2,1)S(1)}, u32[]{:S(2)}, u32[]{:S(2)}) collective-permute-start(bf16[8,4,4,16,128]{4,3,2,1,0:T(8,128)(2,1)S(1)} %dynamic-slice_bitcast_fusion), channel_id=1, source_target_pairs={{0,4},{4,0},{8,12},{12,8},{16,20},{20,16},{24,28},{28,24},{1,5},{5... | collective-permute-start | bytes 1572872 | tf_op jit(solution)/shard_map/ppermute | solution.py:15
  11.4 1.3 %collective-permute-start.6 = (bf16[4,4,32,128]{3,2,1,0:T(8,128)(2,1)S(1)}, bf16[4,4,32,128]{3,2,1,0:T(8,128)(2,1)S(1)}, u32[]{:S(2)}, u32[]{:S(2)}) collective-permute-start(bf16[4,4,32,128]{3,2,1,0:T(8,128)(2,1)S(1)} %collective-permute-done.refs_2_), channel_id=1, source_target_pairs={{0,4},{4,0},{8,12},{12,8},{16,20},{20,16},{24,28},{28,24},{1,5},{5... | collective-permute-start | bytes 393224 | tf_op jit(solution)/shard_map/ppermute | solution.py:15
  11.4 6.0 %collective-permute-start.1 = (bf16[4,4,32,128]{3,2,1,0:T(8,128)(2,1)S(1)}, bf16[4,4,32,128]{3,2,1,0:T(8,128)(2,1)S(1)}, u32[]{:S(2)}, u32[]{:S(2)}) collective-permute-start(bf16[4,4,32,128]{3,2,1,0:T(8,128)(2,1)S(1)} %collective-permute-done.refs_2_), channel_id=1, source_target_pairs={{0,1},{1,0},{2,3},{3,2},{4,5},{5,4},{6,7},{7,6},{8,9},{9,8},{10,11... | collective-permute-start | bytes 393224 | tf_op jit(solution)/shard_map/ppermute | solution.py:15
  12.2 2.2 %collective-permute-start.5 = (bf16[4,4,32,128]{3,2,1,0:T(8,128)(2,1)S(1)}, bf16[4,4,32,128]{3,2,1,0:T(8,128)(2,1)S(1)}, u32[]{:S(2)}, u32[]{:S(2)}) collective-permute-start(bf16[4,4,32,128]{3,2,1,0:T(8,128)(2,1)S(1)} %collective-permute-done.3.refs_1_), channel_id=1, source_target_pairs={{0,4},{4,0},{8,12},{12,8},{16,20},{20,16},{24,28},{28,24},{1,5},{5... | collective-permute-start | bytes 393224 | tf_op jit(solution)/shard_map/ppermute | solution.py:15
  12.7 12.7 %collective-permute-start.12 = (bf16[8,4,16,128]{3,2,1,0:T(8,128)(2,1)S(1)}, bf16[8,4,16,128]{3,2,1,0:T(8,128)(2,1)S(1)}, u32[]{:S(2)}, u32[]{:S(2)}) collective-permute-start(bf16[8,4,16,128]{3,2,1,0:T(8,128)(2,1)S(1)} %bitcast.113), channel_id=1, source_target_pairs={{0,16},{4,20},{8,24},{12,28},{16,0},{20,4},{24,8},{28,12},{1,17},{... | collective-permute-start | bytes 393224 | tf_op jit(solution)/shard_map/ppermute | solution.py:15
  17.4 1.6 %collective-permute-start.7 = (bf16[4,4,32,128]{3,2,1,0:T(8,128)(2,1)S(1)}, bf16[4,4,32,128]{3,2,1,0:T(8,128)(2,1)S(1)}, u32[]{:S(2)}, u32[]{:S(2)}) collective-permute-start(bf16[4,4,32,128]{3,2,1,0:T(8,128)(2,1)S(1)} %collective-permute-done.1.own_ref), channel_id=1, source_target_pairs={{0,4},{4,0},{8,12},{12,8},{16,20},{20,16},{24,28},{28,24},{1,5},{5... | collective-permute-start | bytes 393224 | tf_op jit(solution)/shard_map/ppermute | solution.py:15
  17.4 9.2 %collective-permute-start.13 = (bf16[8,4,16,128]{3,2,1,0:T(8,128)(2,1)S(1)}, bf16[8,4,16,128]{3,2,1,0:T(8,128)(2,1)S(1)}, u32[]{:S(2)}, u32[]{:S(2)}) collective-permute-start(bf16[8,4,16,128]{3,2,1,0:T(8,128)(2,1)S(1)} %bitcast.114), channel_id=1, source_target_pairs={{0,8},{4,12},{8,0},{12,4},{16,24},{20,28},{24,16},{28,20},{1,9},{5... | collective-permute-start | bytes 393224 | tf_op jit(solution)/shard_map/ppermute | solution.py:15
  19.1 8.6 %collective-permute-start.11 = (bf16[8,4,16,128]{3,2,1,0:T(8,128)(2,1)S(1)}, bf16[8,4,16,128]{3,2,1,0:T(8,128)(2,1)S(1)}, u32[]{:S(2)}, u32[]{:S(2)}) collective-permute-start(bf16[8,4,16,128]{3,2,1,0:T(8,128)(2,1)S(1)} %bitcast.115), channel_id=1, source_target_pairs={{0,24},{4,28},{8,16},{12,20},{16,8},{20,12},{24,0},{28,4},{1,25},{... | collective-permute-start | bytes 393224 | tf_op jit(solution)/shard_map/ppermute | solution.py:15
  23.1 10.1 %collective-permute-start.9 = (f16[136,512]{1,0:T(8,128)(2,1)S(1)}, f16[136,512]{1,0:T(8,128)(2,1)S(1)}, u32[]{:S(2)}, u32[]{:S(2)}) collective-permute-start(f16[136,512]{1,0:T(8,128)(2,1)S(1)} %get-tuple-element.21), channel_id=1, source_target_pairs={{0,16},{4,20},{8,24},{12,28},{16,0},{20,4},{24,8},{28,12},{1,17},{... | collective-permute-start | bytes 417800 | tf_op jit(solution)/shard_map/ppermute | solution.py:15
  23.7 9.6 %collective-permute-start.10 = (f16[136,512]{1,0:T(8,128)(2,1)S(1)}, f16[136,512]{1,0:T(8,128)(2,1)S(1)}, u32[]{:S(2)}, u32[]{:S(2)}) collective-permute-start(f16[136,512]{1,0:T(8,128)(2,1)S(1)} %get-tuple-element.22), channel_id=1, source_target_pairs={{0,24},{4,28},{8,16},{12,20},{16,8},{20,12},{24,0},{28,4},{1,25},{... | collective-permute-start | bytes 417800 | tf_op jit(solution)/shard_map/ppermute | solution.py:15
  25.4 7.9 %collective-permute-start.8 = (f16[136,512]{1,0:T(8,128)(2,1)S(1)}, f16[136,512]{1,0:T(8,128)(2,1)S(1)}, u32[]{:S(2)}, u32[]{:S(2)}) collective-permute-start(f16[136,512]{1,0:T(8,128)(2,1)S(1)} %get-tuple-element.20), channel_id=1, source_target_pairs={{0,8},{4,12},{8,0},{12,4},{16,24},{20,28},{24,16},{28,20},{1,9},{5... | collective-permute-start | bytes 417800 | tf_op jit(solution)/shard_map/ppermute | solution.py:15
  34.4 14.9 %all-to-all-start = ((f32[32,16,128]{2,1,0:T(8,128)}), f32[32,16,128]{2,1,0:T(8,128)S(1)}, u32[]{:S(2)}, u32[]{:S(2)}) async-start(f32[32,16,128]{2,1,0:T(8,128)} %shard_map.61), calls=%async_computation | async-start | bytes 524288 | tf_op jit(solution)/shard_map/all_to_all | solution.py:232
